TPU v7x, 32 devices: a whole 2x2x4 slice. The times are simulated.
32 devices in a mesh: rows: 8 (over z, x), cols: 4 (over y, core).
Axes of the slice: x: 2, y: 2, z: 4, core: 2. Of those that a mesh axis runs over, the one named last changes fastest.
Arguments:
- panel_cols: bfloat16 [32, 16, 256, 128], P('rows', 'cols'), may hold values from -2 to 2
- pivot_inv: bfloat16 [16, 256, 256], P('cols'), may hold values from -0.375 to 0.375
- pivot_rows: bfloat16 [16, 24, 256, 128], P('rows', 'cols'), may hold values from -2 to 2
- target_factors: bfloat16 [32, 24, 256, 128], P('rows', 'cols'), may hold values from -5 to 5
- near_blocks: bfloat16 [32, 4, 256, 256], P('rows', 'cols'), may hold values from -6 to 6
- near_cols: int32 [32, 4], P('rows', 'cols'), may hold values from 0 to 5, as said below
- sketch: bfloat16 [24, 256, 64], P('cols'), may hold values from -6 to 6
Outputs:
- near_out: bfloat16 [32, 4, 256, 256], P('rows', 'cols')
- far_out: bfloat16 [32, 24, 256, 128], P('rows', 'cols')
Inputs may be any that keep to these rules, and one draw needn't show every extreme that they name: `near_cols`: for every block row, the 1 entries of each group of slots s with equal s // 1 are distinct.
All inputs are finite; a program needn't handle non-finite values.
Results may differ from a plain program's by a relative error of at most 0.009.
Values may be sent and summed in bfloat16 or wider, within the bound.
No kernel may reach another device: no remote copies, remote signals or barrier semaphores. Data moves between devices by JAX's collectives and lax.ppermute only.
A program may use at most 128 MiB of HBM per device.

v0:
```python
import math

import jax
import jax.numpy as jnp
from jax import lax
from jax.sharding import PartitionSpec as P


def spread(block, axis, holder):
    block = jnp.where(lax.axis_index(axis) == holder, block, jnp.zeros_like(block))
    return lax.psum(block, axis)


def product_of(form, left, right):
    return jnp.einsum(form, left, right, preferred_element_type=jnp.float32)


def row_update(left_row, rows_all, target_row, near_row, near_index, sketch):
    half = left_row.shape[-1] // 2
    root_size = math.sqrt(left_row.shape[1])
    left_x = left_row[..., :half]
    left_y = left_row[..., half:]
    pivot_p = rows_all[..., :half]
    pivot_q = rows_all[..., half:]
    mid_cores = product_of("kbr,kjbs->kjrs", left_y, pivot_p).astype(jnp.bfloat16)
    left_terms = product_of("kbr,kjrs->jkbs", left_x, mid_cores).astype(jnp.bfloat16)
    left_near = jnp.take(left_terms, near_index, axis=0)
    q_near = jnp.take(pivot_q, near_index, axis=1)
    update = product_of("nkbs,kncs->nbc", left_near, q_near)
    near_new = (near_row.astype(jnp.float32) - update).astype(jnp.bfloat16)
    column_ids = jnp.arange(target_row.shape[0], dtype=jnp.int32)
    is_near = jnp.any(near_index[:, None] == column_ids[None, :], axis=0)
    target_u = target_row[..., :half]
    target_v = target_row[..., half:]
    sketch_core = product_of("jbs,jbt->jst", target_v, sketch).astype(jnp.bfloat16)
    pivot_sketch = product_of("kjbs,jbt->jkst", pivot_q, sketch).astype(jnp.bfloat16)
    sampled = product_of("jbs,jst->jbt", target_u, sketch_core) - product_of(
        "jkbs,jkst->jbt", left_terms, pivot_sketch
    )
    gram_matrix = jnp.einsum("jbs,jbt->jst", sampled, sampled, precision=lax.Precision.HIGHEST)
    factor_chol = jnp.linalg.cholesky(gram_matrix)
    orthonormal = lax.linalg.triangular_solve(
        factor_chol, sampled, left_side=False, lower=True, transpose_a=True
    )
    basis = (root_size * orthonormal).astype(jnp.bfloat16)
    basis_core = product_of("jbs,jbt->jst", target_u, basis).astype(jnp.bfloat16)
    left_core = product_of("jkbs,jbt->jkst", left_terms, basis).astype(jnp.bfloat16)
    weights_out = (
        product_of("jbs,jst->jbt", target_v, basis_core)
        - product_of("kjbs,jkst->jbt", pivot_q, left_core)
    ) / root_size
    keep_far = jnp.where(is_near, 0.0, 1.0).astype(jnp.bfloat16)[:, None, None]
    far_new = jnp.concatenate([basis, weights_out.astype(jnp.bfloat16)], axis=-1) * keep_far
    return (near_new, far_new)


def per_device(panel_cols, pivot_inv, pivot_rows, target_factors, near_blocks, near_cols, sketch):
    half = panel_cols.shape[-1] // 2
    col_left = panel_cols[..., :half]
    col_right = panel_cols[..., half:]
    pivot_right = product_of("kab,ikar->ikbr", pivot_inv, col_right).astype(jnp.bfloat16)
    local_panel = jnp.concatenate([col_left, pivot_right], axis=-1)
    panel_all = lax.all_gather(local_panel, "cols", axis=1, tiled=True)
    owned = pivot_rows.shape[0]
    row_count = lax.axis_size("rows")

    def fetch(owner, buffer):
        arrived = spread(pivot_rows, "rows", owner)
        return lax.dynamic_update_slice_in_dim(
            buffer, arrived, (owner * owned).astype(jnp.int32), 0
        )

    empty = jnp.zeros((row_count * owned,) + pivot_rows.shape[1:], jnp.bfloat16)
    rows_all = lax.fori_loop(0, row_count, fetch, empty)

    def one_row(row_items):
        return row_update(row_items[0], rows_all, row_items[1], row_items[2], row_items[3], sketch)

    near_new, far_new = lax.map(one_row, (panel_all, target_factors, near_blocks, near_cols))
    return (near_new, far_new)


def solution(mesh):
    placed = (
        P("rows", "cols", None, None),
        P("cols", None, None),
        P("rows", "cols", None, None),
        P("rows", "cols", None, None),
        P("rows", "cols", None, None),
        P("rows", "cols"),
        P("cols", None, None),
    )
    return jax.shard_map(
        per_device,
        mesh=mesh,
        in_specs=placed,
        out_specs=(P("rows", "cols", None, None), P("rows", "cols", None, None)),
        check_vma=False,
    )
```

profile of v0, /device:TPU:0, one launch (start us, length us, event | category | flops | bytes accessed | tf_op | source)
XLA Modules:
  0.0 1084.0 jit_solution(14271647313446843464)
XLA Ops:
  12.3 4.2 broadcast_in_dim.59
  16.4 649.0 %while.29 = (s32[]{:T(128)}, bf16[16,6,256,128]{3,2,1,0:T(8,128)(2,1)}, bf16[2,6,256,128]{3,2,1,0:T(8,128)(2,1)S(1)}, s32[]{:T(128)}, u32[]{:T(128)}, /*index=5*/u32[]{:T(128)}, s32[]{:T(128)}, s32[]{:T(128)}, s32[]{:T(128)}) while((s32[]{:T(128)}, bf16[16,6,256,128]{3,2,1,0:T(8,128)(2,1)}, bf16[2,6,256,128]{3,2,1,0:T(8,128)(2,1)S(1)}, ...), condition=%wide.region_2.3_spmd, body=%wide.region_0.2_spmd.sunk | while | flops 786442 | bytes 7864545 | solution.py:74
  17.4 81.3 %all-reduce.2.cloned.1.call-done = bf16[2,6,256,128]{3,2,1,0:T(8,128)(2,1)} async-done(((bf16[2,6,256,128]{3,2,1,0:T(8,128)(2,1)}), bf16[2,6,256,128]{3,2,1,0:T(8,128)(2,1)}) %all-reduce.2.cloned.1.call-update) | async-done | bytes 786448 | tf_op jit(solution)/shard_map/while/body/eval_jaxpr/psum | solution.py:11
  98.7 2.1 constant_dynamic-update-slice_fusion.4
  101.8 77.8 %all-reduce.2.cloned.1.call-done = bf16[2,6,256,128]{3,2,1,0:T(8,128)(2,1)} async-done(((bf16[2,6,256,128]{3,2,1,0:T(8,128)(2,1)}), bf16[2,6,256,128]{3,2,1,0:T(8,128)(2,1)}) %all-reduce.2.cloned.1.call-update) | async-done | bytes 786448 | tf_op jit(solution)/shard_map/while/body/eval_jaxpr/psum | solution.py:11
  182.6 77.8 %all-reduce.2.cloned.1.call-done = bf16[2,6,256,128]{3,2,1,0:T(8,128)(2,1)} async-done(((bf16[2,6,256,128]{3,2,1,0:T(8,128)(2,1)}), bf16[2,6,256,128]{3,2,1,0:T(8,128)(2,1)}) %all-reduce.2.cloned.1.call-update) | async-done | bytes 786448 | tf_op jit(solution)/shard_map/while/body/eval_jaxpr/psum | solution.py:11
  260.3 2.1 constant_dynamic-update-slice_fusion.4
  263.4 77.4 %all-reduce.2.cloned.1.call-done = bf16[2,6,256,128]{3,2,1,0:T(8,128)(2,1)} async-done(((bf16[2,6,256,128]{3,2,1,0:T(8,128)(2,1)}), bf16[2,6,256,128]{3,2,1,0:T(8,128)(2,1)}) %all-reduce.2.cloned.1.call-update) | async-done | bytes 786448 | tf_op jit(solution)/shard_map/while/body/eval_jaxpr/psum | solution.py:11
  340.8 2.1 constant_dynamic-update-slice_fusion.4
  343.9 77.4 %all-reduce.2.cloned.1.call-done = bf16[2,6,256,128]{3,2,1,0:T(8,128)(2,1)} async-done(((bf16[2,6,256,128]{3,2,1,0:T(8,128)(2,1)}), bf16[2,6,256,128]{3,2,1,0:T(8,128)(2,1)}) %all-reduce.2.cloned.1.call-update) | async-done | bytes 786448 | tf_op jit(solution)/shard_map/while/body/eval_jaxpr/psum | solution.py:11
  421.3 2.1 constant_dynamic-update-slice_fusion.4
  424.3 77.4 %all-reduce.2.cloned.1.call-done = bf16[2,6,256,128]{3,2,1,0:T(8,128)(2,1)} async-done(((bf16[2,6,256,128]{3,2,1,0:T(8,128)(2,1)}), bf16[2,6,256,128]{3,2,1,0:T(8,128)(2,1)}) %all-reduce.2.cloned.1.call-update) | async-done | bytes 786448 | tf_op jit(solution)/shard_map/while/body/eval_jaxpr/psum | solution.py:11
  504.8 77.8 %all-reduce.2.cloned.1.call-done = bf16[2,6,256,128]{3,2,1,0:T(8,128)(2,1)} async-done(((bf16[2,6,256,128]{3,2,1,0:T(8,128)(2,1)}), bf16[2,6,256,128]{3,2,1,0:T(8,128)(2,1)}) %all-reduce.2.cloned.1.call-update) | async-done | bytes 786448 | tf_op jit(solution)/shard_map/while/body/eval_jaxpr/psum | solution.py:11
  585.6 77.8 %all-reduce.2.cloned.1.call-done = bf16[2,6,256,128]{3,2,1,0:T(8,128)(2,1)} async-done(((bf16[2,6,256,128]{3,2,1,0:T(8,128)(2,1)}), bf16[2,6,256,128]{3,2,1,0:T(8,128)(2,1)}) %all-reduce.2.cloned.1.call-update) | async-done | bytes 786448 | tf_op jit(solution)/shard_map/while/body/eval_jaxpr/psum | solution.py:11
  663.3 2.1 constant_dynamic-update-slice_fusion.4
  666.0 8.7 copy.60
  674.7 8.5 copy.62
  683.3 2.9 fusion.56
  687.8 13.2 %all-gather.2.cloned.1.call-done = bf16[4,16,256,128]{3,2,0,1:T(8,128)(2,1)} async-done(((bf16[4,4,256,128]{3,2,0,1:T(8,128)(2,1)}), bf16[4,16,256,128]{3,2,0,1:T(8,128)(2,1)}) %all-gather.2.cloned.1.call-update) | async-done | bytes 4194320 | tf_op jit(solution)/shard_map/all_gather | solution.py:63
  700.9 375.6 %while.30 = (s32[]{:T(128)}, bf16[4,1,256,256]{3,2,1,0:T(8,128)(2,1)}, bf16[4,6,256,128]{3,2,1,0:T(8,128)(2,1)}, bf16[4,1,256,256]{3,2,1,0:T(8,128)(2,1)}, s32[4...) while((s32[]{:T(128)}, ...), condition=%wide.region_6.7_spmd, body=%wide.region_3.6_spmd.sunk | while | flops 1347256704 | bytes 55335224 | solution.py:79
  702.8 6.2 convolution_convert_fusion.5
  709.0 2.5 convolution_bitcast_fusion.3
  714.7 35.2 %custom-call.15 = f32[6,64,64]{2,1,0:T(8,128)S(1)} custom-call(f32[6,64,64]{2,1,0:T(8,128)S(1)} %fusion.124), custom_call_target="Cholesky" | custom-call | tf_op jit(solution)/shard_map/while/body/eval_jaxpr/jit(cholesky)/cholesky | solution.py:41
  750.2 29.5 %custom-call.16 = f32[6,1,64,64]{2,3,1,0:T(8,128)S(1)} custom-call(f32[6,1,64,64]{3,2,1,0:T(8,128)S(1)} %select_bitcast_fusion.2), custom_call_target="InvertDiagBlocksLowerTriangular" | custom-call | tf_op jit(solution)/shard_map/while/body/eval_jaxpr/triangular_solve | solution.py:42
  780.2 4.3 fusion.126
  789.3 3.2 copy.106
  792.7 2.1 fusion.122
  796.7 6.2 convolution_convert_fusion.5
  802.9 2.5 convolution_bitcast_fusion.3
  808.6 35.2 %custom-call.15 = f32[6,64,64]{2,1,0:T(8,128)S(1)} custom-call(f32[6,64,64]{2,1,0:T(8,128)S(1)} %fusion.124), custom_call_target="Cholesky" | custom-call | tf_op jit(solution)/shard_map/while/body/eval_jaxpr/jit(cholesky)/cholesky | solution.py:41
  844.0 29.5 %custom-call.16 = f32[6,1,64,64]{2,3,1,0:T(8,128)S(1)} custom-call(f32[6,1,64,64]{3,2,1,0:T(8,128)S(1)} %select_bitcast_fusion.2), custom_call_target="InvertDiagBlocksLowerTriangular" | custom-call | tf_op jit(solution)/shard_map/while/body/eval_jaxpr/triangular_solve | solution.py:42
  874.1 4.3 fusion.126
  883.2 3.2 copy.106
  886.6 2.1 fusion.122
  890.6 6.2 convolution_convert_fusion.5
  896.8 2.5 convolution_bitcast_fusion.3
  902.5 35.2 %custom-call.15 = f32[6,64,64]{2,1,0:T(8,128)S(1)} custom-call(f32[6,64,64]{2,1,0:T(8,128)S(1)} %fusion.124), custom_call_target="Cholesky" | custom-call | tf_op jit(solution)/shard_map/while/body/eval_jaxpr/jit(cholesky)/cholesky | solution.py:41
  937.9 29.5 %custom-call.16 = f32[6,1,64,64]{2,3,1,0:T(8,128)S(1)} custom-call(f32[6,1,64,64]{3,2,1,0:T(8,128)S(1)} %select_bitcast_fusion.2), custom_call_target="InvertDiagBlocksLowerTriangular" | custom-call | tf_op jit(solution)/shard_map/while/body/eval_jaxpr/triangular_solve | solution.py:42
  968.0 4.3 fusion.126
  977.0 3.2 copy.106
  980.5 2.1 fusion.122
  984.5 6.2 convolution_convert_fusion.5
  990.7 2.5 convolution_bitcast_fusion.3
  996.4 35.2 %custom-call.15 = f32[6,64,64]{2,1,0:T(8,128)S(1)} custom-call(f32[6,64,64]{2,1,0:T(8,128)S(1)} %fusion.124), custom_call_target="Cholesky" | custom-call | tf_op jit(solution)/shard_map/while/body/eval_jaxpr/jit(cholesky)/cholesky | solution.py:41
  1031.8 29.5 %custom-call.16 = f32[6,1,64,64]{2,3,1,0:T(8,128)S(1)} custom-call(f32[6,1,64,64]{3,2,1,0:T(8,128)S(1)} %select_bitcast_fusion.2), custom_call_target="InvertDiagBlocksLowerTriangular" | custom-call | tf_op jit(solution)/shard_map/while/body/eval_jaxpr/triangular_solve | solution.py:42
  1061.9 4.3 fusion.126
  1070.9 3.2 copy.106
  1074.4 2.1 fusion.122
  (145 shorter events, 55.5 us)
Async XLA Ops:
  8.0 2.4 copy-start
  12.3 4.2 copy-start.2
  16.4 82.2 %all-reduce.2.cloned.1.call-start = ((), (), s32[]{:S(2)}) async-start(), calls=%async_computation.1 | async-start | bytes 1572864 | tf_op jit(solution)/shard_map/while/body/eval_jaxpr/psum | solution.py:11
  100.8 78.7 %all-reduce.2.cloned.1.call-start = ((), (), s32[]{:S(2)}) async-start(), calls=%async_computation.1 | async-start | bytes 1572864 | tf_op jit(solution)/shard_map/while/body/eval_jaxpr/psum | solution.py:11
  181.6 78.7 %all-reduce.2.cloned.1.call-start = ((), (), s32[]{:S(2)}) async-start(), calls=%async_computation.1 | async-start | bytes 1572864 | tf_op jit(solution)/shard_map/while/body/eval_jaxpr/psum | solution.py:11
  262.4 78.4 %all-reduce.2.cloned.1.call-start = ((), (), s32[]{:S(2)}) async-start(), calls=%async_computation.1 | async-start | bytes 1572864 | tf_op jit(solution)/shard_map/while/body/eval_jaxpr/psum | solution.py:11
  342.9 78.4 %all-reduce.2.cloned.1.call-start = ((), (), s32[]{:S(2)}) async-start(), calls=%async_computation.1 | async-start | bytes 1572864 | tf_op jit(solution)/shard_map/while/body/eval_jaxpr/psum | solution.py:11
  423.4 78.4 %all-reduce.2.cloned.1.call-start = ((), (), s32[]{:S(2)}) async-start(), calls=%async_computation.1 | async-start | bytes 1572864 | tf_op jit(solution)/shard_map/while/body/eval_jaxpr/psum | solution.py:11
  503.8 78.7 %all-reduce.2.cloned.1.call-start = ((), (), s32[]{:S(2)}) async-start(), calls=%async_computation.1 | async-start | bytes 1572864 | tf_op jit(solution)/shard_map/while/body/eval_jaxpr/psum | solution.py:11
  584.6 78.7 %all-reduce.2.cloned.1.call-start = ((), (), s32[]{:S(2)}) async-start(), calls=%async_computation.1 | async-start | bytes 1572864 | tf_op jit(solution)/shard_map/while/body/eval_jaxpr/psum | solution.py:11
  665.4 35.5 %all-gather.2.cloned.1.call-start = ((), (), s32[]{:S(2)}) async-start(), calls=%async_computation | async-start | bytes 5242880 | tf_op jit(solution)/shard_map/all_gather | solution.py:63
  674.7 8.5 copy-start.3
  683.3 17.7 %copy-start.5 = (s32[4,1]{0,1:T(1,128)S(1)}, s32[4,1]{0,1:T(1,128)}, u32[]{:S(2)}) copy-start(s32[4,1]{0,1:T(1,128)} %param.16) | copy-start | bytes 52
  702.8 6.2 copy-start.1
  792.5 2.4 copy-start.4
  796.7 6.2 copy-start.1
  886.4 2.4 copy-start.4
  890.6 6.2 copy-start.1
  980.3 2.4 copy-start.4
  984.5 6.2 copy-start.1
  1074.2 2.4 copy-start.4
Sparse Core Ops, SparseCore 0:
  21.3 77.3 all-reduce.1
  105.6 73.8 all-reduce.1
  186.4 73.8 all-reduce.1
  266.9 73.8 all-reduce.1
  347.4 73.8 all-reduce.1
  427.9 73.8 all-reduce.1
  508.6 73.8 all-reduce.1
  589.4 73.8 all-reduce.1
Sparse Core Ops, SparseCore 1:
  667.4 33.4 all-gather.1
where the time goes:
time: 1090 us; the launch traced here: 1080 us
  waiting for transfers between devices  638 us (59%)
  other arithmetic  271 us (25%)
  local copies, waits for them, and re-layouts  76.2 us (7%)
  matrix products  74.7 us (7%)
  between operations  15.5 us (1%)
    psum x8, waiting for transfers between devices, spread(): return lax.psum(block, axis)  625 us
    another operation x16, other arithmetic, row_update(): factor_chol = jnp.linalg.cholesky(gram_matrix)  141 us
    another operation x12, other arithmetic, row_update(): lax.linalg.triangular_solve(factor_chol, sampled, left_side=False, lower=...  118 us
    dot_general x26, matrix products, product_of(): return jnp.einsum(form, left, right, preferred_element_type=jnp.float32)  70.7 us
  transfers between devices with their start and end apart: 9, of which 9 were waited for; matrix products, arithmetic and copies ran while one was open for 2% of the time, Pallas kernels for 0%

commit v1 on v0

v1 whole, which is shorter than its diff:
```python
import math

import jax
import jax.numpy as jnp
from jax import lax
from jax.experimental import pallas as pl
from jax.experimental.pallas import tpu as pltpu
from jax.sharding import PartitionSpec as P

F32 = jnp.float32
BF16 = jnp.bfloat16
NN = (((1,), (0,)), ((), ()))
NT = (((1,), (1,)), ((), ()))
TN = (((0,), (0,)), ((), ()))
VMEM_BYTES = 50 * 1024 * 1024


def dot(left, right, dims=NN, precision=None):
    return lax.dot_general(left, right, dims, precision=precision, preferred_element_type=F32)


def halves(shape, half):
    return lax.broadcasted_iota(jnp.int32, shape, len(shape) - 1) // half % 2 == 0


def swap(value, half):
    return jnp.concatenate([value[:, half:], value[:, :half]], axis=1)


def call(kernel, out_shape, in_specs, scratch=(), flops=0, moved=0):
    out_specs = jax.tree.map(lambda _: pl.BlockSpec(memory_space=pltpu.VMEM), out_shape)
    return pl.pallas_call(
        kernel,
        out_shape=out_shape,
        in_specs=in_specs,
        out_specs=out_specs,
        scratch_shapes=list(scratch),
        compiler_params=pltpu.CompilerParams(vmem_limit_bytes=VMEM_BYTES),
        cost_estimate=pl.CostEstimate(flops=flops, bytes_accessed=moved, transcendentals=0),
    )


IN_VMEM = pl.BlockSpec(memory_space=pltpu.VMEM)
IN_SMEM = pl.BlockSpec(memory_space=pltpu.SMEM)
ANYWHERE = pl.BlockSpec(memory_space=pl.ANY)


def pack_rows_kernel(rows_ref, sketch_ref, pb_ref, q_ref):
    _, columns, size, width = rows_ref.shape
    half = width // 2
    for j in range(columns):
        first, second = rows_ref[0, j], rows_ref[1, j]
        lanes = pl.ds(j * width, width)
        pb_ref[:size, lanes] = jnp.concatenate([first[:, :half], second[:, :half]], axis=1)
        q_pair = jnp.concatenate([first[:, half:], second[:, half:]], axis=1)
        q_ref[:, lanes] = q_pair
        pb_ref[pl.ds(size, half), lanes] = dot(sketch_ref[j], q_pair).astype(BF16)


def pack_panel_kernel(panel_ref, inv_ref, out_ref):
    count, pivots, size, width = panel_ref.shape
    half = width // 2
    for k in range(pivots):
        rights = [jnp.transpose(panel_ref[i, k])[half:] for i in range(count)]
        hat = dot(jnp.concatenate(rights, axis=0), inv_ref[k]).astype(BF16)
        for i in range(count):
            start = (k // 2) * count * width + i * width + (k % 2) * half
            out_ref[pl.ds(start, half), :] = hat[i * half : (i + 1) * half]
    base = (pivots // 2) * count * width
    for i in range(count):
        for k in range(0, pivots, 2):
            pair = [panel_ref[i, k + m][:, :half] for m in range(2)]
            out_ref[pl.ds(base + i * size, size), pl.ds(k * half, width)] = jnp.concatenate(pair, axis=1)


def target_sketch_kernel(target_ref, sketch_ref, out_ref):
    count, columns, size, width = target_ref.shape
    half = width // 2
    first = halves((half, width), half)
    zero = jnp.zeros((half, width), BF16)
    for i in range(count):
        for j in range(0, columns, 2):
            core = []
            for m in range(2):
                product = dot(sketch_ref[j + m], target_ref[i, j + m])
                core.append(jnp.where(first, swap(product, half), 0.0).astype(BF16))
            left = jnp.concatenate([target_ref[i, j], target_ref[i, j + 1]], axis=1)
            right = jnp.concatenate(
                [jnp.concatenate([core[0], zero], axis=1), jnp.concatenate([zero, core[1]], axis=1)], axis=0
            )
            out_ref[i, :, pl.ds(j * half, width)] = dot(left, right, NT)


def fetch_all(sources, target, owners_ref, sem):
    copies = []
    for n, source in enumerate(sources):
        copies.append(pltpu.make_async_copy(source, target.at[owners_ref[n]], sem.at[n]))
    for copy in copies:
        copy.start()
    return copies


def sampled_kernel(n_rows, n_cols, row_owner_ref, col_owner_ref, *refs):
    blocks, panels = refs[:n_rows], refs[n_rows : n_rows + n_cols]
    target_ref, mid_ref, sampled_ref, panel_ref, pb_all, weight, sem, sem_panel = refs[n_rows + n_cols :]
    count, size, wide = target_ref.shape
    half = pb_all.shape[1] - size
    width = 2 * half
    columns = wide // half
    copies = fetch_all(blocks, pb_all, row_owner_ref, sem)
    copies += fetch_all(panels, panel_ref, col_owner_ref, sem_panel)
    for copy in copies:
        copy.wait()
    tall = count * width
    row_half = lax.broadcasted_iota(jnp.int32, (tall, 2 * width), 0) // half % 2
    lane_half = lax.broadcasted_iota(jnp.int32, (tall, 2 * width), 1) // half % 2
    same = row_half == lane_half
    zero = jnp.zeros((half, width), BF16)
    per_col = panel_ref.shape[2] // width

    def one_owner(o, carry):
        left = panel_ref[o // per_col, pl.ds(pl.multiple_of(o % per_col * tall, tall), tall), :]
        for j in range(0, columns, 2):
            lanes = pl.ds(j * width, 2 * width)
            mid = dot(left, pb_all[o, :size, lanes])
            mid = jnp.where(same, mid, 0.0).astype(BF16)
            mid_ref[o, :, lanes] = mid
            b_pair = pb_all[o, size:, lanes]
            right = jnp.concatenate(
                [
                    jnp.concatenate([b_pair[:, :width], zero], axis=1),
                    jnp.concatenate([zero, b_pair[:, width:]], axis=1),
                ],
                axis=0,
            )
            product = dot(mid, right, NT).astype(BF16)
            for i in range(count):
                weight[i, pl.ds(pl.multiple_of(o * width, width), width), pl.ds(j * half, width)] = product[
                    i * width : (i + 1) * width
                ]
        return carry

    lax.fori_loop(0, n_rows, one_owner, 0)
    base = per_col * tall
    deep = panel_ref.shape[2]
    for i in range(count):
        total = target_ref[i]
        for c in range(n_cols):
            total = total - dot(panel_ref[c, pl.ds(base + i * size, size), :], weight[i, pl.ds(c * deep, deep), :])
        sampled_ref[i] = total


def basis_kernel(sampled_ref, basis_ref, state):
    count, size, wide = sampled_ref.shape
    _, half, width = state.shape
    columns = wide // half
    pairs = columns // 2
    root_size = math.sqrt(size)
    highest = lax.Precision.HIGHEST
    first = halves((half, width), half)
    lane = lax.broadcasted_iota(jnp.int32, (half, width), 1)
    row = lax.broadcasted_iota(jnp.int32, (half, width), 0)
    n_even = count * pairs
    for i in range(count):
        for p in range(pairs):
            z_pair = sampled_ref[i, :, pl.ds(p * width, width)]
            gram = swap(dot(z_pair, z_pair, TN, highest), half)
            g = i * pairs + p
            state[g] = jnp.where(first, (lane == row).astype(F32), gram[:half])
            state[n_even + g] = jnp.where(first, gram[half:], (lane == row + half).astype(F32))
    sub = 8
    for block in range(half // sub):

        def eliminate(q, carry, block=block):
            pivot = block * sub + q
            below = lax.broadcasted_iota(jnp.int32, (sub, width), 0) > q
            for g in range(2 * n_even):
                offset = half if g < n_even else 0
                index = jnp.full((sub, width), pivot + offset, jnp.int32)
                line = jnp.broadcast_to(state[g, pl.ds(pivot, 1), :], (sub, width))
                top = jnp.take_along_axis(line, index, axis=1)
                line = line / top
                for v in range(block, half // sub):
                    rows = pl.ds(v * sub, sub)
                    tile = state[g, rows, :]
                    column = jnp.take_along_axis(tile, index, axis=1)
                    if v == block:
                        column = jnp.where(below, column, 0.0)
                    state[g, rows, :] = tile - column * line
            return carry

        lax.fori_loop(0, sub, eliminate, 0)
    for i in range(count):
        for p in range(pairs):
            g = i * pairs + p
            even, odd = state[g], state[n_even + g]
            even_diag = jnp.sum(jnp.where(lane == row + half, even, 0.0), axis=1, keepdims=True)
            odd_diag = jnp.sum(jnp.where(lane == row, odd, 0.0), axis=1, keepdims=True)
            even = jnp.where(first, even * (root_size * lax.rsqrt(even_diag)), 0.0)
            odd = jnp.where(first, 0.0, odd * (root_size * lax.rsqrt(odd_diag)))
            inverse = jnp.concatenate([even, odd], axis=0)
            z_pair = sampled_ref[i, :, pl.ds(p * width, width)]
            basis_ref[i, :, pl.ds(p * width, width)] = dot(z_pair, inverse, NT, highest).astype(BF16)


def cores_kernel(n_rows, near_ref, basis_ref, mid_ref, panel_ref, target_ref, left_ref, value_ref, near_left_ref, cores):
    count, size, wide = basis_ref.shape
    columns, width = target_ref.shape[1], target_ref.shape[3]
    half = width // 2
    n_cols, _, deep = panel_ref.shape
    per_col = deep // width
    base = per_col * count * width
    first = halves((half, width), half)
    zero = jnp.zeros((half, width), BF16)
    tall = count * width
    turned = []
    for i in range(count):
        basis_t = jnp.transpose(basis_ref[i])
        turned.append(basis_t)
        for c in range(n_cols):
            cores[i, :, pl.ds(c * deep, deep)] = dot(basis_t, panel_ref[c, pl.ds(base + i * size, size), :]).astype(BF16)
    for i in range(0, count, 2):
        for j in range(columns):
            core = []
            for m in range(2):
                product = dot(turned[i + m][j * half : (j + 1) * half], target_ref[i + m, j])
                core.append(jnp.where(first, 0.0, swap(product, half)).astype(BF16))
            left = jnp.concatenate([target_ref[i, j], target_ref[i + 1, j]], axis=1)
            right = jnp.concatenate(
                [jnp.concatenate([core[0], zero], axis=1), jnp.concatenate([zero, core[1]], axis=1)], axis=0
            )
            value_ref[j, :, pl.ds(i * half, width)] = dot(left, right, NT)

    def one_owner(o, carry):
        lanes = pl.ds(pl.multiple_of(o * width, width), width)
        for i in range(count):
            for j in range(columns):
                product = dot(
                    cores[i, pl.ds(j * half, half), lanes],
                    mid_ref[o, pl.ds(i * width, width), pl.ds(j * width, width)],
                )
                left_ref[j, pl.ds(i * half, half), lanes] = product.astype(BF16)
            near = pl.ds(pl.multiple_of(near_ref[i, 0] * width, width), width)
            x_part = panel_ref[
                o // per_col, pl.ds(base + i * size, size), pl.ds(pl.multiple_of(o % per_col * width, width), width)
            ]
            near_left_ref[i, :, lanes] = dot(x_part, mid_ref[o, pl.ds(i * width, width), near]).astype(BF16)
        return carry

    lax.fori_loop(0, n_rows, one_owner, 0)


def output_kernel(n_rows, near_ref, row_owner_ref, *refs):
    blocks = refs[:n_rows]
    basis_ref, left_ref, value_ref, near_left_ref, near_block_ref, near_out_ref, far_out_ref, q_all, sem = refs[n_rows:]
    count, columns, size, width = far_out_ref.shape
    half = width // 2
    root_size = math.sqrt(size)
    first = halves((size, width), half)
    for copy in fetch_all(blocks, q_all, row_owner_ref, sem):
        copy.wait()
    for j in range(columns):
        right = jnp.concatenate([q_all[o, :, pl.ds(j * width, width)] for o in range(n_rows)], axis=1)
        weights = (value_ref[j] - dot(right, left_ref[j], NT)) / root_size
        for i in range(count):
            tile = weights[:, i // 2 * width : (i // 2 + 1) * width]
            if i % 2 == 0:
                tile = swap(tile, half)
            basis = basis_ref[i, :, pl.ds(j // 2 * width, width)]
            if j % 2 == 1:
                basis = swap(basis, half)
            block = jnp.where(first, basis, tile.astype(BF16))
            is_near = near_ref[i, 0] == j
            for s in range(1, near_ref.shape[1]):
                is_near = jnp.logical_or(is_near, near_ref[i, s] == j)
            far_out_ref[i, j] = jnp.where(is_near, jnp.zeros_like(block), block)
    for i in range(count):
        near = pl.ds(pl.multiple_of(near_ref[i, 0] * width, width), width)
        right = jnp.concatenate([q_all[o, :, near] for o in range(n_rows)], axis=1)
        update = dot(near_left_ref[i], right, NT)
        near_out_ref[i, 0] = (near_block_ref[i, 0].astype(F32) - update).astype(BF16)


def gather_rows(block, after=None):
    n = lax.axis_size("rows")
    me = lax.axis_index("rows")
    if n != 8:
        whole = lax.all_gather(block, "rows")
        return [whole[o] for o in range(n)], jnp.arange(n, dtype=jnp.int32)
    inner = [(2, 4), (4, 2), (3, 5), (5, 3)]
    outward = [(2, 0), (3, 1), (4, 6), (5, 7)]
    exchange = [(i, i ^ 2) for i in range(n)]
    across = [(i, i ^ 1) for i in range(n)]
    send = lambda value, pairs: lax.ppermute(value, "rows", pairs)
    plane = me // 2
    is_end = jnp.logical_or(plane == 0, plane == 3)
    a = send(block, exchange)
    b = send(block, inner)
    x_own = send(block, across)
    c = send(b, outward)
    d = send(a, inner)
    x_a = send(a, across)
    second = jnp.where(is_end, c, b)
    e = send(d, outward)
    x_second = send(second, across)
    third = jnp.where(is_end, e, d)
    x_third = send(third, across)
    low = plane < 2
    near_plane = jnp.where(low, 2, 1) * 2 + me % 2
    far_plane = jnp.where(low, 3, 0) * 2 + me % 2
    owners = jnp.stack([me, me ^ 1, me ^ 2, me ^ 3, near_plane, near_plane ^ 1, far_plane, far_plane ^ 1])
    return [block, x_own, a, x_a, second, x_second, third, x_third], owners.astype(jnp.int32)


def gather_cols(block):
    n = lax.axis_size("cols")
    me = lax.axis_index("cols")
    if n != 4:
        whole = lax.all_gather(block, "cols")
        return [whole[o] for o in range(n)], jnp.arange(n, dtype=jnp.int32)
    core = [(i, i ^ 1) for i in range(n)]
    other = [(i, i ^ 2) for i in range(n)]
    y = lax.ppermute(block, "cols", other)
    own = lax.ppermute(block, "cols", core)
    y_core = lax.ppermute(y, "cols", core)
    owners = jnp.stack([me, me ^ 1, me ^ 2, me ^ 3])
    return [block, own, y, y_core], owners.astype(jnp.int32)


def per_device(panel_cols, pivot_inv, pivot_rows, target_factors, near_blocks, near_cols, sketch):
    n_rows, n_cols = lax.axis_size("rows"), lax.axis_size("cols")
    count, pivots, size, width = panel_cols.shape
    owned, columns = pivot_rows.shape[:2]
    half = width // 2
    wide = columns * half
    assert owned == 2 and columns % 2 == 0 and count % 2 == 0 and pivots % 2 == 0
    assert near_cols.shape[1] == 1
    shape = jax.ShapeDtypeStruct
    sketch_t = jnp.swapaxes(sketch, 1, 2)

    with jax.named_scope("pack_rows"):
        pb, q = call(
            pack_rows_kernel,
            (shape((size + half, columns * width), BF16), shape((size, columns * width), BF16)),
            [IN_VMEM] * 2,
            flops=2 * columns * half * size * width,
            moved=4 * pivot_rows.size,
        )(pivot_rows, sketch_t)
    panel_rows = (pivots // 2) * count * width + count * size
    with jax.named_scope("pack_panel"):
        panel = call(
            pack_panel_kernel,
            shape((panel_rows, pivots * half), BF16),
            [IN_VMEM] * 2,
            flops=2 * count * pivots * half * size * size,
            moved=4 * panel_cols.size,
        )(panel_cols, pivot_inv)
    with jax.named_scope("target_sketch"):
        target_sketch = call(
            target_sketch_kernel,
            shape((count, size, wide), F32),
            [IN_VMEM] * 2,
            flops=4 * target_factors.size * half,
            moved=2 * target_factors.size * 2,
        )(target_factors, sketch_t)

    pb_all, row_owners = gather_rows(pb)
    panels, col_owners = gather_cols(panel)
    q, _ = lax.optimization_barrier((q, pb_all[4]))
    q_all, _ = gather_rows(q)

    vmem = pltpu.VMEM
    with jax.named_scope("sampled"):
        mid, sampled, panel_whole = call(
            lambda *refs: sampled_kernel(n_rows, n_cols, *refs),
            (
                shape((n_rows, count * width, columns * width), BF16),
                shape((count, size, wide), F32),
                shape((n_cols,) + panel.shape, BF16),
            ),
            [IN_SMEM] * 2 + [ANYWHERE] * (n_rows + n_cols) + [IN_VMEM],
            [
                vmem((n_rows,) + pb.shape, BF16),
                vmem((count, n_rows * width, wide), BF16),
                pltpu.SemaphoreType.DMA((n_rows,)),
                pltpu.SemaphoreType.DMA((n_cols,)),
            ],
            flops=8 * n_rows * count * width * size * columns * width // 2,
            moved=2 * n_rows * (pb.size + count * width * columns * width),
        )(row_owners, col_owners, *pb_all, *panels, target_sketch)
    with jax.named_scope("basis"):
        basis = call(
            basis_kernel,
            shape((count, size, wide), BF16),
            [IN_VMEM],
            [vmem((count * columns, half, width), F32)],
            flops=8 * count * columns * half * half * size,
            moved=6 * count * size * wide,
        )(sampled)
    deep = n_rows * width
    with jax.named_scope("cores"):
        left, value, near_left = call(
            lambda *refs: cores_kernel(n_rows, *refs),
            (
                shape((columns, count * half, deep), BF16),
                shape((columns, size, count * half), F32),
                shape((count, size, deep), BF16),
            ),
            [IN_SMEM] + [IN_VMEM] * 4,
            [vmem((count, wide, deep), BF16)],
            flops=6 * n_rows * count * width * size * columns * width // 2,
            moved=2 * n_rows * (pb.size + count * width * columns * width),
        )(near_cols, basis, mid, panel_whole, target_factors)
    with jax.named_scope("output"):
        near_new, far_new = call(
            lambda *refs: output_kernel(n_rows, *refs),
            (shape(near_blocks.shape, BF16), shape(target_factors.shape, BF16)),
            [IN_SMEM] * 2 + [ANYWHERE] * n_rows + [IN_VMEM] * 5,
            [vmem((n_rows,) + q.shape, BF16), pltpu.SemaphoreType.DMA((n_rows,))],
            flops=2 * columns * size * deep * count * half,
            moved=2 * n_rows * q.size,
        )(near_cols, row_owners, *q_all, basis, left, value, near_left, near_blocks)
    return near_new, far_new


def solution(mesh):
    placed = (
        P("rows", "cols", None, None),
        P("cols", None, None),
        P("rows", "cols", None, None),
        P("rows", "cols", None, None),
        P("rows", "cols", None, None),
        P("rows", "cols"),
        P("cols", None, None),
    )
    return jax.shard_map(
        per_device,
        mesh=mesh,
        in_specs=placed,
        out_specs=(P("rows", "cols", None, None), P("rows", "cols", None, None)),
        check_vma=False,
    )
```

time: 1090 us -> 265 us (0.24)
  waiting for transfers between devices: 638 us -> 56 us
  other arithmetic: 271 us -> 4.78 us
  Pallas kernels: 0 us -> 164 us
  matrix products: 74.7 us -> 0 us
  local copies, waits for them, and re-layouts: 76.2 us -> 7.87 us
  starting transfers between devices: 0.02 us -> 29.5 us
  between operations: 15.5 us -> 1.03 us
    psum x8 -> x0, waiting for transfers between devices: 625 us -> none  [spread(): return lax.psum(block, axis)]
    another operation x28 -> x1, other arithmetic: 260 us -> 0.08 us  [gather_cols(): owners = jnp.stack([me, me ^ 1, me ^ 2, me ^ 3])]
    pallas_call x0 -> x7, Pallas kernels: none -> 164 us  [the longest x1 126 us: per_device(): call(basis_kernel, shape((count, size, wide), BF16), [IN_VMEM], [vmem((co...]
    dot_general x30 -> x0, matrix products: 72.6 us -> none  [the longest x26 70.7 us: product_of(): return jnp.einsum(form, left, right, preferred_element_type=jnp.float32)]
    ppermute x0 -> x21, waiting for transfers between devices: none -> 56 us  [the longest x18 56 us: gather_rows(): send = lambda value, pairs: lax.ppermute(value, 'rows', pairs)]
    ppermute x0 -> x21, starting transfers between devices: none -> 29.5 us  [the longest x18 27.4 us: gather_rows(): send = lambda value, pairs: lax.ppermute(value, 'rows', pairs)]
    dynamic_update_slice x16 -> x0, local copies, waits for them, and re-layouts: 20.7 us -> none  [the longest x8 16.7 us: fetch(): lax.dynamic_update_slice_in_dim(buffer, arrived, (owner * owned).astype(j...]
    while x19 -> x0, local copies, waits for them, and re-layouts: 18.9 us -> none  [the longest x2 10.1 us: per_device(): lax.map(one_row, (panel_all, target_factors, near_blocks, near_cols))]
  transfers between devices with their start and end apart: 9 -> 21, of which waited for: 9 -> 9; matrix products, arithmetic and copies ran while one was open for 2% -> 2% of each run, Pallas kernels for 0% -> 59%
where the time goes in v1:
time: 265 us; the launch traced here: 264 us
  Pallas kernels  164 us (62%)
  waiting for transfers between devices  56 us (21%)
  starting transfers between devices  29.5 us (11%)
  local copies, waits for them, and re-layouts  7.87 us (3%)
  other arithmetic  4.78 us (2%)
    pallas_call x1, Pallas kernels, per_device(): call(basis_kernel, shape((count, size, wide), BF16), [IN_VMEM], [vmem((co...  126 us
    ppermute x18, waiting for transfers between devices, gather_rows(): send = lambda value, pairs: lax.ppermute(value, 'rows', pairs)  56 us
    ppermute x18, starting transfers between devices, gather_rows(): send = lambda value, pairs: lax.ppermute(value, 'rows', pairs)  27.4 us
    pallas_call x1, Pallas kernels, per_device(): call(lambda *refs: sampled_kernel(n_rows, n_cols, *refs), (shape((n_rows,...  15.6 us
    pallas_call x1, Pallas kernels, per_device(): call(lambda *refs: cores_kernel(n_rows, *refs), (shape((columns, count *...  13 us
    unnamed x35, local copies, waits for them, and re-layouts  7.78 us
    pallas_call x1, Pallas kernels, per_device(): call(lambda *refs: output_kernel(n_rows, *refs), (shape(near_blocks.shape...  7.34 us
  transfers between devices with their start and end apart: 21, of which 9 were waited for; matrix products, arithmetic and copies ran while one was open for 2% of the time, Pallas kernels for 59%

profile of v1, /device:TPU:0, one launch (start us, length us, event | category | flops | bytes accessed | tf_op | source)
XLA Modules:
  0.0 263.5 jit_solution(5693812742948481045)
XLA Ops:
  0.6 1.1 copy-done.7
  1.8 0.9 copy-done.8
  2.7 0.3 pack_rows.1
  3.0 0.7 copy-done.12
  3.8 1.6 collective-permute-start
  5.4 5.1 %collective-permute-start.12 = (bf16[320,768]{1,0:T(8,128)(2,1)S(1)}, bf16[320,768]{1,0:T(8,128)(2,1)}, u32[]{:S(2)}, u32[]{:S(2)}) collective-permute-start(bf16[320,768]{1,0:T(8,128)(2,1)S(1)} %get-tuple-element.12.refs_2_), channel_id=1, source_target_pairs={{0,8},{4,12},{8,0},{12,4},{16,24},{20,28},{24,16},{28,20},{1,9},{5... | collective-permute-start | bytes 1474568 | tf_op jit(solution)/shard_map/ppermute | solution.py:294
  10.5 1.3 collective-permute-start.1
  11.8 1.2 copy-done.5
  13.0 1.0 copy-done.10
  14.0 0.5 pack_panel.1.refs_10_
  14.5 1.6 collective-permute-start.19
  16.1 5.4 %collective-permute-done.12.refs_4_ = bf16[320,768]{1,0:T(8,128)(2,1)} collective-permute-done((bf16[320,768]{1,0:T(8,128)(2,1)S(1)}, bf16[320,768]{1,0:T(8,128)(2,1)}, u32[]{:S(2)}, u32[]{:S(2)}) %collective-permute-start.12) | collective-permute-done | bytes 491552 | tf_op jit(solution)/shard_map/ppermute | solution.py:294
  21.5 1.4 collective-permute-start.15
  23.0 10.8 %collective-permute-done.1 = bf16[320,768]{1,0:T(8,128)(2,1)} collective-permute-done((bf16[320,768]{1,0:T(8,128)(2,1)}, bf16[320,768]{1,0:T(8,128)(2,1)}, u32[]{:S(2)}, u32[]{:S(2)}) %collective-permute-start.1) | collective-permute-done | bytes 491552 | tf_op jit(solution)/shard_map/ppermute | solution.py:294
  33.8 1.1 broadcast_select_fusion.1.refs_6_
  35.0 1.5 collective-permute-start.5
  36.4 1.3 collective-permute-start.16
  37.7 8.9 %collective-permute-done.3.refs_4_ = bf16[256,768]{1,0:T(8,128)(2,1)} collective-permute-done((bf16[256,768]{1,0:T(8,128)(2,1)}, bf16[256,768]{1,0:T(8,128)(2,1)}, u32[]{:S(2)}, u32[]{:S(2)}) %collective-permute-start.3) | collective-permute-done | bytes 393248 | tf_op jit(solution)/shard_map/ppermute | solution.py:294
  46.6 1.4 collective-permute-start.8
  48.1 0.5 collective-permute-start.20
  48.6 1.5 collective-permute-start.11
  50.1 0.1 copy.10.refs_0_
  50.2 5.0 %collective-permute-done.16 = bf16[320,768]{1,0:T(8,128)(2,1)} collective-permute-done((bf16[320,768]{1,0:T(8,128)(2,1)}, bf16[320,768]{1,0:T(8,128)(2,1)}, u32[]{:S(2)}, u32[]{:S(2)}) %collective-permute-start.16) | collective-permute-done | bytes 491552 | tf_op jit(solution)/shard_map/ppermute | solution.py:294
  55.2 1.3 collective-permute-start.6
  56.5 1.3 collective-permute-start.9
  57.8 0.1 stack.50.refs_0_.refs_1_
  57.8 2.0 target_sketch.1.refs_14_
  59.9 1.5 broadcast_select_fusion.refs_8_
  61.4 0.7 collective-permute-done.11.refs_3_
  62.1 1.5 collective-permute-start.13
  63.6 5.8 %collective-permute-done.6 = bf16[256,768]{1,0:T(8,128)(2,1)} collective-permute-done((bf16[256,768]{1,0:T(8,128)(2,1)}, bf16[256,768]{1,0:T(8,128)(2,1)}, u32[]{:S(2)}, u32[]{:S(2)}) %collective-permute-start.6) | collective-permute-done | bytes 393248 | tf_op jit(solution)/shard_map/ppermute | solution.py:294
  69.4 1.5 collective-permute-start.14
  70.9 2.8 %collective-permute-done.9 = bf16[256,768]{1,0:T(8,128)(2,1)} collective-permute-done((bf16[256,768]{1,0:T(8,128)(2,1)}, bf16[256,768]{1,0:T(8,128)(2,1)}, u32[]{:S(2)}, u32[]{:S(2)}) %collective-permute-start.9) | collective-permute-done | bytes 393248 | tf_op jit(solution)/shard_map/ppermute | solution.py:294
  73.7 1.5 collective-permute-start.17
  75.2 1.0 broadcast_select_fusion.3.refs_6_
  76.2 1.1 broadcast_select_fusion.2.refs_8_
  77.3 0.7 collective-permute-start.2
  78.0 1.4 collective-permute-start.4
  79.4 7.6 %collective-permute-done.14.refs_7_ = bf16[320,768]{1,0:T(8,128)(2,1)S(1)} collective-permute-done((bf16[320,768]{1,0:T(8,128)(2,1)S(1)}, bf16[320,768]{1,0:T(8,128)(2,1)S(1)}, u32[]{:S(2)}, u32[]{:S(2)}) %collective-permute-start.14) | collective-permute-done | bytes 491552 | tf_op jit(solution)/shard_map/ppermute | solution.py:294
  87.0 1.5 collective-permute-start.7
  88.5 9.0 %collective-permute-done.17.refs_9_ = bf16[320,768]{1,0:T(8,128)(2,1)S(1)} collective-permute-done((bf16[320,768]{1,0:T(8,128)(2,1)S(1)}, bf16[320,768]{1,0:T(8,128)(2,1)S(1)}, u32[]{:S(2)}, u32[]{:S(2)}) %collective-permute-start.17) | collective-permute-done | bytes 491552 | tf_op jit(solution)/shard_map/ppermute | solution.py:294
  97.5 1.5 collective-permute-start.10
  99.0 15.6 %sampled.1 = (bf16[8,512,768]{2,1,0:T(8,128)(2,1)}, f32[4,256,384]{2,1,0:T(8,128)}, bf16[4,2048,256]{2,1,0:T(8,128)(2,1)}) custom-call(s32[8]{0:T(128)S(1)} %stack.50.refs_0_.refs_1_, s32[4]{0:T(128)S(1)} %pad_add_fusion.refs_1_, bf16[320,768]{1,0:T(8,128)(2,1)S(1)} %copy-done.15, bf16[320,768]{1,0:T(8,128)(2,1)} %collective-permute-done.11.refs_3_, ...), custom_call_target="tpu_custom_call" | custom-call | flops 3221225472 | bytes 10223616 | tf_op jit(solution)/shard_map/sampled/pallas_call | solution.py:374
  114.7 1.4 copy-done.4
  116.1 125.7 %basis.1.refs_1_.refs_10_ = bf16[4,256,384]{2,1,0:T(8,128)(2,1)S(1)} custom-call(f32[4,256,384]{2,1,0:T(8,128)S(1)} %copy-done.4), custom_call_target="tpu_custom_call" | custom-call | flops 201326592 | bytes 2359296 | tf_op jit(solution)/shard_map/basis/pallas_call | solution.py:392
  241.8 13.0 %cores.1 = (bf16[6,256,1024]{2,1,0:T(8,128)(2,1)}, f32[6,256,256]{2,1,0:T(8,128)S(1)}, bf16[4,256,1024]{2,1,0:T(8,128)(2,1)}) custom-call(s32[4,1]{1,0:T(4,128)S(1)} %copy.10.refs_0_, bf16[4,256,384]{2,1,0:T(8,128)(2,1)S(1)} %basis.1.refs_1_.refs_10_, bf16[8,512,768]{2,1,0:T(8,128)(2,1)} %get-tuple-element.15.refs_2_, ...), custom_call_target="tpu_custom_call" | custom-call | flops 2415919104 | bytes 10223616 | tf_op jit(solution)/shard_map/cores/pallas_call | solution.py:402
  254.8 1.2 copy-done.2
  256.0 7.3 %output.1 = (bf16[4,1,256,256]{3,2,1,0:T(8,128)(2,1)}, bf16[4,6,256,128]{3,2,1,0:T(8,128)(2,1)}) custom-call(s32[4,1]{1,0:T(4,128)S(1)} %copy.10.refs_0_, s32[8]{0:T(128)S(1)} %stack.50.refs_0_.refs_1_, bf16[256,768]{1,0:T(8,128)(2,1)S(1)} %copy-done.13, bf16[256,768]{1,0:T(8,128)(2,1)S(1)} %collective-permute-done.2.refs_3_, ...), custom_call_target="tpu_custom_call" | custom-call | flops 805306368 | bytes 3145728 | tf_op jit(solution)/shard_map/output/pallas_call | solution.py:415
  (42 shorter events, 0.2 us)
Async XLA Ops:
  0.6 1.1 copy-start.7
  1.8 0.9 copy-start.8
  2.7 55.2 %copy-start.9 = (bf16[6,256,64]{1,2,0:T(8,128)(2,1)S(1)}, bf16[6,256,64]{1,2,0:T(8,128)(2,1)}, u32[]{:S(2)}) copy-start(bf16[6,256,64]{1,2,0:T(8,128)(2,1)} %param.13) | copy-start | bytes 589828
  3.0 0.8 copy-start.12
  3.8 19.2 %copy-start.14 = (bf16[320,768]{1,0:T(8,128)(2,1)}, bf16[320,768]{1,0:T(8,128)(2,1)S(1)}, u32[]{:S(2)}) copy-start(bf16[320,768]{1,0:T(8,128)(2,1)S(1)} %get-tuple-element.12.refs_2_) | copy-start | bytes 1474564
  3.8 46.3 %copy-start.16 = (s32[4,1]{0,1:T(1,128)S(1)}, s32[4,1]{0,1:T(1,128)}, u32[]{:S(2)}) copy-start(s32[4,1]{0,1:T(1,128)} %param.12) | copy-start | bytes 52
  3.8 54.1 %copy-start.1 = (bf16[4,6,256,128]{3,2,1,0:T(8,128)(2,1)S(1)}, bf16[4,6,256,128]{3,2,1,0:T(8,128)(2,1)}, u32[]{:S(2)}) copy-start(bf16[4,6,256,128]{3,2,1,0:T(8,128)(2,1)} %refs_4_.1) | copy-start | bytes 4718596
  3.8 6.7 %collective-permute-start = (bf16[320,768]{1,0:T(8,128)(2,1)S(1)}, bf16[320,768]{1,0:T(8,128)(2,1)}, u32[]{:S(2)}, u32[]{:S(2)}) collective-permute-start(bf16[320,768]{1,0:T(8,128)(2,1)S(1)} %get-tuple-element.12.refs_2_), channel_id=1, source_target_pairs={{8,16},{16,8},{12,20},{20,12},{9,17},{17,9},{13,21},{21,13},{10,18... | collective-permute-start | bytes 1474568 | tf_op jit(solution)/shard_map/ppermute | solution.py:294
  5.4 16.2 %collective-permute-start.12 = (bf16[320,768]{1,0:T(8,128)(2,1)S(1)}, bf16[320,768]{1,0:T(8,128)(2,1)}, u32[]{:S(2)}, u32[]{:S(2)}) collective-permute-start(bf16[320,768]{1,0:T(8,128)(2,1)S(1)} %get-tuple-element.12.refs_2_), channel_id=1, source_target_pairs={{0,8},{4,12},{8,0},{12,4},{16,24},{20,28},{24,16},{28,20},{1,9},{5... | collective-permute-start | bytes 1474568 | tf_op jit(solution)/shard_map/ppermute | solution.py:294
  10.5 23.3 %collective-permute-start.1 = (bf16[320,768]{1,0:T(8,128)(2,1)}, bf16[320,768]{1,0:T(8,128)(2,1)}, u32[]{:S(2)}, u32[]{:S(2)}) collective-permute-start(bf16[320,768]{1,0:T(8,128)(2,1)} %collective-permute-done), channel_id=1, source_target_pairs={{8,0},{12,4},{16,24},{20,28},{9,1},{13,5},{17,25},{21,29},{10,2},{... | collective-permute-start | bytes 1474568 | tf_op jit(solution)/shard_map/ppermute | solution.py:294
  11.8 1.2 copy-start.5
  13.0 1.0 copy-start.10
  14.5 45.3 %copy-start.6 = (bf16[2048,256]{1,0:T(8,128)(2,1)}, bf16[2048,256]{1,0:T(8,128)(2,1)S(1)}, u32[]{:S(2)}) copy-start(bf16[2048,256]{1,0:T(8,128)(2,1)S(1)} %pack_panel.1.refs_10_) | copy-start | bytes 3145732
  14.5 33.5 %collective-permute-start.19 = (bf16[2048,256]{1,0:T(8,128)(2,1)S(1)}, bf16[2048,256]{1,0:T(8,128)(2,1)}, u32[]{:S(2)}, u32[]{:S(2)}) collective-permute-start(bf16[2048,256]{1,0:T(8,128)(2,1)S(1)} %pack_panel.1.refs_10_), channel_id=1, source_target_pairs={{0,2},{1,3},{2,0},{3,1},{4,6},{5,7},{6,4},{7,5},{8,10},{9,11},{10,... | collective-permute-start | bytes 3145736 | tf_op jit(solution)/shard_map/ppermute | solution.py:323
  21.5 14.9 %collective-permute-start.15 = (bf16[320,768]{1,0:T(8,128)(2,1)}, bf16[320,768]{1,0:T(8,128)(2,1)}, u32[]{:S(2)}, u32[]{:S(2)}) collective-permute-start(bf16[320,768]{1,0:T(8,128)(2,1)} %collective-permute-done.12.refs_4_), channel_id=1, source_target_pairs={{8,16},{16,8},{12,20},{20,12},{9,17},{17,9},{13,21},{21,13},{10,18... | collective-permute-start | bytes 1474568 | tf_op jit(solution)/shard_map/ppermute | solution.py:294
  34.9 11.7 %collective-permute-start.3 = (bf16[256,768]{1,0:T(8,128)(2,1)}, bf16[256,768]{1,0:T(8,128)(2,1)}, u32[]{:S(2)}, u32[]{:S(2)}) collective-permute-start(bf16[256,768]{1,0:T(8,128)(2,1)} %copy-done.12), channel_id=1, source_target_pairs={{0,8},{4,12},{8,0},{12,4},{16,24},{20,28},{24,16},{28,20},{1,9},{5... | collective-permute-start | bytes 1179656 | tf_op jit(solution)/shard_map/ppermute | solution.py:294
  35.0 13.6 %collective-permute-start.5 = (bf16[256,768]{1,0:T(8,128)(2,1)}, bf16[256,768]{1,0:T(8,128)(2,1)}, u32[]{:S(2)}, u32[]{:S(2)}) collective-permute-start(bf16[256,768]{1,0:T(8,128)(2,1)} %copy-done.12), channel_id=1, source_target_pairs={{8,16},{16,8},{12,20},{20,12},{9,17},{17,9},{13,21},{21,13},{10,18... | collective-permute-start | bytes 1179656 | tf_op jit(solution)/shard_map/ppermute | solution.py:294
  36.4 18.7 %collective-permute-start.16 = (bf16[320,768]{1,0:T(8,128)(2,1)}, bf16[320,768]{1,0:T(8,128)(2,1)}, u32[]{:S(2)}, u32[]{:S(2)}) collective-permute-start(bf16[320,768]{1,0:T(8,128)(2,1)} %collective-permute-done.15), channel_id=1, source_target_pairs={{8,0},{12,4},{16,24},{20,28},{9,1},{13,5},{17,25},{21,29},{10,2},{... | collective-permute-start | bytes 1474568 | tf_op jit(solution)/shard_map/ppermute | solution.py:294
  46.6 9.8 %collective-permute-start.8 = (bf16[256,768]{1,0:T(8,128)(2,1)}, bf16[256,768]{1,0:T(8,128)(2,1)}, u32[]{:S(2)}, u32[]{:S(2)}) collective-permute-start(bf16[256,768]{1,0:T(8,128)(2,1)} %collective-permute-done.3.refs_4_), channel_id=1, source_target_pairs={{8,16},{16,8},{12,20},{20,12},{9,17},{17,9},{13,21},{21,13},{10,18... | collective-permute-start | bytes 1179656 | tf_op jit(solution)/shard_map/ppermute | solution.py:294
  48.1 29.9 %collective-permute-start.18 = (bf16[2048,256]{1,0:T(8,128)(2,1)S(1)}, bf16[2048,256]{1,0:T(8,128)(2,1)}, u32[]{:S(2)}, u32[]{:S(2)}) collective-permute-start(bf16[2048,256]{1,0:T(8,128)(2,1)S(1)} %pack_panel.1.refs_10_), channel_id=1, source_target_pairs={{0,1},{1,0},{2,3},{3,2},{4,5},{5,4},{6,7},{7,6},{8,9},{9,8},{10,11... | collective-permute-start | bytes 3145736 | tf_op jit(solution)/shard_map/ppermute | solution.py:324
  48.1 51.0 %collective-permute-start.20 = (bf16[2048,256]{1,0:T(8,128)(2,1)}, bf16[2048,256]{1,0:T(8,128)(2,1)}, u32[]{:S(2)}, u32[]{:S(2)}) collective-permute-start(bf16[2048,256]{1,0:T(8,128)(2,1)} %collective-permute-done.19.refs_12_), channel_id=1, source_target_pairs={{0,1},{1,0},{2,3},{3,2},{4,5},{5,4},{6,7},{7,6},{8,9},{9,8},{10,11... | collective-permute-start | bytes 3145736 | tf_op jit(solution)/shard_map/ppermute | solution.py:325
  48.6 13.5 %collective-permute-start.11 = (bf16[320,768]{1,0:T(8,128)(2,1)}, bf16[320,768]{1,0:T(8,128)(2,1)}, u32[]{:S(2)}, u32[]{:S(2)}) collective-permute-start(bf16[320,768]{1,0:T(8,128)(2,1)} %copy-done.14), channel_id=1, source_target_pairs={{0,4},{4,0},{8,12},{12,8},{16,20},{20,16},{24,28},{28,24},{1,5},{5... | collective-permute-start | bytes 1474568 | tf_op jit(solution)/shard_map/ppermute | solution.py:294
  55.2 14.3 %collective-permute-start.6 = (bf16[256,768]{1,0:T(8,128)(2,1)}, bf16[256,768]{1,0:T(8,128)(2,1)}, u32[]{:S(2)}, u32[]{:S(2)}) collective-permute-start(bf16[256,768]{1,0:T(8,128)(2,1)} %collective-permute-done.5), channel_id=1, source_target_pairs={{8,0},{12,4},{16,24},{20,28},{9,1},{13,5},{17,25},{21,29},{10,2},{... | collective-permute-start | bytes 1179656 | tf_op jit(solution)/shard_map/ppermute | solution.py:294
  56.5 17.2 %collective-permute-start.9 = (bf16[256,768]{1,0:T(8,128)(2,1)}, bf16[256,768]{1,0:T(8,128)(2,1)}, u32[]{:S(2)}, u32[]{:S(2)}) collective-permute-start(bf16[256,768]{1,0:T(8,128)(2,1)} %collective-permute-done.8), channel_id=1, source_target_pairs={{8,0},{12,4},{16,24},{20,28},{9,1},{13,5},{17,25},{21,29},{10,2},{... | collective-permute-start | bytes 1179656 | tf_op jit(solution)/shard_map/ppermute | solution.py:294
  59.8 17.5 %copy-start.3 = (f32[4,256,384]{2,1,0:T(8,128)}, f32[4,256,384]{2,1,0:T(8,128)S(1)}, u32[]{:S(2)}) copy-start(f32[4,256,384]{2,1,0:T(8,128)S(1)} %target_sketch.1.refs_14_) | copy-start | bytes 4718596
  59.9 17.4 %copy-start.13 = (bf16[256,768]{1,0:T(8,128)(2,1)S(1)}, bf16[256,768]{1,0:T(8,128)(2,1)}, u32[]{:S(2)}) copy-start(bf16[256,768]{1,0:T(8,128)(2,1)} %copy-done.12) | copy-start | bytes 1179652
  59.9 39.1 %copy-start.15 = (bf16[320,768]{1,0:T(8,128)(2,1)S(1)}, bf16[320,768]{1,0:T(8,128)(2,1)}, u32[]{:S(2)}) copy-start(bf16[320,768]{1,0:T(8,128)(2,1)} %copy-done.14) | copy-start | bytes 1474564
  62.1 15.2 %collective-permute-start.13 = (bf16[320,768]{1,0:T(8,128)(2,1)}, bf16[320,768]{1,0:T(8,128)(2,1)S(1)}, u32[]{:S(2)}, u32[]{:S(2)}) collective-permute-start(bf16[320,768]{1,0:T(8,128)(2,1)} %collective-permute-done.12.refs_4_), channel_id=1, source_target_pairs={{0,4},{4,0},{8,12},{12,8},{16,20},{20,16},{24,28},{28,24},{1,5},{5... | collective-permute-start | bytes 1474568 | tf_op jit(solution)/shard_map/ppermute | solution.py:294
  69.4 17.6 %collective-permute-start.14 = (bf16[320,768]{1,0:T(8,128)(2,1)S(1)}, bf16[320,768]{1,0:T(8,128)(2,1)S(1)}, u32[]{:S(2)}, u32[]{:S(2)}) collective-permute-start(bf16[320,768]{1,0:T(8,128)(2,1)S(1)} %broadcast_select_fusion.1.refs_6_), channel_id=1, source_target_pairs={{0,4},{4,0},{8,12},{12,8},{16,20},{20,16},{24,28},{28,24},{1,5},{5... | collective-permute-start | bytes 1474568 | tf_op jit(solution)/shard_map/ppermute | solution.py:294
  73.7 23.9 %collective-permute-start.17 = (bf16[320,768]{1,0:T(8,128)(2,1)S(1)}, bf16[320,768]{1,0:T(8,128)(2,1)S(1)}, u32[]{:S(2)}, u32[]{:S(2)}) collective-permute-start(bf16[320,768]{1,0:T(8,128)(2,1)S(1)} %broadcast_select_fusion.refs_8_), channel_id=1, source_target_pairs={{0,4},{4,0},{8,12},{12,8},{16,20},{20,16},{24,28},{28,24},{1,5},{5... | collective-permute-start | bytes 1474568 | tf_op jit(solution)/shard_map/ppermute | solution.py:294
  77.3 178.7 %collective-permute-start.2 = (bf16[256,768]{1,0:T(8,128)(2,1)S(1)}, bf16[256,768]{1,0:T(8,128)(2,1)S(1)}, u32[]{:S(2)}, u32[]{:S(2)}) collective-permute-start(bf16[256,768]{1,0:T(8,128)(2,1)S(1)} %copy-done.13), channel_id=1, source_target_pairs={{0,4},{4,0},{8,12},{12,8},{16,20},{20,16},{24,28},{28,24},{1,5},{5... | collective-permute-start | bytes 1179656 | tf_op jit(solution)/shard_map/ppermute | solution.py:294
  78.0 178.0 %collective-permute-start.4 = (bf16[256,768]{1,0:T(8,128)(2,1)}, bf16[256,768]{1,0:T(8,128)(2,1)S(1)}, u32[]{:S(2)}, u32[]{:S(2)}) collective-permute-start(bf16[256,768]{1,0:T(8,128)(2,1)} %collective-permute-done.3.refs_4_), channel_id=1, source_target_pairs={{0,4},{4,0},{8,12},{12,8},{16,20},{20,16},{24,28},{28,24},{1,5},{5... | collective-permute-start | bytes 1179656 | tf_op jit(solution)/shard_map/ppermute | solution.py:294
  87.0 169.0 %collective-permute-start.7 = (bf16[256,768]{1,0:T(8,128)(2,1)S(1)}, bf16[256,768]{1,0:T(8,128)(2,1)S(1)}, u32[]{:S(2)}, u32[]{:S(2)}) collective-permute-start(bf16[256,768]{1,0:T(8,128)(2,1)S(1)} %broadcast_select_fusion.3.refs_6_), channel_id=1, source_target_pairs={{0,4},{4,0},{8,12},{12,8},{16,20},{20,16},{24,28},{28,24},{1,5},{5... | collective-permute-start | bytes 1179656 | tf_op jit(solution)/shard_map/ppermute | solution.py:294
  97.5 158.5 %collective-permute-start.10 = (bf16[256,768]{1,0:T(8,128)(2,1)S(1)}, bf16[256,768]{1,0:T(8,128)(2,1)S(1)}, u32[]{:S(2)}, u32[]{:S(2)}) collective-permute-start(bf16[256,768]{1,0:T(8,128)(2,1)S(1)} %broadcast_select_fusion.2.refs_8_), channel_id=1, source_target_pairs={{0,4},{4,0},{8,12},{12,8},{16,20},{20,16},{24,28},{28,24},{1,5},{5... | collective-permute-start | bytes 1179656 | tf_op jit(solution)/shard_map/ppermute | solution.py:294
  114.7 1.4 copy-start.4
  241.8 13.0 %copy-start = (bf16[4,256,384]{2,1,0:T(8,128)(2,1)}, bf16[4,256,384]{2,1,0:T(8,128)(2,1)S(1)}, u32[]{:S(2)}) copy-start(bf16[4,256,384]{2,1,0:T(8,128)(2,1)S(1)} %basis.1.refs_1_.refs_10_) | copy-start | bytes 2359300
  241.8 14.2 %copy-start.11 = (bf16[4,1,256,256]{3,2,1,0:T(8,128)(2,1)S(1)}, bf16[4,1,256,256]{3,2,1,0:T(8,128)(2,1)}, u32[]{:S(2)}) copy-start(bf16[4,1,256,256]{3,2,1,0:T(8,128)(2,1)} %refs_14_.1) | copy-start | bytes 1572868
  254.8 1.2 copy-start.2

commit v2 on v1

--- a/solution.py
+++ b/solution.py
@@ -169,27 +169,55 @@
             state[g] = jnp.where(first, (lane == row).astype(F32), gram[:half])
             state[n_even + g] = jnp.where(first, gram[half:], (lane == row + half).astype(F32))
     sub = 8
-    for block in range(half // sub):
-
-        def eliminate(q, carry, block=block):
-            pivot = block * sub + q
-            below = lax.broadcasted_iota(jnp.int32, (sub, width), 0) > q
-            for g in range(2 * n_even):
-                offset = half if g < n_even else 0
-                index = jnp.full((sub, width), pivot + offset, jnp.int32)
-                line = jnp.broadcast_to(state[g, pl.ds(pivot, 1), :], (sub, width))
-                top = jnp.take_along_axis(line, index, axis=1)
-                line = line / top
-                for v in range(block, half // sub):
-                    rows = pl.ds(v * sub, sub)
-                    tile = state[g, rows, :]
-                    column = jnp.take_along_axis(tile, index, axis=1)
-                    if v == block:
-                        column = jnp.where(below, column, 0.0)
-                    state[g, rows, :] = tile - column * line
-            return carry
-
-        lax.fori_loop(0, sub, eliminate, 0)
+    total = 2 * n_even
+    offsets = [half if g < n_even else 0 for g in range(total)]
+    sublane = lax.broadcasted_iota(jnp.int32, (sub, width), 0)
+
+    def pick(tile, index):
+        return jnp.take_along_axis(tile, index, axis=1)
+
+    def spread(tile, q):
+        return jnp.broadcast_to(tile[q : q + 1], (sub, width))
+
+    def one_block(block, carry):
+        start = pl.multiple_of(block * sub, sub)
+        tiles = [state[g, pl.ds(start, sub), :] for g in range(total)]
+
+        def lanes_of(q):
+            index = jnp.full((sub, width), start + q, jnp.int32)
+            return {0: index, half: index + half}
+
+        for q in range(sub - 1):
+            index = lanes_of(q)
+            columns_q = [pick(tile, index[off]) for tile, off in zip(tiles, offsets)]
+            lines = [spread(tile, q) / spread(column, q) for tile, column in zip(tiles, columns_q)]
+            below = sublane > q
+            tiles = [
+                tile - jnp.where(below, column, 0.0) * line for tile, column, line in zip(tiles, columns_q, lines)
+            ]
+        on_diag = {off: start + off + sublane for off in (0, half)}
+        scaled = []
+        for g in range(total):
+            state[g, pl.ds(start, sub), :] = tiles[g]
+            scaled.append(tiles[g] / pick(tiles[g], on_diag[offsets[g]]))
+
+        def update(v, inner):
+            rows = pl.ds(pl.multiple_of(v * sub, sub), sub)
+            below_tiles = [state[g, rows, :] for g in range(total)]
+            for q in range(sub):
+                index = lanes_of(q)
+                below_tiles = [
+                    tile - pick(tile, index[off]) * spread(line, q)
+                    for tile, off, line in zip(below_tiles, offsets, scaled)
+                ]
+            for g in range(total):
+                state[g, rows, :] = below_tiles[g]
+            return inner
+
+        lax.fori_loop(block + 1, half // sub, update, 0)
+        return carry
+
+    lax.fori_loop(0, half // sub, one_block, 0)
     for i in range(count):
         for p in range(pairs):
             g = i * pairs + p

time: 265 us -> 164 us (0.62)
  Pallas kernels: 164 us -> 63.7 us
    pallas_call x1, Pallas kernels: 126 us -> 24.9 us  [per_device(): call(basis_kernel, shape((count, size, wide), BF16), [IN_VMEM], [vmem((co...]
  transfers between devices with their start and end apart: 21 -> 21, of which waited for: 9 -> 9; matrix products, arithmetic and copies ran while one was open for 2% -> 3% of each run, Pallas kernels for 59% -> 34%
where the time goes in v2:
time: 164 us; the launch traced here: 163 us
  Pallas kernels  63.7 us (39%)
  waiting for transfers between devices  56 us (34%)
  starting transfers between devices  29.5 us (18%)
  local copies, waits for them, and re-layouts  7.87 us (5%)
  other arithmetic  4.78 us (3%)
    ppermute x18, waiting for transfers between devices, gather_rows(): send = lambda value, pairs: lax.ppermute(value, 'rows', pairs)  56 us
    ppermute x18, starting transfers between devices, gather_rows(): send = lambda value, pairs: lax.ppermute(value, 'rows', pairs)  27.4 us
    pallas_call x1, Pallas kernels, per_device(): call(basis_kernel, shape((count, size, wide), BF16), [IN_VMEM], [vmem((co...  24.9 us
    pallas_call x1, Pallas kernels, per_device(): call(lambda *refs: sampled_kernel(n_rows, n_cols, *refs), (shape((n_rows,...  15.6 us
    pallas_call x1, Pallas kernels, per_device(): call(lambda *refs: cores_kernel(n_rows, *refs), (shape((columns, count *...  13 us
    unnamed x35, local copies, waits for them, and re-layouts  7.78 us
    pallas_call x1, Pallas kernels, per_device(): call(lambda *refs: output_kernel(n_rows, *refs), (shape(near_blocks.shape...  7.37 us
  transfers between devices with their start and end apart: 21, of which 9 were waited for; matrix products, arithmetic and copies ran while one was open for 3% of the time, Pallas kernels for 34%

profile of v2, /device:TPU:0, one launch (start us, length us, event | category | flops | bytes accessed | tf_op | source)
XLA Modules:
  0.0 162.8 jit_solution(8674372872833810499)
XLA Ops:
  0.6 1.1 copy-done.7
  1.8 0.9 copy-done.8
  2.7 0.3 pack_rows.1
  3.0 0.7 copy-done.12
  3.8 1.6 collective-permute-start
  5.4 5.1 %collective-permute-start.12 = (bf16[320,768]{1,0:T(8,128)(2,1)S(1)}, bf16[320,768]{1,0:T(8,128)(2,1)}, u32[]{:S(2)}, u32[]{:S(2)}) collective-permute-start(bf16[320,768]{1,0:T(8,128)(2,1)S(1)} %get-tuple-element.12.refs_2_), channel_id=1, source_target_pairs={{0,8},{4,12},{8,0},{12,4},{16,24},{20,28},{24,16},{28,20},{1,9},{5... | collective-permute-start | bytes 1474568 | tf_op jit(solution)/shard_map/ppermute | solution.py:322
  10.5 1.3 collective-permute-start.1
  11.8 1.2 copy-done.5
  13.0 1.0 copy-done.10
  14.0 0.5 pack_panel.1.refs_10_
  14.5 1.6 collective-permute-start.19
  16.1 5.4 %collective-permute-done.12.refs_4_ = bf16[320,768]{1,0:T(8,128)(2,1)} collective-permute-done((bf16[320,768]{1,0:T(8,128)(2,1)S(1)}, bf16[320,768]{1,0:T(8,128)(2,1)}, u32[]{:S(2)}, u32[]{:S(2)}) %collective-permute-start.12) | collective-permute-done | bytes 491552 | tf_op jit(solution)/shard_map/ppermute | solution.py:322
  21.5 1.4 collective-permute-start.15
  23.0 10.8 %collective-permute-done.1 = bf16[320,768]{1,0:T(8,128)(2,1)} collective-permute-done((bf16[320,768]{1,0:T(8,128)(2,1)}, bf16[320,768]{1,0:T(8,128)(2,1)}, u32[]{:S(2)}, u32[]{:S(2)}) %collective-permute-start.1) | collective-permute-done | bytes 491552 | tf_op jit(solution)/shard_map/ppermute | solution.py:322
  33.8 1.1 broadcast_select_fusion.1.refs_6_
  35.0 1.5 collective-permute-start.5
  36.4 1.3 collective-permute-start.16
  37.7 8.9 %collective-permute-done.3.refs_4_ = bf16[256,768]{1,0:T(8,128)(2,1)} collective-permute-done((bf16[256,768]{1,0:T(8,128)(2,1)}, bf16[256,768]{1,0:T(8,128)(2,1)}, u32[]{:S(2)}, u32[]{:S(2)}) %collective-permute-start.3) | collective-permute-done | bytes 393248 | tf_op jit(solution)/shard_map/ppermute | solution.py:322
  46.6 1.4 collective-permute-start.8
  48.1 0.5 collective-permute-start.20
  48.6 1.5 collective-permute-start.11
  50.1 0.1 copy.10.refs_0_
  50.2 5.0 %collective-permute-done.16 = bf16[320,768]{1,0:T(8,128)(2,1)} collective-permute-done((bf16[320,768]{1,0:T(8,128)(2,1)}, bf16[320,768]{1,0:T(8,128)(2,1)}, u32[]{:S(2)}, u32[]{:S(2)}) %collective-permute-start.16) | collective-permute-done | bytes 491552 | tf_op jit(solution)/shard_map/ppermute | solution.py:322
  55.2 1.3 collective-permute-start.6
  56.5 1.3 collective-permute-start.9
  57.8 0.1 stack.50.refs_0_.refs_1_
  57.8 2.0 %target_sketch.1.refs_14_ = f32[4,256,384]{2,1,0:T(8,128)S(1)} custom-call(bf16[4,6,256,128]{3,2,1,0:T(8,128)(2,1)S(1)} %copy-done.1, bf16[6,64,256]{2,1,0:T(8,128)(2,1)S(1)} %bitcast.14), custom_call_target="tpu_custom_call" | custom-call | flops 201326592 | bytes 3145728 | tf_op jit(solution)/shard_map/target_sketch/pallas_call | solution.py:387
  59.9 1.5 broadcast_select_fusion.refs_8_
  61.4 0.7 collective-permute-done.11.refs_3_
  62.1 1.5 collective-permute-start.13
  63.6 5.8 %collective-permute-done.6 = bf16[256,768]{1,0:T(8,128)(2,1)} collective-permute-done((bf16[256,768]{1,0:T(8,128)(2,1)}, bf16[256,768]{1,0:T(8,128)(2,1)}, u32[]{:S(2)}, u32[]{:S(2)}) %collective-permute-start.6) | collective-permute-done | bytes 393248 | tf_op jit(solution)/shard_map/ppermute | solution.py:322
  69.4 1.5 collective-permute-start.14
  70.9 2.8 %collective-permute-done.9 = bf16[256,768]{1,0:T(8,128)(2,1)} collective-permute-done((bf16[256,768]{1,0:T(8,128)(2,1)}, bf16[256,768]{1,0:T(8,128)(2,1)}, u32[]{:S(2)}, u32[]{:S(2)}) %collective-permute-start.9) | collective-permute-done | bytes 393248 | tf_op jit(solution)/shard_map/ppermute | solution.py:322
  73.7 1.5 collective-permute-start.17
  75.2 1.0 broadcast_select_fusion.3.refs_6_
  76.2 1.1 broadcast_select_fusion.2.refs_8_
  77.3 0.7 collective-permute-start.2
  78.0 1.4 collective-permute-start.4
  79.4 7.6 %collective-permute-done.14.refs_7_ = bf16[320,768]{1,0:T(8,128)(2,1)S(1)} collective-permute-done((bf16[320,768]{1,0:T(8,128)(2,1)S(1)}, bf16[320,768]{1,0:T(8,128)(2,1)S(1)}, u32[]{:S(2)}, u32[]{:S(2)}) %collective-permute-start.14) | collective-permute-done | bytes 491552 | tf_op jit(solution)/shard_map/ppermute | solution.py:322
  87.0 1.5 collective-permute-start.7
  88.5 9.0 %collective-permute-done.17.refs_9_ = bf16[320,768]{1,0:T(8,128)(2,1)S(1)} collective-permute-done((bf16[320,768]{1,0:T(8,128)(2,1)S(1)}, bf16[320,768]{1,0:T(8,128)(2,1)S(1)}, u32[]{:S(2)}, u32[]{:S(2)}) %collective-permute-start.17) | collective-permute-done | bytes 491552 | tf_op jit(solution)/shard_map/ppermute | solution.py:322
  97.5 1.5 collective-permute-start.10
  99.0 15.6 %sampled.1 = (bf16[8,512,768]{2,1,0:T(8,128)(2,1)}, f32[4,256,384]{2,1,0:T(8,128)}, bf16[4,2048,256]{2,1,0:T(8,128)(2,1)}) custom-call(s32[8]{0:T(128)S(1)} %stack.50.refs_0_.refs_1_, s32[4]{0:T(128)S(1)} %pad_add_fusion.refs_1_, bf16[320,768]{1,0:T(8,128)(2,1)S(1)} %copy-done.15, bf16[320,768]{1,0:T(8,128)(2,1)} %collective-permute-done.11.refs_3_, ...), custom_call_target="tpu_custom_call" | custom-call | flops 3221225472 | bytes 10223616 | tf_op jit(solution)/shard_map/sampled/pallas_call | solution.py:402
  114.7 1.4 copy-done.4
  116.1 24.9 %basis.1.refs_1_.refs_10_ = bf16[4,256,384]{2,1,0:T(8,128)(2,1)S(1)} custom-call(f32[4,256,384]{2,1,0:T(8,128)S(1)} %copy-done.4), custom_call_target="tpu_custom_call" | custom-call | flops 201326592 | bytes 2359296 | tf_op jit(solution)/shard_map/basis/pallas_call | solution.py:420
  141.0 13.0 %cores.1 = (bf16[6,256,1024]{2,1,0:T(8,128)(2,1)}, f32[6,256,256]{2,1,0:T(8,128)S(1)}, bf16[4,256,1024]{2,1,0:T(8,128)(2,1)}) custom-call(s32[4,1]{1,0:T(4,128)S(1)} %copy.10.refs_0_, bf16[4,256,384]{2,1,0:T(8,128)(2,1)S(1)} %basis.1.refs_1_.refs_10_, bf16[8,512,768]{2,1,0:T(8,128)(2,1)} %get-tuple-element.15.refs_2_, ...), custom_call_target="tpu_custom_call" | custom-call | flops 2415919104 | bytes 10223616 | tf_op jit(solution)/shard_map/cores/pallas_call | solution.py:430
  154.0 1.2 copy-done.2
  155.2 7.4 %output.1 = (bf16[4,1,256,256]{3,2,1,0:T(8,128)(2,1)}, bf16[4,6,256,128]{3,2,1,0:T(8,128)(2,1)}) custom-call(s32[4,1]{1,0:T(4,128)S(1)} %copy.10.refs_0_, s32[8]{0:T(128)S(1)} %stack.50.refs_0_.refs_1_, bf16[256,768]{1,0:T(8,128)(2,1)S(1)} %copy-done.13, bf16[256,768]{1,0:T(8,128)(2,1)S(1)} %collective-permute-done.2.refs_3_, ...), custom_call_target="tpu_custom_call" | custom-call | flops 805306368 | bytes 3145728 | tf_op jit(solution)/shard_map/output/pallas_call | solution.py:443
  (42 shorter events, 0.2 us)
Async XLA Ops:
  0.6 1.1 copy-start.7
  1.8 0.9 copy-start.8
  2.7 55.2 %copy-start.9 = (bf16[6,256,64]{1,2,0:T(8,128)(2,1)S(1)}, bf16[6,256,64]{1,2,0:T(8,128)(2,1)}, u32[]{:S(2)}) copy-start(bf16[6,256,64]{1,2,0:T(8,128)(2,1)} %param.13) | copy-start | bytes 589828
  3.0 0.8 copy-start.12
  3.8 19.2 %copy-start.14 = (bf16[320,768]{1,0:T(8,128)(2,1)}, bf16[320,768]{1,0:T(8,128)(2,1)S(1)}, u32[]{:S(2)}) copy-start(bf16[320,768]{1,0:T(8,128)(2,1)S(1)} %get-tuple-element.12.refs_2_) | copy-start | bytes 1474564
  3.8 46.3 %copy-start.16 = (s32[4,1]{0,1:T(1,128)S(1)}, s32[4,1]{0,1:T(1,128)}, u32[]{:S(2)}) copy-start(s32[4,1]{0,1:T(1,128)} %param.12) | copy-start | bytes 52
  3.8 54.1 %copy-start.1 = (bf16[4,6,256,128]{3,2,1,0:T(8,128)(2,1)S(1)}, bf16[4,6,256,128]{3,2,1,0:T(8,128)(2,1)}, u32[]{:S(2)}) copy-start(bf16[4,6,256,128]{3,2,1,0:T(8,128)(2,1)} %refs_4_.1) | copy-start | bytes 4718596
  3.8 6.7 %collective-permute-start = (bf16[320,768]{1,0:T(8,128)(2,1)S(1)}, bf16[320,768]{1,0:T(8,128)(2,1)}, u32[]{:S(2)}, u32[]{:S(2)}) collective-permute-start(bf16[320,768]{1,0:T(8,128)(2,1)S(1)} %get-tuple-element.12.refs_2_), channel_id=1, source_target_pairs={{8,16},{16,8},{12,20},{20,12},{9,17},{17,9},{13,21},{21,13},{10,18... | collective-permute-start | bytes 1474568 | tf_op jit(solution)/shard_map/ppermute | solution.py:322
  5.4 16.2 %collective-permute-start.12 = (bf16[320,768]{1,0:T(8,128)(2,1)S(1)}, bf16[320,768]{1,0:T(8,128)(2,1)}, u32[]{:S(2)}, u32[]{:S(2)}) collective-permute-start(bf16[320,768]{1,0:T(8,128)(2,1)S(1)} %get-tuple-element.12.refs_2_), channel_id=1, source_target_pairs={{0,8},{4,12},{8,0},{12,4},{16,24},{20,28},{24,16},{28,20},{1,9},{5... | collective-permute-start | bytes 1474568 | tf_op jit(solution)/shard_map/ppermute | solution.py:322
  10.5 23.3 %collective-permute-start.1 = (bf16[320,768]{1,0:T(8,128)(2,1)}, bf16[320,768]{1,0:T(8,128)(2,1)}, u32[]{:S(2)}, u32[]{:S(2)}) collective-permute-start(bf16[320,768]{1,0:T(8,128)(2,1)} %collective-permute-done), channel_id=1, source_target_pairs={{8,0},{12,4},{16,24},{20,28},{9,1},{13,5},{17,25},{21,29},{10,2},{... | collective-permute-start | bytes 1474568 | tf_op jit(solution)/shard_map/ppermute | solution.py:322
  11.8 1.2 copy-start.5
  13.0 1.0 copy-start.10
  14.5 45.3 %copy-start.6 = (bf16[2048,256]{1,0:T(8,128)(2,1)}, bf16[2048,256]{1,0:T(8,128)(2,1)S(1)}, u32[]{:S(2)}) copy-start(bf16[2048,256]{1,0:T(8,128)(2,1)S(1)} %pack_panel.1.refs_10_) | copy-start | bytes 3145732
  14.5 33.5 %collective-permute-start.19 = (bf16[2048,256]{1,0:T(8,128)(2,1)S(1)}, bf16[2048,256]{1,0:T(8,128)(2,1)}, u32[]{:S(2)}, u32[]{:S(2)}) collective-permute-start(bf16[2048,256]{1,0:T(8,128)(2,1)S(1)} %pack_panel.1.refs_10_), channel_id=1, source_target_pairs={{0,2},{1,3},{2,0},{3,1},{4,6},{5,7},{6,4},{7,5},{8,10},{9,11},{10,... | collective-permute-start | bytes 3145736 | tf_op jit(solution)/shard_map/ppermute | solution.py:351
  21.5 14.9 %collective-permute-start.15 = (bf16[320,768]{1,0:T(8,128)(2,1)}, bf16[320,768]{1,0:T(8,128)(2,1)}, u32[]{:S(2)}, u32[]{:S(2)}) collective-permute-start(bf16[320,768]{1,0:T(8,128)(2,1)} %collective-permute-done.12.refs_4_), channel_id=1, source_target_pairs={{8,16},{16,8},{12,20},{20,12},{9,17},{17,9},{13,21},{21,13},{10,18... | collective-permute-start | bytes 1474568 | tf_op jit(solution)/shard_map/ppermute | solution.py:322
  34.9 11.7 %collective-permute-start.3 = (bf16[256,768]{1,0:T(8,128)(2,1)}, bf16[256,768]{1,0:T(8,128)(2,1)}, u32[]{:S(2)}, u32[]{:S(2)}) collective-permute-start(bf16[256,768]{1,0:T(8,128)(2,1)} %copy-done.12), channel_id=1, source_target_pairs={{0,8},{4,12},{8,0},{12,4},{16,24},{20,28},{24,16},{28,20},{1,9},{5... | collective-permute-start | bytes 1179656 | tf_op jit(solution)/shard_map/ppermute | solution.py:322
  35.0 13.6 %collective-permute-start.5 = (bf16[256,768]{1,0:T(8,128)(2,1)}, bf16[256,768]{1,0:T(8,128)(2,1)}, u32[]{:S(2)}, u32[]{:S(2)}) collective-permute-start(bf16[256,768]{1,0:T(8,128)(2,1)} %copy-done.12), channel_id=1, source_target_pairs={{8,16},{16,8},{12,20},{20,12},{9,17},{17,9},{13,21},{21,13},{10,18... | collective-permute-start | bytes 1179656 | tf_op jit(solution)/shard_map/ppermute | solution.py:322
  36.4 18.7 %collective-permute-start.16 = (bf16[320,768]{1,0:T(8,128)(2,1)}, bf16[320,768]{1,0:T(8,128)(2,1)}, u32[]{:S(2)}, u32[]{:S(2)}) collective-permute-start(bf16[320,768]{1,0:T(8,128)(2,1)} %collective-permute-done.15), channel_id=1, source_target_pairs={{8,0},{12,4},{16,24},{20,28},{9,1},{13,5},{17,25},{21,29},{10,2},{... | collective-permute-start | bytes 1474568 | tf_op jit(solution)/shard_map/ppermute | solution.py:322
  46.6 9.8 %collective-permute-start.8 = (bf16[256,768]{1,0:T(8,128)(2,1)}, bf16[256,768]{1,0:T(8,128)(2,1)}, u32[]{:S(2)}, u32[]{:S(2)}) collective-permute-start(bf16[256,768]{1,0:T(8,128)(2,1)} %collective-permute-done.3.refs_4_), channel_id=1, source_target_pairs={{8,16},{16,8},{12,20},{20,12},{9,17},{17,9},{13,21},{21,13},{10,18... | collective-permute-start | bytes 1179656 | tf_op jit(solution)/shard_map/ppermute | solution.py:322
  48.1 29.9 %collective-permute-start.18 = (bf16[2048,256]{1,0:T(8,128)(2,1)S(1)}, bf16[2048,256]{1,0:T(8,128)(2,1)}, u32[]{:S(2)}, u32[]{:S(2)}) collective-permute-start(bf16[2048,256]{1,0:T(8,128)(2,1)S(1)} %pack_panel.1.refs_10_), channel_id=1, source_target_pairs={{0,1},{1,0},{2,3},{3,2},{4,5},{5,4},{6,7},{7,6},{8,9},{9,8},{10,11... | collective-permute-start | bytes 3145736 | tf_op jit(solution)/shard_map/ppermute | solution.py:352
  48.1 51.0 %collective-permute-start.20 = (bf16[2048,256]{1,0:T(8,128)(2,1)}, bf16[2048,256]{1,0:T(8,128)(2,1)}, u32[]{:S(2)}, u32[]{:S(2)}) collective-permute-start(bf16[2048,256]{1,0:T(8,128)(2,1)} %collective-permute-done.19.refs_12_), channel_id=1, source_target_pairs={{0,1},{1,0},{2,3},{3,2},{4,5},{5,4},{6,7},{7,6},{8,9},{9,8},{10,11... | collective-permute-start | bytes 3145736 | tf_op jit(solution)/shard_map/ppermute | solution.py:353
  48.6 13.5 %collective-permute-start.11 = (bf16[320,768]{1,0:T(8,128)(2,1)}, bf16[320,768]{1,0:T(8,128)(2,1)}, u32[]{:S(2)}, u32[]{:S(2)}) collective-permute-start(bf16[320,768]{1,0:T(8,128)(2,1)} %copy-done.14), channel_id=1, source_target_pairs={{0,4},{4,0},{8,12},{12,8},{16,20},{20,16},{24,28},{28,24},{1,5},{5... | collective-permute-start | bytes 1474568 | tf_op jit(solution)/shard_map/ppermute | solution.py:322
  55.2 14.3 %collective-permute-start.6 = (bf16[256,768]{1,0:T(8,128)(2,1)}, bf16[256,768]{1,0:T(8,128)(2,1)}, u32[]{:S(2)}, u32[]{:S(2)}) collective-permute-start(bf16[256,768]{1,0:T(8,128)(2,1)} %collective-permute-done.5), channel_id=1, source_target_pairs={{8,0},{12,4},{16,24},{20,28},{9,1},{13,5},{17,25},{21,29},{10,2},{... | collective-permute-start | bytes 1179656 | tf_op jit(solution)/shard_map/ppermute | solution.py:322
  56.5 17.2 %collective-permute-start.9 = (bf16[256,768]{1,0:T(8,128)(2,1)}, bf16[256,768]{1,0:T(8,128)(2,1)}, u32[]{:S(2)}, u32[]{:S(2)}) collective-permute-start(bf16[256,768]{1,0:T(8,128)(2,1)} %collective-permute-done.8), channel_id=1, source_target_pairs={{8,0},{12,4},{16,24},{20,28},{9,1},{13,5},{17,25},{21,29},{10,2},{... | collective-permute-start | bytes 1179656 | tf_op jit(solution)/shard_map/ppermute | solution.py:322
  59.8 17.5 %copy-start.3 = (f32[4,256,384]{2,1,0:T(8,128)}, f32[4,256,384]{2,1,0:T(8,128)S(1)}, u32[]{:S(2)}) copy-start(f32[4,256,384]{2,1,0:T(8,128)S(1)} %target_sketch.1.refs_14_) | copy-start | bytes 4718596
  59.9 17.4 %copy-start.13 = (bf16[256,768]{1,0:T(8,128)(2,1)S(1)}, bf16[256,768]{1,0:T(8,128)(2,1)}, u32[]{:S(2)}) copy-start(bf16[256,768]{1,0:T(8,128)(2,1)} %copy-done.12) | copy-start | bytes 1179652
  59.9 39.1 %copy-start.15 = (bf16[320,768]{1,0:T(8,128)(2,1)S(1)}, bf16[320,768]{1,0:T(8,128)(2,1)}, u32[]{:S(2)}) copy-start(bf16[320,768]{1,0:T(8,128)(2,1)} %copy-done.14) | copy-start | bytes 1474564
  62.1 15.2 %collective-permute-start.13 = (bf16[320,768]{1,0:T(8,128)(2,1)}, bf16[320,768]{1,0:T(8,128)(2,1)S(1)}, u32[]{:S(2)}, u32[]{:S(2)}) collective-permute-start(bf16[320,768]{1,0:T(8,128)(2,1)} %collective-permute-done.12.refs_4_), channel_id=1, source_target_pairs={{0,4},{4,0},{8,12},{12,8},{16,20},{20,16},{24,28},{28,24},{1,5},{5... | collective-permute-start | bytes 1474568 | tf_op jit(solution)/shard_map/ppermute | solution.py:322
  69.4 17.6 %collective-permute-start.14 = (bf16[320,768]{1,0:T(8,128)(2,1)S(1)}, bf16[320,768]{1,0:T(8,128)(2,1)S(1)}, u32[]{:S(2)}, u32[]{:S(2)}) collective-permute-start(bf16[320,768]{1,0:T(8,128)(2,1)S(1)} %broadcast_select_fusion.1.refs_6_), channel_id=1, source_target_pairs={{0,4},{4,0},{8,12},{12,8},{16,20},{20,16},{24,28},{28,24},{1,5},{5... | collective-permute-start | bytes 1474568 | tf_op jit(solution)/shard_map/ppermute | solution.py:322
  73.7 23.9 %collective-permute-start.17 = (bf16[320,768]{1,0:T(8,128)(2,1)S(1)}, bf16[320,768]{1,0:T(8,128)(2,1)S(1)}, u32[]{:S(2)}, u32[]{:S(2)}) collective-permute-start(bf16[320,768]{1,0:T(8,128)(2,1)S(1)} %broadcast_select_fusion.refs_8_), channel_id=1, source_target_pairs={{0,4},{4,0},{8,12},{12,8},{16,20},{20,16},{24,28},{28,24},{1,5},{5... | collective-permute-start | bytes 1474568 | tf_op jit(solution)/shard_map/ppermute | solution.py:322
  77.3 77.9 %collective-permute-start.2 = (bf16[256,768]{1,0:T(8,128)(2,1)S(1)}, bf16[256,768]{1,0:T(8,128)(2,1)S(1)}, u32[]{:S(2)}, u32[]{:S(2)}) collective-permute-start(bf16[256,768]{1,0:T(8,128)(2,1)S(1)} %copy-done.13), channel_id=1, source_target_pairs={{0,4},{4,0},{8,12},{12,8},{16,20},{20,16},{24,28},{28,24},{1,5},{5... | collective-permute-start | bytes 1179656 | tf_op jit(solution)/shard_map/ppermute | solution.py:322
  78.0 77.2 %collective-permute-start.4 = (bf16[256,768]{1,0:T(8,128)(2,1)}, bf16[256,768]{1,0:T(8,128)(2,1)S(1)}, u32[]{:S(2)}, u32[]{:S(2)}) collective-permute-start(bf16[256,768]{1,0:T(8,128)(2,1)} %collective-permute-done.3.refs_4_), channel_id=1, source_target_pairs={{0,4},{4,0},{8,12},{12,8},{16,20},{20,16},{24,28},{28,24},{1,5},{5... | collective-permute-start | bytes 1179656 | tf_op jit(solution)/shard_map/ppermute | solution.py:322
  87.0 68.2 %collective-permute-start.7 = (bf16[256,768]{1,0:T(8,128)(2,1)S(1)}, bf16[256,768]{1,0:T(8,128)(2,1)S(1)}, u32[]{:S(2)}, u32[]{:S(2)}) collective-permute-start(bf16[256,768]{1,0:T(8,128)(2,1)S(1)} %broadcast_select_fusion.3.refs_6_), channel_id=1, source_target_pairs={{0,4},{4,0},{8,12},{12,8},{16,20},{20,16},{24,28},{28,24},{1,5},{5... | collective-permute-start | bytes 1179656 | tf_op jit(solution)/shard_map/ppermute | solution.py:322
  97.5 57.7 %collective-permute-start.10 = (bf16[256,768]{1,0:T(8,128)(2,1)S(1)}, bf16[256,768]{1,0:T(8,128)(2,1)S(1)}, u32[]{:S(2)}, u32[]{:S(2)}) collective-permute-start(bf16[256,768]{1,0:T(8,128)(2,1)S(1)} %broadcast_select_fusion.2.refs_8_), channel_id=1, source_target_pairs={{0,4},{4,0},{8,12},{12,8},{16,20},{20,16},{24,28},{28,24},{1,5},{5... | collective-permute-start | bytes 1179656 | tf_op jit(solution)/shard_map/ppermute | solution.py:322
  114.7 1.4 copy-start.4
  141.0 13.0 %copy-start = (bf16[4,256,384]{2,1,0:T(8,128)(2,1)}, bf16[4,256,384]{2,1,0:T(8,128)(2,1)S(1)}, u32[]{:S(2)}) copy-start(bf16[4,256,384]{2,1,0:T(8,128)(2,1)S(1)} %basis.1.refs_1_.refs_10_) | copy-start | bytes 2359300
  141.0 14.2 %copy-start.11 = (bf16[4,1,256,256]{3,2,1,0:T(8,128)(2,1)S(1)}, bf16[4,1,256,256]{3,2,1,0:T(8,128)(2,1)}, u32[]{:S(2)}) copy-start(bf16[4,1,256,256]{3,2,1,0:T(8,128)(2,1)} %refs_14_.1) | copy-start | bytes 1572868
  154.0 1.2 copy-start.2

commit v3 on v1

--- a/solution.py
+++ b/solution.py
@@ -12,7 +12,9 @@
 NN = (((1,), (0,)), ((), ()))
 NT = (((1,), (1,)), ((), ()))
 TN = (((0,), (0,)), ((), ()))
-VMEM_BYTES = 50 * 1024 * 1024
+PLACE_P = 10
+PLACE_Q = 8
+VMEM_BYTES = 20 * 1024 * 1024
 
 
 def dot(left, right, dims=NN, precision=None):
@@ -100,15 +102,14 @@
     return copies
 
 
-def sampled_kernel(n_rows, n_cols, row_owner_ref, col_owner_ref, *refs):
-    blocks, panels = refs[:n_rows], refs[n_rows : n_rows + n_cols]
-    target_ref, mid_ref, sampled_ref, panel_ref, pb_all, weight, sem, sem_panel = refs[n_rows + n_cols :]
+def sampled_kernel(n_rows, n_cols, col_owner_ref, pb_all, *refs):
+    panels = refs[:n_cols]
+    target_ref, mid_ref, sampled_ref, panel_ref, weight, sem_panel = refs[n_cols:]
     count, size, wide = target_ref.shape
     half = pb_all.shape[1] - size
     width = 2 * half
     columns = wide // half
-    copies = fetch_all(blocks, pb_all, row_owner_ref, sem)
-    copies += fetch_all(panels, panel_ref, col_owner_ref, sem_panel)
+    copies = fetch_all(panels, panel_ref, col_owner_ref, sem_panel)
     for copy in copies:
         copy.wait()
     tall = count * width
@@ -152,53 +153,62 @@
 
 def basis_kernel(sampled_ref, basis_ref, state):
     count, size, wide = sampled_ref.shape
-    _, half, width = state.shape
-    columns = wide // half
-    pairs = columns // 2
+    half, held, width = state.shape
+    pairs = wide // width
     root_size = math.sqrt(size)
     highest = lax.Precision.HIGHEST
     first = halves((half, width), half)
-    lane = lax.broadcasted_iota(jnp.int32, (half, width), 1)
-    row = lax.broadcasted_iota(jnp.int32, (half, width), 0)
-    n_even = count * pairs
     for i in range(count):
         for p in range(pairs):
             z_pair = sampled_ref[i, :, pl.ds(p * width, width)]
-            gram = swap(dot(z_pair, z_pair, TN, highest), half)
-            g = i * pairs + p
-            state[g] = jnp.where(first, (lane == row).astype(F32), gram[:half])
-            state[n_even + g] = jnp.where(first, gram[half:], (lane == row + half).astype(F32))
+            gram = dot(z_pair, z_pair, TN, highest)
+            state[:, i * pairs + p, :] = jnp.where(first, gram[:half], gram[half:])
     sub = 8
-    for block in range(half // sub):
-
-        def eliminate(q, carry, block=block):
-            pivot = block * sub + q
-            below = lax.broadcasted_iota(jnp.int32, (sub, width), 0) > q
-            for g in range(2 * n_even):
-                offset = half if g < n_even else 0
-                index = jnp.full((sub, width), pivot + offset, jnp.int32)
-                line = jnp.broadcast_to(state[g, pl.ds(pivot, 1), :], (sub, width))
-                top = jnp.take_along_axis(line, index, axis=1)
-                line = line / top
-                for v in range(block, half // sub):
-                    rows = pl.ds(v * sub, sub)
-                    tile = state[g, rows, :]
-                    column = jnp.take_along_axis(tile, index, axis=1)
-                    if v == block:
-                        column = jnp.where(below, column, 0.0)
-                    state[g, rows, :] = tile - column * line
-            return carry
-
-        lax.fori_loop(0, sub, eliminate, 0)
+    lane = lax.broadcasted_iota(jnp.int32, (held, width), 1)
+    column = lane % half
+    origin = lane - column
+
+    def pick(row, pivot):
+        return jnp.take_along_axis(row, origin + pivot, axis=1)
+
+    def one_block(block, carry):
+        start = block * sub
+        rows = [state[start + r] for r in range(sub)]
+        core = {(r, s): pick(rows[r], start + s) for r in range(sub) for s in range(r, sub)}
+        lines, finals = [], []
+        for q in range(sub):
+            pivot = start + q
+            root = lax.rsqrt(core[q, q])
+            inverse = root * root
+            finals.append(rows[q])
+            unit = jnp.where(column == pivot, 1.0, rows[q])
+            state[pivot] = jnp.where(column <= pivot, unit * (root_size * root), 0.0)
+            line = unit * inverse
+            lines.append(jnp.where(jnp.logical_and(column > pivot, column < start + sub), 0.0, line))
+            for r in range(q + 1, sub):
+                scaled = core[q, r] * inverse
+                rows[r] = jnp.where(column == pivot, 0.0, rows[r]) - core[q, r] * line
+                for s in range(r, sub):
+                    core[r, s] = core[r, s] - scaled * core[q, s]
+        inside = jnp.logical_and(column >= start, column < start + sub)
+
+        def update(v, inner):
+            for r in range(sub):
+                row = v * sub + r
+                value = jnp.where(inside, 0.0, state[row])
+                for q in range(sub):
+                    value = value - pick(finals[q], row) * lines[q]
+                state[row] = value
+            return inner
+
+        lax.fori_loop(block + 1, half // sub, update, 0)
+        return carry
+
+    lax.fori_loop(0, half // sub, one_block, 0)
     for i in range(count):
         for p in range(pairs):
-            g = i * pairs + p
-            even, odd = state[g], state[n_even + g]
-            even_diag = jnp.sum(jnp.where(lane == row + half, even, 0.0), axis=1, keepdims=True)
-            odd_diag = jnp.sum(jnp.where(lane == row, odd, 0.0), axis=1, keepdims=True)
-            even = jnp.where(first, even * (root_size * lax.rsqrt(even_diag)), 0.0)
-            odd = jnp.where(first, 0.0, odd * (root_size * lax.rsqrt(odd_diag)))
-            inverse = jnp.concatenate([even, odd], axis=0)
+            inverse = state[:, i * pairs + p, :]
+            inverse = jnp.concatenate([jnp.where(first, inverse, 0.0), jnp.where(first, 0.0, inverse)], axis=0)
             z_pair = sampled_ref[i, :, pl.ds(p * width, width)]
             basis_ref[i, :, pl.ds(p * width, width)] = dot(z_pair, inverse, NT, highest).astype(BF16)
 
@@ -250,15 +260,12 @@
     lax.fori_loop(0, n_rows, one_owner, 0)
 
 
-def output_kernel(n_rows, near_ref, row_owner_ref, *refs):
-    blocks = refs[:n_rows]
-    basis_ref, left_ref, value_ref, near_left_ref, near_block_ref, near_out_ref, far_out_ref, q_all, sem = refs[n_rows:]
+def output_kernel(n_rows, near_ref, q_all, *refs):
+    basis_ref, left_ref, value_ref, near_left_ref, near_block_ref, near_out_ref, far_out_ref = refs
     count, columns, size, width = far_out_ref.shape
     half = width // 2
     root_size = math.sqrt(size)
     first = halves((size, width), half)
-    for copy in fetch_all(blocks, q_all, row_owner_ref, sem):
-        copy.wait()
     for j in range(columns):
         right = jnp.concatenate([q_all[o, :, pl.ds(j * width, width)] for o in range(n_rows)], axis=1)
         weights = (value_ref[j] - dot(right, left_ref[j], NT)) / root_size
@@ -281,12 +288,34 @@
         near_out_ref[i, 0] = (near_block_ref[i, 0].astype(F32) - update).astype(BF16)
 
 
-def gather_rows(block, after=None):
+def place(buffer, owners, blocks, count, micros):
+    n = len(blocks)
+
+    def kernel(*refs):
+        sources, target, sem = refs[:n], refs[-2], refs[-1]
+        copies = fetch_all(sources, target, owners(lax.axis_index("rows")), sem)
+        for copy in copies:
+            copy.wait()
+
+    held = [] if buffer is None else [buffer]
+    return pl.pallas_call(
+        kernel,
+        out_shape=jax.ShapeDtypeStruct((count,) + blocks[0].shape, blocks[0].dtype),
+        in_specs=[IN_VMEM] * (n + len(held)),
+        out_specs=IN_VMEM,
+        scratch_shapes=[pltpu.SemaphoreType.DMA((n,))],
+        input_output_aliases={n: 0} if held else {},
+        compiler_params=pltpu.CompilerParams(vmem_limit_bytes=1024 * 1024),
+        cost_estimate=pl.CostEstimate(flops=int(micros * 1.15e9), bytes_accessed=0, transcendentals=0),
+    )(*blocks, *held)
+
+
+def gather_rows(block, micros, after=None):
     n = lax.axis_size("rows")
     me = lax.axis_index("rows")
     if n != 8:
-        whole = lax.all_gather(block, "rows")
-        return [whole[o] for o in range(n)], jnp.arange(n, dtype=jnp.int32)
+        gathered = lax.all_gather(block, "rows")
+        return gathered, (block, block), [gathered] * 4
     inner = [(2, 4), (4, 2), (3, 5), (5, 3)]
     outward = [(2, 0), (3, 1), (4, 6), (5, 7)]
     exchange = [(i, i ^ 2) for i in range(n)]
@@ -294,22 +323,26 @@
     send = lambda value, pairs: lax.ppermute(value, "rows", pairs)
     plane = me // 2
     is_end = jnp.logical_or(plane == 0, plane == 3)
+    pair = lambda owner: (owner, owner + 1 - 2 * (owner % 2))
+    zy = lambda plane, d: pair(plane * 2 + d % 2)
     a = send(block, exchange)
     b = send(block, inner)
+    if after is not None:
+        block, _ = lax.optimization_barrier((block, after))
     x_own = send(block, across)
+    stages = [place(None, pair, [block, x_own], n, micros)]
     c = send(b, outward)
     d = send(a, inner)
     x_a = send(a, across)
+    stages.append(place(stages[-1], lambda d: zy(d // 2 + 1 - 2 * (d // 2 % 2), d), [a, x_a], n, micros))
     second = jnp.where(is_end, c, b)
     e = send(d, outward)
     x_second = send(second, across)
+    stages.append(place(stages[-1], lambda d: zy(jnp.where(d < 4, 2, 1), d), [second, x_second], n, micros))
     third = jnp.where(is_end, e, d)
     x_third = send(third, across)
-    low = plane < 2
-    near_plane = jnp.where(low, 2, 1) * 2 + me % 2
-    far_plane = jnp.where(low, 3, 0) * 2 + me % 2
-    owners = jnp.stack([me, me ^ 1, me ^ 2, me ^ 3, near_plane, near_plane ^ 1, far_plane, far_plane ^ 1])
-    return [block, x_own, a, x_a, second, x_second, third, x_third], owners.astype(jnp.int32)
+    stages.append(place(stages[-1], lambda d: zy(jnp.where(d < 4, 3, 0), d), [third, x_third], n, micros))
+    return stages[-1], (second, third), stages
 
 
 def gather_cols(block):
@@ -355,6 +388,9 @@
             flops=2 * count * pivots * half * size * size,
             moved=4 * panel_cols.size,
         )(panel_cols, pivot_inv)
+    pb_all, (_, pb_third), _ = gather_rows(pb, PLACE_P)
+    panels, col_owners = gather_cols(panel)
+    q, target_late, _ = lax.optimization_barrier((q, target_factors, pb_third))
     with jax.named_scope("target_sketch"):
         target_sketch = call(
             target_sketch_kernel,
@@ -362,12 +398,8 @@
             [IN_VMEM] * 2,
             flops=4 * target_factors.size * half,
             moved=2 * target_factors.size * 2,
-        )(target_factors, sketch_t)
-
-    pb_all, row_owners = gather_rows(pb)
-    panels, col_owners = gather_cols(panel)
-    q, _ = lax.optimization_barrier((q, pb_all[4]))
-    q_all, _ = gather_rows(q)
+        )(target_late, sketch_t)
+    q_all, _, q_stages = gather_rows(q, PLACE_Q, pb_all)
 
     vmem = pltpu.VMEM
     with jax.named_scope("sampled"):
@@ -378,26 +410,26 @@
                 shape((count, size, wide), F32),
                 shape((n_cols,) + panel.shape, BF16),
             ),
-            [IN_SMEM] * 2 + [ANYWHERE] * (n_rows + n_cols) + [IN_VMEM],
+            [IN_SMEM, IN_VMEM] + [ANYWHERE] * n_cols + [IN_VMEM],
             [
-                vmem((n_rows,) + pb.shape, BF16),
                 vmem((count, n_rows * width, wide), BF16),
-                pltpu.SemaphoreType.DMA((n_rows,)),
                 pltpu.SemaphoreType.DMA((n_cols,)),
             ],
             flops=8 * n_rows * count * width * size * columns * width // 2,
             moved=2 * n_rows * (pb.size + count * width * columns * width),
-        )(row_owners, col_owners, *pb_all, *panels, target_sketch)
+        )(col_owners, pb_all, *panels, target_sketch)
+    sampled, _ = lax.optimization_barrier((sampled, q_stages[1]))
     with jax.named_scope("basis"):
         basis = call(
             basis_kernel,
             shape((count, size, wide), BF16),
             [IN_VMEM],
-            [vmem((count * columns, half, width), F32)],
+            [vmem((half, -(-count * columns // 2 // 8) * 8, width), F32)],
             flops=8 * count * columns * half * half * size,
             moved=6 * count * size * wide,
         )(sampled)
     deep = n_rows * width
+    basis, _ = lax.optimization_barrier((basis, q_stages[2]))
     with jax.named_scope("cores"):
         left, value, near_left = call(
             lambda *refs: cores_kernel(n_rows, *refs),
@@ -415,11 +447,10 @@
         near_new, far_new = call(
             lambda *refs: output_kernel(n_rows, *refs),
             (shape(near_blocks.shape, BF16), shape(target_factors.shape, BF16)),
-            [IN_SMEM] * 2 + [ANYWHERE] * n_rows + [IN_VMEM] * 5,
-            [vmem((n_rows,) + q.shape, BF16), pltpu.SemaphoreType.DMA((n_rows,))],
+            [IN_SMEM] + [IN_VMEM] * 6,
             flops=2 * columns * size * deep * count * half,
             moved=2 * n_rows * q.size,
-        )(near_cols, row_owners, *q_all, basis, left, value, near_left, near_blocks)
+        )(near_cols, q_all, basis, left, value, near_left, near_blocks)
     return near_new, far_new
 
 

time: 265 us -> 106 us (0.40)
  Pallas kernels: 164 us -> 39.8 us
  waiting for transfers between devices: 56 us -> 36.2 us
  starting transfers between devices: 29.5 us -> 22.8 us
  other arithmetic: 4.78 us -> 0.27 us
  local copies, waits for them, and re-layouts: 7.87 us -> 5.03 us
    pallas_call x1 -> x9, Pallas kernels: 126 us -> 18.2 us  [the longest x1 11.7 us: per_device(): call(basis_kernel, shape((count, size, wide), BF16), [IN_VMEM], [vmem((ha...]
    ppermute x18, waiting for transfers between devices: 56 us -> 36.2 us  [gather_rows(): send = lambda value, pairs: lax.ppermute(value, 'rows', pairs)]
    pallas_call x1, Pallas kernels: 15.6 us -> 7.75 us  [per_device(): call(lambda *refs: sampled_kernel(n_rows, n_cols, *refs), (shape((n_rows,...]
    ppermute x18, starting transfers between devices: 27.4 us -> 21.1 us  [gather_rows(): send = lambda value, pairs: lax.ppermute(value, 'rows', pairs)]
    pallas_call x1, Pallas kernels: 13 us -> 6.95 us  [per_device(): call(lambda *refs: cores_kernel(n_rows, *refs), (shape((columns, count *...]
    pallas_call x1, Pallas kernels: 7.34 us -> 3.33 us  [per_device(): call(lambda *refs: output_kernel(n_rows, *refs), (shape(near_blocks.shape...]
    unnamed x35 -> x17, local copies, waits for them, and re-layouts: 7.78 us -> 5.03 us
  transfers between devices with their start and end apart: 21 -> 21, of which waited for: 9 -> 8; matrix products, arithmetic and copies ran while one was open for 2% -> 0% of each run, Pallas kernels for 59% -> 33%
where the time goes in v3:
time: 106 us; the launch traced here: 105 us
  Pallas kernels  39.8 us (38%)
  waiting for transfers between devices  36.2 us (34%)
  starting transfers between devices  22.8 us (22%)
  local copies, waits for them, and re-layouts  5.03 us (5%)
    ppermute x18, waiting for transfers between devices, gather_rows(): send = lambda value, pairs: lax.ppermute(value, 'rows', pairs)  36.2 us
    ppermute x18, starting transfers between devices, gather_rows(): send = lambda value, pairs: lax.ppermute(value, 'rows', pairs)  21.1 us
    pallas_call x1, Pallas kernels, per_device(): call(basis_kernel, shape((count, size, wide), BF16), [IN_VMEM], [vmem((ha...  11.7 us
    pallas_call x1, Pallas kernels, per_device(): call(lambda *refs: sampled_kernel(n_rows, n_cols, *refs), (shape((n_rows,...  7.75 us
    pallas_call x1, Pallas kernels, per_device(): call(lambda *refs: cores_kernel(n_rows, *refs), (shape((columns, count *...  6.95 us
    pallas_call x8, Pallas kernels, place(): pl.pallas_call(kernel, out_shape=jax.ShapeDtypeStruct((count,) + blocks[0...  6.46 us
    unnamed x17, local copies, waits for them, and re-layouts  5.03 us
    pallas_call x1, Pallas kernels, per_device(): call(lambda *refs: output_kernel(n_rows, *refs), (shape(near_blocks.shape...  3.33 us
  transfers between devices with their start and end apart: 21, of which 8 were waited for; matrix products, arithmetic and copies ran while one was open for 0% of the time, Pallas kernels for 33%

profile of v3, /device:TPU:0, one launch (start us, length us, event | category | flops | bytes accessed | tf_op | source)
XLA Modules:
  0.0 105.0 jit_solution(14748559202295903055)
XLA Ops:
  0.6 1.1 %copy-done.2 = bf16[2,6,256,128]{3,2,1,0:T(8,128)(2,1)S(1)} copy-done((bf16[2,6,256,128]{3,2,1,0:T(8,128)(2,1)S(1)}, bf16[2,6,256,128]{3,2,1,0:T(8,128)(2,1)}, u32[]{:S(2)}) %copy-start.2) | copy-done | bytes 786456
  1.8 0.9 copy-done.3
  2.7 1.1 %pack_rows.1 = (bf16[320,768]{1,0:T(8,128)(2,1)}, bf16[256,768]{1,0:T(8,128)(2,1)S(1)}) custom-call(bf16[2,6,256,128]{3,2,1,0:T(8,128)(2,1)S(1)} %copy-done.2, bf16[6,64,256]{2,1,0:T(8,128)(2,1)S(1)} %bitcast.5), custom_call_target="tpu_custom_call" | custom-call | flops 25165824 | bytes 1572864 | tf_op jit(solution)/shard_map/pack_rows/pallas_call | solution.py:375
  3.8 3.0 %collective-permute-start = (bf16[320,768]{1,0:T(8,128)(2,1)}, bf16[320,768]{1,0:T(8,128)(2,1)}, u32[]{:S(2)}, u32[]{:S(2)}) collective-permute-start(bf16[320,768]{1,0:T(8,128)(2,1)} %get-tuple-element.16.refs_0_), channel_id=1, source_target_pairs={{0,8},{4,12},{8,0},{12,4},{16,24},{20,28},{24,16},{28,20},{1,9},{5... | collective-permute-start | bytes 1474568 | tf_op jit(solution)/shard_map/ppermute | solution.py:323
  6.8 1.5 %collective-permute-start.12 = (bf16[320,768]{1,0:T(8,128)(2,1)}, bf16[320,768]{1,0:T(8,128)(2,1)}, u32[]{:S(2)}, u32[]{:S(2)}) collective-permute-start(bf16[320,768]{1,0:T(8,128)(2,1)} %get-tuple-element.16.refs_0_), channel_id=1, source_target_pairs={{8,16},{16,8},{12,20},{20,12},{9,17},{17,9},{13,21},{21,13},{10,18... | collective-permute-start | bytes 1474568 | tf_op jit(solution)/shard_map/ppermute | solution.py:323
  8.3 1.5 %collective-permute-start.16 = (bf16[320,768]{1,0:T(8,128)(2,1)}, bf16[320,768]{1,0:T(8,128)(2,1)}, u32[]{:S(2)}, u32[]{:S(2)}) collective-permute-start(bf16[320,768]{1,0:T(8,128)(2,1)} %get-tuple-element.16.refs_0_), channel_id=1, source_target_pairs={{0,4},{4,0},{8,12},{12,8},{16,20},{20,16},{24,28},{28,24},{1,5},{5... | collective-permute-start | bytes 1474568 | tf_op jit(solution)/shard_map/ppermute | solution.py:323
  9.8 1.2 %copy-done.1 = bf16[4,4,256,128]{3,2,1,0:T(8,128)(2,1)S(1)} copy-done((bf16[4,4,256,128]{3,2,1,0:T(8,128)(2,1)S(1)}, bf16[4,4,256,128]{3,2,1,0:T(8,128)(2,1)}, u32[]{:S(2)}) %copy-start.1) | copy-done | bytes 1048600
  11.0 1.0 copy-done.5
  12.1 0.5 pack_panel.1.refs_2_
  12.6 1.6 %collective-permute-start.19 = (bf16[2048,256]{1,0:T(8,128)(2,1)S(1)}, bf16[2048,256]{1,0:T(8,128)(2,1)S(1)}, u32[]{:S(2)}, u32[]{:S(2)}) collective-permute-start(bf16[2048,256]{1,0:T(8,128)(2,1)S(1)} %pack_panel.1.refs_2_), channel_id=1, source_target_pairs={{0,2},{1,3},{2,0},{3,1},{4,6},{5,7},{6,4},{7,5},{8,10},{9,11},{10,... | collective-permute-start | bytes 3145736 | tf_op jit(solution)/shard_map/ppermute | solution.py:356
  14.2 0.1 copy.16.refs_0_
  14.3 0.1 pad_add_fusion.refs_0_
  14.4 4.0 %collective-permute-done.refs_0_ = bf16[320,768]{1,0:T(8,128)(2,1)} collective-permute-done((bf16[320,768]{1,0:T(8,128)(2,1)}, bf16[320,768]{1,0:T(8,128)(2,1)}, u32[]{:S(2)}, u32[]{:S(2)}) %collective-permute-start) | collective-permute-done | bytes 491552 | tf_op jit(solution)/shard_map/ppermute | solution.py:323
  18.4 0.7 collective-permute-start.1
  19.1 1.7 %collective-permute-start.15 = (bf16[320,768]{1,0:T(8,128)(2,1)}, bf16[320,768]{1,0:T(8,128)(2,1)S(1)}, u32[]{:S(2)}, u32[]{:S(2)}) collective-permute-start(bf16[320,768]{1,0:T(8,128)(2,1)} %collective-permute-done.refs_0_), channel_id=1, source_target_pairs={{0,4},{4,0},{8,12},{12,8},{16,20},{20,16},{24,28},{28,24},{1,5},{5... | collective-permute-start | bytes 1474568 | tf_op jit(solution)/shard_map/ppermute | solution.py:323
  20.8 0.5 collective-permute-done.16.refs_1_
  21.3 1.3 %collective-permute-start.13 = (bf16[320,768]{1,0:T(8,128)(2,1)}, bf16[320,768]{1,0:T(8,128)(2,1)S(1)}, u32[]{:S(2)}, u32[]{:S(2)}) collective-permute-start(bf16[320,768]{1,0:T(8,128)(2,1)} %collective-permute-done.12), channel_id=1, source_target_pairs={{8,0},{12,4},{16,24},{20,28},{9,1},{13,5},{17,25},{21,29},{10,2},{... | collective-permute-start | bytes 1474568 | tf_op jit(solution)/shard_map/ppermute | solution.py:323
  22.6 1.8 %shard_map.86.refs_2_ = bf16[8,320,768]{2,1,0:T(8,128)(2,1)S(1)} custom-call(bf16[320,768]{1,0:T(8,128)(2,1)} %get-tuple-element.16.refs_0_, bf16[320,768]{1,0:T(8,128)(2,1)} %collective-permute-done.16.refs_1_), custom_call_target="tpu_custom_call" | custom-call | flops 11500000256 | tf_op jit(solution)/shard_map/pallas_call | solution.py:301
  24.4 12.0 %collective-permute-done.13 = bf16[320,768]{1,0:T(8,128)(2,1)S(1)} collective-permute-done((bf16[320,768]{1,0:T(8,128)(2,1)}, bf16[320,768]{1,0:T(8,128)(2,1)S(1)}, u32[]{:S(2)}, u32[]{:S(2)}) %collective-permute-start.13) | collective-permute-done | bytes 491552 | tf_op jit(solution)/shard_map/ppermute | solution.py:323
  36.5 1.0 collective-permute-start.14
  37.5 1.3 %collective-permute-start.2 = (bf16[320,768]{1,0:T(8,128)(2,1)S(1)}, bf16[320,768]{1,0:T(8,128)(2,1)S(1)}, u32[]{:S(2)}, u32[]{:S(2)}) collective-permute-start(bf16[320,768]{1,0:T(8,128)(2,1)S(1)} %collective-permute-done.1), channel_id=1, source_target_pairs={{8,0},{12,4},{16,24},{20,28},{9,1},{13,5},{17,25},{21,29},{10,2},{... | collective-permute-start | bytes 1474568 | tf_op jit(solution)/shard_map/ppermute | solution.py:323
  38.8 1.7 %shard_map.87.refs_2_ = bf16[8,320,768]{2,1,0:T(8,128)(2,1)S(1)} custom-call(bf16[320,768]{1,0:T(8,128)(2,1)} %collective-permute-done.refs_0_, bf16[320,768]{1,0:T(8,128)(2,1)S(1)} %collective-permute-done.15.refs_1_, bf16[8,320,768]{2,1,0:T(8,128)(2,1)S(1)} %shard_map.86.refs_2_), custom_call_target="tpu_custom_call", output_to_operand_aliasing={{}: (2, {})} | custom-call | flops 11500000256 | tf_op jit(solution)/shard_map/pallas_call | solution.py:301
  40.6 9.4 %collective-permute-done.2 = bf16[320,768]{1,0:T(8,128)(2,1)S(1)} collective-permute-done((bf16[320,768]{1,0:T(8,128)(2,1)S(1)}, bf16[320,768]{1,0:T(8,128)(2,1)S(1)}, u32[]{:S(2)}, u32[]{:S(2)}) %collective-permute-start.2) | collective-permute-done | bytes 491552 | tf_op jit(solution)/shard_map/ppermute | solution.py:323
  50.0 1.3 %collective-permute-start.11 = (bf16[320,768]{1,0:T(8,128)(2,1)S(1)}, bf16[320,768]{1,0:T(8,128)(2,1)S(1)}, u32[]{:S(2)}, u32[]{:S(2)}) collective-permute-start(bf16[320,768]{1,0:T(8,128)(2,1)S(1)} %broadcast_select_fusion.1.refs_0_), channel_id=1, source_target_pairs={{0,4},{4,0},{8,12},{12,8},{16,20},{20,16},{24,28},{28,24},{1,5},{5... | collective-permute-start | bytes 1474568 | tf_op jit(solution)/shard_map/ppermute | solution.py:323
  51.3 0.8 collective-permute-start.7
  52.1 0.7 shard_map.88.refs_2_
  52.8 2.0 %target_sketch.1.refs_6_ = f32[4,256,384]{2,1,0:T(8,128)S(1)} custom-call(bf16[4,6,256,128]{3,2,1,0:T(8,128)(2,1)S(1)} %copy-done, bf16[6,64,256]{2,1,0:T(8,128)(2,1)S(1)} %bitcast.6), custom_call_target="tpu_custom_call" | custom-call | flops 201326592 | bytes 3145728 | tf_op jit(solution)/shard_map/target_sketch/pallas_call | solution.py:395
  54.8 4.3 %collective-permute-done.3.refs_0_ = bf16[256,768]{1,0:T(8,128)(2,1)S(1)} collective-permute-done((bf16[256,768]{1,0:T(8,128)(2,1)S(1)}, bf16[256,768]{1,0:T(8,128)(2,1)S(1)}, u32[]{:S(2)}, u32[]{:S(2)}) %collective-permute-start.3) | collective-permute-done | bytes 393248 | tf_op jit(solution)/shard_map/ppermute | solution.py:323
  59.1 0.8 collective-permute-start.10
  59.9 0.7 collective-permute-start.4
  60.6 1.8 %collective-permute-done.11.refs_1_ = bf16[320,768]{1,0:T(8,128)(2,1)S(1)} collective-permute-done((bf16[320,768]{1,0:T(8,128)(2,1)S(1)}, bf16[320,768]{1,0:T(8,128)(2,1)S(1)}, u32[]{:S(2)}, u32[]{:S(2)}) %collective-permute-start.11) | collective-permute-done | bytes 491552 | tf_op jit(solution)/shard_map/ppermute | solution.py:323
  62.4 1.3 %collective-permute-start.8 = (bf16[256,768]{1,0:T(8,128)(2,1)S(1)}, bf16[256,768]{1,0:T(8,128)(2,1)S(1)}, u32[]{:S(2)}, u32[]{:S(2)}) collective-permute-start(bf16[256,768]{1,0:T(8,128)(2,1)S(1)} %collective-permute-done.7), channel_id=1, source_target_pairs={{8,0},{12,4},{16,24},{20,28},{9,1},{13,5},{17,25},{21,29},{10,2},{... | collective-permute-start | bytes 1179656 | tf_op jit(solution)/shard_map/ppermute | solution.py:323
  63.7 0.7 shard_map.89.refs_1_
  64.3 1.4 %collective-permute-start.17 = (bf16[256,768]{1,0:T(8,128)(2,1)S(1)}, bf16[256,768]{1,0:T(8,128)(2,1)S(1)}, u32[]{:S(2)}, u32[]{:S(2)}) collective-permute-start(bf16[256,768]{1,0:T(8,128)(2,1)S(1)} %get-tuple-element.18.refs_0_), channel_id=1, source_target_pairs={{0,4},{4,0},{8,12},{12,8},{16,20},{20,16},{24,28},{28,24},{1,5},{5... | collective-permute-start | bytes 1179656 | tf_op jit(solution)/shard_map/ppermute | solution.py:323
  65.8 7.8 %sampled.1 = (bf16[8,512,768]{2,1,0:T(8,128)(2,1)S(1)}, f32[4,256,384]{2,1,0:T(8,128)S(1)}, bf16[4,2048,256]{2,1,0:T(8,128)(2,1)S(1)}) custom-call(s32[4]{0:T(128)S(1)} %pad_add_fusion.refs_0_, bf16[8,320,768]{2,1,0:T(8,128)(2,1)S(1)} %shard_map.89.refs_1_, bf16[2048,256]{1,0:T(8,128)(2,1)S(1)} %pack_panel.1.refs_2_, ...), custom_call_target="tpu_custom_call" | custom-call | flops 3221225472 | bytes 10223616 | tf_op jit(solution)/shard_map/sampled/pallas_call | solution.py:406
  73.5 0.5 collective-permute-done.8
  74.0 0.3 collective-permute-start.9
  74.3 1.5 %collective-permute-start.5 = (bf16[256,768]{1,0:T(8,128)(2,1)S(1)}, bf16[256,768]{1,0:T(8,128)(2,1)S(1)}, u32[]{:S(2)}, u32[]{:S(2)}) collective-permute-start(bf16[256,768]{1,0:T(8,128)(2,1)S(1)} %collective-permute-done.4), channel_id=1, source_target_pairs={{8,0},{12,4},{16,24},{20,28},{9,1},{13,5},{17,25},{21,29},{10,2},{... | collective-permute-start | bytes 1179656 | tf_op jit(solution)/shard_map/ppermute | solution.py:323
  75.8 3.7 %collective-permute-done.17.refs_1_ = bf16[256,768]{1,0:T(8,128)(2,1)S(1)} collective-permute-done((bf16[256,768]{1,0:T(8,128)(2,1)S(1)}, bf16[256,768]{1,0:T(8,128)(2,1)S(1)}, u32[]{:S(2)}, u32[]{:S(2)}) %collective-permute-start.17) | collective-permute-done | bytes 393248 | tf_op jit(solution)/shard_map/ppermute | solution.py:323
  79.5 0.4 shard_map.90.refs_2_
  79.9 0.4 shard_map.91.refs_2_
  80.4 11.7 %basis.1.refs_1_.refs_2_ = bf16[4,256,384]{2,1,0:T(8,128)(2,1)S(1)} custom-call(f32[4,256,384]{2,1,0:T(8,128)S(1)} %get-tuple-element.21.sampled_ref), custom_call_target="tpu_custom_call" | custom-call | flops 201326592 | bytes 2359296 | tf_op jit(solution)/shard_map/basis/pallas_call | solution.py:423
  92.2 1.1 %collective-permute-start.6 = (bf16[256,768]{1,0:T(8,128)(2,1)S(1)}, bf16[256,768]{1,0:T(8,128)(2,1)S(1)}, u32[]{:S(2)}, u32[]{:S(2)}) collective-permute-start(bf16[256,768]{1,0:T(8,128)(2,1)S(1)} %broadcast_select_fusion.3.refs_0_), channel_id=1, source_target_pairs={{0,4},{4,0},{8,12},{12,8},{16,20},{20,16},{24,28},{28,24},{1,5},{5... | collective-permute-start | bytes 1179656 | tf_op jit(solution)/shard_map/ppermute | solution.py:323
  93.3 0.4 shard_map.92.refs_2_
  93.7 7.0 %cores.1 = (bf16[6,256,1024]{2,1,0:T(8,128)(2,1)S(1)}, f32[6,256,256]{2,1,0:T(8,128)S(1)}, bf16[4,256,1024]{2,1,0:T(8,128)(2,1)S(1)}) custom-call(s32[4,1]{1,0:T(4,128)S(1)} %copy.16.refs_0_, bf16[4,256,384]{2,1,0:T(8,128)(2,1)S(1)} %basis.1.refs_1_.refs_2_, bf16[8,512,768]{2,1,0:T(8,128)(2,1)S(1)} %get-tuple-element.23.refs_2_, ...), custom_call_target="tpu_custom_call" | custom-call | flops 2415919104 | bytes 10223616 | tf_op jit(solution)/shard_map/cores/pallas_call | solution.py:434
  100.7 0.4 shard_map.93.refs_1_
  101.1 0.6 copy-done.6
  101.7 3.3 %output.1 = (bf16[4,1,256,256]{3,2,1,0:T(8,128)(2,1)}, bf16[4,6,256,128]{3,2,1,0:T(8,128)(2,1)}) custom-call(s32[4,1]{1,0:T(4,128)S(1)} %copy.16.refs_0_, bf16[8,256,768]{2,1,0:T(8,128)(2,1)S(1)} %shard_map.93.refs_1_, bf16[4,256,384]{2,1,0:T(8,128)(2,1)S(1)} %basis.1.refs_1_.refs_2_, bf16[6,256,1024]{2,1,0:T(8,128)(2,1)S(1)} %get-tuple-element.25.refs_3_, ...), custom_call_target="tpu_custom_call" | custom-call | flops 805306368 | bytes 3145728 | tf_op jit(solution)/shard_map/output/pallas_call | solution.py:447
  (31 shorter events, 0.4 us)
Async XLA Ops:
  0.6 13.6 %copy-start.7 = (s32[4,1]{0,1:T(1,128)S(1)}, s32[4,1]{0,1:T(1,128)}, u32[]{:S(2)}) copy-start(s32[4,1]{0,1:T(1,128)} %param.12) | copy-start | bytes 52
  0.6 1.1 %copy-start.2 = (bf16[2,6,256,128]{3,2,1,0:T(8,128)(2,1)S(1)}, bf16[2,6,256,128]{3,2,1,0:T(8,128)(2,1)}, u32[]{:S(2)}) copy-start(bf16[2,6,256,128]{3,2,1,0:T(8,128)(2,1)} %rows_ref.1) | copy-start | bytes 2359300
  1.8 0.9 copy-start.3
  3.8 14.6 %collective-permute-start = (bf16[320,768]{1,0:T(8,128)(2,1)}, bf16[320,768]{1,0:T(8,128)(2,1)}, u32[]{:S(2)}, u32[]{:S(2)}) collective-permute-start(bf16[320,768]{1,0:T(8,128)(2,1)} %get-tuple-element.16.refs_0_), channel_id=1, source_target_pairs={{0,8},{4,12},{8,0},{12,4},{16,24},{20,28},{24,16},{28,20},{1,9},{5... | collective-permute-start | bytes 1474568 | tf_op jit(solution)/shard_map/ppermute | solution.py:323
  6.8 12.2 %collective-permute-start.12 = (bf16[320,768]{1,0:T(8,128)(2,1)}, bf16[320,768]{1,0:T(8,128)(2,1)}, u32[]{:S(2)}, u32[]{:S(2)}) collective-permute-start(bf16[320,768]{1,0:T(8,128)(2,1)} %get-tuple-element.16.refs_0_), channel_id=1, source_target_pairs={{8,16},{16,8},{12,20},{20,12},{9,17},{17,9},{13,21},{21,13},{10,18... | collective-permute-start | bytes 1474568 | tf_op jit(solution)/shard_map/ppermute | solution.py:323
  8.3 13.0 %collective-permute-start.16 = (bf16[320,768]{1,0:T(8,128)(2,1)}, bf16[320,768]{1,0:T(8,128)(2,1)}, u32[]{:S(2)}, u32[]{:S(2)}) collective-permute-start(bf16[320,768]{1,0:T(8,128)(2,1)} %get-tuple-element.16.refs_0_), channel_id=1, source_target_pairs={{0,4},{4,0},{8,12},{12,8},{16,20},{20,16},{24,28},{28,24},{1,5},{5... | collective-permute-start | bytes 1474568 | tf_op jit(solution)/shard_map/ppermute | solution.py:323
  9.8 1.2 %copy-start.1 = (bf16[4,4,256,128]{3,2,1,0:T(8,128)(2,1)S(1)}, bf16[4,4,256,128]{3,2,1,0:T(8,128)(2,1)}, u32[]{:S(2)}) copy-start(bf16[4,4,256,128]{3,2,1,0:T(8,128)(2,1)} %panel_ref.1) | copy-start | bytes 3145732
  11.0 1.0 copy-start.5
  12.5 51.8 %collective-permute-start.18 = (bf16[2048,256]{1,0:T(8,128)(2,1)S(1)}, bf16[2048,256]{1,0:T(8,128)(2,1)S(1)}, u32[]{:S(2)}, u32[]{:S(2)}) collective-permute-start(bf16[2048,256]{1,0:T(8,128)(2,1)S(1)} %pack_panel.1.refs_2_), channel_id=1, source_target_pairs={{0,1},{1,0},{2,3},{3,2},{4,5},{5,4},{6,7},{7,6},{8,9},{9,8},{10,11... | collective-permute-start | bytes 3145736 | tf_op jit(solution)/shard_map/ppermute | solution.py:357
  12.6 27.9 %collective-permute-start.19 = (bf16[2048,256]{1,0:T(8,128)(2,1)S(1)}, bf16[2048,256]{1,0:T(8,128)(2,1)S(1)}, u32[]{:S(2)}, u32[]{:S(2)}) collective-permute-start(bf16[2048,256]{1,0:T(8,128)(2,1)S(1)} %pack_panel.1.refs_2_), channel_id=1, source_target_pairs={{0,2},{1,3},{2,0},{3,1},{4,6},{5,7},{6,4},{7,5},{8,10},{9,11},{10,... | collective-permute-start | bytes 3145736 | tf_op jit(solution)/shard_map/ppermute | solution.py:356
  18.4 19.1 %collective-permute-start.1 = (bf16[320,768]{1,0:T(8,128)(2,1)}, bf16[320,768]{1,0:T(8,128)(2,1)S(1)}, u32[]{:S(2)}, u32[]{:S(2)}) collective-permute-start(bf16[320,768]{1,0:T(8,128)(2,1)} %collective-permute-done.refs_0_), channel_id=1, source_target_pairs={{8,16},{16,8},{12,20},{20,12},{9,17},{17,9},{13,21},{21,13},{10,18... | collective-permute-start | bytes 1474568 | tf_op jit(solution)/shard_map/ppermute | solution.py:323
  19.1 19.7 %collective-permute-start.15 = (bf16[320,768]{1,0:T(8,128)(2,1)}, bf16[320,768]{1,0:T(8,128)(2,1)S(1)}, u32[]{:S(2)}, u32[]{:S(2)}) collective-permute-start(bf16[320,768]{1,0:T(8,128)(2,1)} %collective-permute-done.refs_0_), channel_id=1, source_target_pairs={{0,4},{4,0},{8,12},{12,8},{16,20},{20,16},{24,28},{28,24},{1,5},{5... | collective-permute-start | bytes 1474568 | tf_op jit(solution)/shard_map/ppermute | solution.py:323
  21.3 15.1 %collective-permute-start.13 = (bf16[320,768]{1,0:T(8,128)(2,1)}, bf16[320,768]{1,0:T(8,128)(2,1)S(1)}, u32[]{:S(2)}, u32[]{:S(2)}) collective-permute-start(bf16[320,768]{1,0:T(8,128)(2,1)} %collective-permute-done.12), channel_id=1, source_target_pairs={{8,0},{12,4},{16,24},{20,28},{9,1},{13,5},{17,25},{21,29},{10,2},{... | collective-permute-start | bytes 1474568 | tf_op jit(solution)/shard_map/ppermute | solution.py:323
  36.5 14.8 %collective-permute-start.14 = (bf16[320,768]{1,0:T(8,128)(2,1)S(1)}, bf16[320,768]{1,0:T(8,128)(2,1)S(1)}, u32[]{:S(2)}, u32[]{:S(2)}) collective-permute-start(bf16[320,768]{1,0:T(8,128)(2,1)S(1)} %broadcast_select_fusion.refs_0_), channel_id=1, source_target_pairs={{0,4},{4,0},{8,12},{12,8},{16,20},{20,16},{24,28},{28,24},{1,5},{5... | collective-permute-start | bytes 1474568 | tf_op jit(solution)/shard_map/ppermute | solution.py:323
  37.5 12.4 %collective-permute-start.2 = (bf16[320,768]{1,0:T(8,128)(2,1)S(1)}, bf16[320,768]{1,0:T(8,128)(2,1)S(1)}, u32[]{:S(2)}, u32[]{:S(2)}) collective-permute-start(bf16[320,768]{1,0:T(8,128)(2,1)S(1)} %collective-permute-done.1), channel_id=1, source_target_pairs={{8,0},{12,4},{16,24},{20,28},{9,1},{13,5},{17,25},{21,29},{10,2},{... | collective-permute-start | bytes 1474568 | tf_op jit(solution)/shard_map/ppermute | solution.py:323
  40.5 25.2 %collective-permute-start.20 = (bf16[2048,256]{1,0:T(8,128)(2,1)S(1)}, bf16[2048,256]{1,0:T(8,128)(2,1)S(1)}, u32[]{:S(2)}, u32[]{:S(2)}) collective-permute-start(bf16[2048,256]{1,0:T(8,128)(2,1)S(1)} %collective-permute-done.19.refs_4_), channel_id=1, source_target_pairs={{0,1},{1,0},{2,3},{3,2},{4,5},{5,4},{6,7},{7,6},{8,9},{9,8},{10,11... | collective-permute-start | bytes 3145736 | tf_op jit(solution)/shard_map/ppermute | solution.py:358
  50.0 12.4 %collective-permute-start.11 = (bf16[320,768]{1,0:T(8,128)(2,1)S(1)}, bf16[320,768]{1,0:T(8,128)(2,1)S(1)}, u32[]{:S(2)}, u32[]{:S(2)}) collective-permute-start(bf16[320,768]{1,0:T(8,128)(2,1)S(1)} %broadcast_select_fusion.1.refs_0_), channel_id=1, source_target_pairs={{0,4},{4,0},{8,12},{12,8},{16,20},{20,16},{24,28},{28,24},{1,5},{5... | collective-permute-start | bytes 1474568 | tf_op jit(solution)/shard_map/ppermute | solution.py:323
  51.3 1.5 %copy-start = (bf16[4,6,256,128]{3,2,1,0:T(8,128)(2,1)S(1)}, bf16[4,6,256,128]{3,2,1,0:T(8,128)(2,1)}, u32[]{:S(2)}) copy-start(bf16[4,6,256,128]{3,2,1,0:T(8,128)(2,1)} %refs_4_.1) | copy-start | bytes 4718596
  51.3 1.5 %copy-start.4 = (bf16[6,256,64]{1,2,0:T(8,128)(2,1)S(1)}, bf16[6,256,64]{1,2,0:T(8,128)(2,1)}, u32[]{:S(2)}) copy-start(bf16[6,256,64]{1,2,0:T(8,128)(2,1)} %param.13) | copy-start | bytes 589828
  51.3 7.8 %collective-permute-start.3 = (bf16[256,768]{1,0:T(8,128)(2,1)S(1)}, bf16[256,768]{1,0:T(8,128)(2,1)S(1)}, u32[]{:S(2)}, u32[]{:S(2)}) collective-permute-start(bf16[256,768]{1,0:T(8,128)(2,1)S(1)} %get-tuple-element.18.refs_0_), channel_id=1, source_target_pairs={{0,8},{4,12},{8,0},{12,4},{16,24},{20,28},{24,16},{28,20},{1,9},{5... | collective-permute-start | bytes 1179656 | tf_op jit(solution)/shard_map/ppermute | solution.py:323
  51.3 8.6 %collective-permute-start.7 = (bf16[256,768]{1,0:T(8,128)(2,1)S(1)}, bf16[256,768]{1,0:T(8,128)(2,1)S(1)}, u32[]{:S(2)}, u32[]{:S(2)}) collective-permute-start(bf16[256,768]{1,0:T(8,128)(2,1)S(1)} %get-tuple-element.18.refs_0_), channel_id=1, source_target_pairs={{8,16},{16,8},{12,20},{20,12},{9,17},{17,9},{13,21},{21,13},{10,18... | collective-permute-start | bytes 1179656 | tf_op jit(solution)/shard_map/ppermute | solution.py:323
  59.1 20.9 %collective-permute-start.10 = (bf16[256,768]{1,0:T(8,128)(2,1)S(1)}, bf16[256,768]{1,0:T(8,128)(2,1)S(1)}, u32[]{:S(2)}, u32[]{:S(2)}) collective-permute-start(bf16[256,768]{1,0:T(8,128)(2,1)S(1)} %collective-permute-done.3.refs_0_), channel_id=1, source_target_pairs={{0,4},{4,0},{8,12},{12,8},{16,20},{20,16},{24,28},{28,24},{1,5},{5... | collective-permute-start | bytes 1179656 | tf_op jit(solution)/shard_map/ppermute | solution.py:323
  59.9 14.4 %collective-permute-start.4 = (bf16[256,768]{1,0:T(8,128)(2,1)S(1)}, bf16[256,768]{1,0:T(8,128)(2,1)S(1)}, u32[]{:S(2)}, u32[]{:S(2)}) collective-permute-start(bf16[256,768]{1,0:T(8,128)(2,1)S(1)} %collective-permute-done.3.refs_0_), channel_id=1, source_target_pairs={{8,16},{16,8},{12,20},{20,12},{9,17},{17,9},{13,21},{21,13},{10,18... | collective-permute-start | bytes 1179656 | tf_op jit(solution)/shard_map/ppermute | solution.py:323
  62.4 11.6 %collective-permute-start.8 = (bf16[256,768]{1,0:T(8,128)(2,1)S(1)}, bf16[256,768]{1,0:T(8,128)(2,1)S(1)}, u32[]{:S(2)}, u32[]{:S(2)}) collective-permute-start(bf16[256,768]{1,0:T(8,128)(2,1)S(1)} %collective-permute-done.7), channel_id=1, source_target_pairs={{8,0},{12,4},{16,24},{20,28},{9,1},{13,5},{17,25},{21,29},{10,2},{... | collective-permute-start | bytes 1179656 | tf_op jit(solution)/shard_map/ppermute | solution.py:323
  64.3 15.2 %collective-permute-start.17 = (bf16[256,768]{1,0:T(8,128)(2,1)S(1)}, bf16[256,768]{1,0:T(8,128)(2,1)S(1)}, u32[]{:S(2)}, u32[]{:S(2)}) collective-permute-start(bf16[256,768]{1,0:T(8,128)(2,1)S(1)} %get-tuple-element.18.refs_0_), channel_id=1, source_target_pairs={{0,4},{4,0},{8,12},{12,8},{16,20},{20,16},{24,28},{28,24},{1,5},{5... | collective-permute-start | bytes 1179656 | tf_op jit(solution)/shard_map/ppermute | solution.py:323
  74.0 19.2 %collective-permute-start.9 = (bf16[256,768]{1,0:T(8,128)(2,1)S(1)}, bf16[256,768]{1,0:T(8,128)(2,1)S(1)}, u32[]{:S(2)}, u32[]{:S(2)}) collective-permute-start(bf16[256,768]{1,0:T(8,128)(2,1)S(1)} %broadcast_select_fusion.2.refs_0_), channel_id=1, source_target_pairs={{0,4},{4,0},{8,12},{12,8},{16,20},{20,16},{24,28},{28,24},{1,5},{5... | collective-permute-start | bytes 1179656 | tf_op jit(solution)/shard_map/ppermute | solution.py:323
  74.3 17.8 %collective-permute-start.5 = (bf16[256,768]{1,0:T(8,128)(2,1)S(1)}, bf16[256,768]{1,0:T(8,128)(2,1)S(1)}, u32[]{:S(2)}, u32[]{:S(2)}) collective-permute-start(bf16[256,768]{1,0:T(8,128)(2,1)S(1)} %collective-permute-done.4), channel_id=1, source_target_pairs={{8,0},{12,4},{16,24},{20,28},{9,1},{13,5},{17,25},{21,29},{10,2},{... | collective-permute-start | bytes 1179656 | tf_op jit(solution)/shard_map/ppermute | solution.py:323
  92.2 8.5 %collective-permute-start.6 = (bf16[256,768]{1,0:T(8,128)(2,1)S(1)}, bf16[256,768]{1,0:T(8,128)(2,1)S(1)}, u32[]{:S(2)}, u32[]{:S(2)}) collective-permute-start(bf16[256,768]{1,0:T(8,128)(2,1)S(1)} %broadcast_select_fusion.3.refs_0_), channel_id=1, source_target_pairs={{0,4},{4,0},{8,12},{12,8},{16,20},{20,16},{24,28},{28,24},{1,5},{5... | collective-permute-start | bytes 1179656 | tf_op jit(solution)/shard_map/ppermute | solution.py:323
  100.6 1.0 copy-start.6

commit v4 on v3

v4 whole, which is shorter than its diff:
```python
import math

import jax
import jax.numpy as jnp
from jax import lax
from jax.experimental import pallas as pl
from jax.experimental.pallas import tpu as pltpu
from jax.sharding import PartitionSpec as P

F32 = jnp.float32
BF16 = jnp.bfloat16
NN = (((1,), (0,)), ((), ()))
NT = (((1,), (1,)), ((), ()))
TN = (((0,), (0,)), ((), ()))
PLACE_VMEM = 1024 * 1024
PLACE_P = 10
PLACE_Q = 8
PLACE_Q0 = 1
MID_SCALE = 1
SAMPLED_SCALE = 1
BLOCKS = 3
GRAM_FLOPS = int(1e9)
BETWEEN = "second"
CORES_SCALE = 1
TIE0 = 2
TIE_Y = 1
TIE_GRAM = 0
BASIS_FLOPS = int(1e9)
FORWARD_AT = "gram"
NEAR_AT = "pb"
GATE_ALONG = "third"
GATE_FORWARD = "pb"
TIE1 = "cores"
EARLY_Q = 0
VMEM_BYTES = 14 * 1024 * 1024


def dot(left, right, dims=NN, precision=None):
    return lax.dot_general(left, right, dims, precision=precision, preferred_element_type=F32)


def halves(shape, half):
    return lax.broadcasted_iota(jnp.int32, shape, len(shape) - 1) // half % 2 == 0


def swap(value, half):
    return jnp.concatenate([value[:, half:], value[:, :half]], axis=1)


def call(kernel, out_shape, in_specs, scratch=(), flops=0, moved=0, aliases=None):
    out_specs = jax.tree.map(lambda _: pl.BlockSpec(memory_space=pltpu.VMEM), out_shape)
    return pl.pallas_call(
        kernel,
        out_shape=out_shape,
        in_specs=in_specs,
        out_specs=out_specs,
        scratch_shapes=list(scratch),
        input_output_aliases=aliases or {},
        compiler_params=pltpu.CompilerParams(vmem_limit_bytes=VMEM_BYTES),
        cost_estimate=pl.CostEstimate(flops=flops, bytes_accessed=moved, transcendentals=0),
    )


IN_VMEM = pl.BlockSpec(memory_space=pltpu.VMEM)
IN_SMEM = pl.BlockSpec(memory_space=pltpu.SMEM)
ANYWHERE = pl.BlockSpec(memory_space=pl.ANY)


def pack_rows_kernel(rows_ref, sketch_ref, pb_ref, q_ref):
    _, columns, size, width = rows_ref.shape
    half = width // 2
    for j in range(columns):
        first, second = rows_ref[0, j], rows_ref[1, j]
        lanes = pl.ds(j * width, width)
        pb_ref[:size, lanes] = jnp.concatenate([first[:, :half], second[:, :half]], axis=1)
        q_pair = jnp.concatenate([first[:, half:], second[:, half:]], axis=1)
        q_ref[:, lanes] = q_pair
        pb_ref[pl.ds(size, half), lanes] = dot(sketch_ref[j], q_pair).astype(BF16)


def pack_panel_kernel(panel_ref, inv_ref, out_ref):
    count, pivots, size, width = panel_ref.shape
    half = width // 2
    for k in range(pivots):
        rights = [jnp.transpose(panel_ref[i, k])[half:] for i in range(count)]
        hat = dot(jnp.concatenate(rights, axis=0), inv_ref[k]).astype(BF16)
        for i in range(count):
            start = (k // 2) * count * width + i * width + (k % 2) * half
            out_ref[pl.ds(start, half), :] = hat[i * half : (i + 1) * half]
    base = (pivots // 2) * count * width
    for i in range(count):
        for k in range(0, pivots, 2):
            pair = [panel_ref[i, k + m][:, :half] for m in range(2)]
            out_ref[pl.ds(base + i * size, size), pl.ds(k * half, width)] = jnp.concatenate(pair, axis=1)


def target_sketch(target_ref, sketch_ref, out_ref):
    count, columns, size, width = target_ref.shape
    half = width // 2
    first = halves((half, width), half)
    zero = jnp.zeros((half, width), BF16)
    for i in range(count):
        for j in range(0, columns, 2):
            core = []
            for m in range(2):
                product = dot(sketch_ref[j + m], target_ref[i, j + m])
                core.append(jnp.where(first, swap(product, half), 0.0).astype(BF16))
            left = jnp.concatenate([target_ref[i, j], target_ref[i, j + 1]], axis=1)
            right = jnp.concatenate(
                [jnp.concatenate([core[0], zero], axis=1), jnp.concatenate([zero, core[1]], axis=1)], axis=0
            )
            out_ref[i, :, pl.ds(j * half, width)] = dot(left, right, NT)


def fetch_all(sources, target, owners_ref, sem):
    copies = []
    for n, source in enumerate(sources):
        copies.append(pltpu.make_async_copy(source, target.at[owners_ref[n]], sem.at[n]))
    for copy in copies:
        copy.start()
    return copies


def mid_pair(n_rows, t, pb_all, panel_ref, mid_ref, slot, weight_ref):
    _, tall, wide = mid_ref.shape
    count = weight_ref.shape[0]
    width = tall // count
    half = width // 2
    columns = wide // width
    size = pb_all.shape[1] - half
    row_half = lax.broadcasted_iota(jnp.int32, (tall, 2 * width), 0) // half % 2
    lane_half = lax.broadcasted_iota(jnp.int32, (tall, 2 * width), 1) // half % 2
    same = row_half == lane_half
    zero = jnp.zeros((half, width), BF16)
    first = arrivals(n_rows)(lax.axis_index("rows"), t)
    plane = first // 2
    for m in range(2):
        part = (first + m) % 2
        left = panel_ref[plane, pl.ds(pl.multiple_of(part * tall, tall), tall), :]
        for j in range(0, columns, 2):
            lanes = pl.ds(j * width, 2 * width)
            mid = dot(left, pb_all[t + m, :size, lanes])
            mid = jnp.where(same, mid, 0.0).astype(BF16)
            mid_ref[slot + m, :, lanes] = mid
            b_pair = pb_all[t + m, size:, lanes]
            right = jnp.concatenate(
                [
                    jnp.concatenate([b_pair[:, :width], zero], axis=1),
                    jnp.concatenate([zero, b_pair[:, width:]], axis=1),
                ],
                axis=0,
            )
            product = dot(mid, right, NT).astype(BF16)
            for i in range(count):
                weight_ref[i, pl.ds(pl.multiple_of(part * width, width), width), pl.ds(j * half, width)] = product[
                    i * width : (i + 1) * width
                ]
    return plane


def subtract(total_ref, panel_ref, plane, weight_ref):
    count, size, _ = total_ref.shape
    base = panel_ref.shape[1] - count * size
    for i in range(count):
        total_ref[i] = total_ref[i] - dot(panel_ref[plane, pl.ds(base + i * size, size), :], weight_ref[i])


def mid_kernel(n_rows, n_cols, pb_all, target_ref, sketch_ref, *refs):
    panels = refs[:n_cols]
    mid_ref, total_ref, panel_ref, weight, sem_panel = refs[n_cols:]
    copies = fetch_all(panels, panel_ref, column_owners(n_cols), sem_panel)
    target_sketch(target_ref, sketch_ref, total_ref)
    for copy in copies:
        copy.wait()

    def step(s, carry):
        plane = mid_pair(n_rows, 2 * s, pb_all, panel_ref, mid_ref, 2 * s, weight)
        subtract(total_ref, panel_ref, plane, weight)
        return carry

    lax.fori_loop(0, n_rows // 2 - 1, step, 0)


def sampled_kernel(n_rows, pb_all, panel_ref, total_ref, mid_ref, sampled_ref, weight):
    plane = mid_pair(n_rows, n_rows - 2, pb_all, panel_ref, mid_ref, 0, weight)
    sampled_ref[...] = total_ref[...]
    subtract(sampled_ref, panel_ref, plane, weight)


def gram_kernel(blocks, sampled_ref, state):
    count, _, wide = sampled_ref.shape
    half, _, width = state.shape
    pairs = wide // width
    first = halves((half, width), half)
    for i in range(count):
        for p in range(pairs):
            z_pair = sampled_ref[i, :, pl.ds(p * width, width)]
            gram = dot(z_pair, z_pair, TN, lax.Precision.HIGHEST)
            state[:, i * pairs + p, :] = jnp.where(first, gram[:half], gram[half:])
    eliminate(state, 0, blocks, math.sqrt(sampled_ref.shape[1]))


def basis_kernel(blocks, sampled_ref, state_in, state, basis_ref):
    count, size, wide = sampled_ref.shape
    half, _, width = state.shape
    pairs = wide // width
    first = halves((half, width), half)
    eliminate(state, blocks, half // 8, math.sqrt(size))
    for i in range(count):
        for p in range(pairs):
            inverse = state[:, i * pairs + p, :]
            inverse = jnp.concatenate([jnp.where(first, inverse, 0.0), jnp.where(first, 0.0, inverse)], axis=0)
            z_pair = sampled_ref[i, :, pl.ds(p * width, width)]
            product = dot(z_pair, inverse, NT, lax.Precision.HIGHEST)
            basis_ref[i, :, pl.ds(p * width, width)] = product.astype(BF16)


def eliminate(state, first_block, last_block, root_size):
    half, held, width = state.shape
    sub = 8
    lane = lax.broadcasted_iota(jnp.int32, (held, width), 1)
    column = lane % half
    origin = lane - column

    def pick(row, pivot):
        return jnp.take_along_axis(row, origin + pivot, axis=1)

    def one_block(block, carry):
        start = block * sub
        rows = [state[start + r] for r in range(sub)]
        core = {(r, s): pick(rows[r], start + s) for r in range(sub) for s in range(r, sub)}
        lines, finals = [], []
        for q in range(sub):
            pivot = start + q
            root = lax.rsqrt(core[q, q])
            inverse = root * root
            finals.append(rows[q])
            unit = jnp.where(column == pivot, 1.0, rows[q])
            state[pivot] = jnp.where(column <= pivot, unit * (root_size * root), 0.0)
            line = unit * inverse
            lines.append(jnp.where(jnp.logical_and(column > pivot, column < start + sub), 0.0, line))
            for r in range(q + 1, sub):
                scaled = core[q, r] * inverse
                rows[r] = jnp.where(column == pivot, 0.0, rows[r]) - core[q, r] * line
                for s in range(r, sub):
                    core[r, s] = core[r, s] - scaled * core[q, s]
        inside = jnp.logical_and(column >= start, column < start + sub)

        def update(v, inner):
            for r in range(sub):
                row = v * sub + r
                value = jnp.where(inside, 0.0, state[row])
                for q in range(sub):
                    value = value - pick(finals[q], row) * lines[q]
                state[row] = value
            return inner

        lax.fori_loop(block + 1, half // sub, update, 0)
        return carry

    lax.fori_loop(first_block, last_block, one_block, 0)


def cores_kernel(
    n_rows, near_ref, basis_ref, early_ref, late_ref, panel_ref, target_ref, left_ref, value_ref, near_left_ref, cores
):
    count, size, wide = basis_ref.shape
    columns, width = target_ref.shape[1], target_ref.shape[3]
    half = width // 2
    n_cols, _, deep = panel_ref.shape
    per_col = deep // width
    base = per_col * count * width
    first = halves((half, width), half)
    zero = jnp.zeros((half, width), BF16)
    tall = count * width
    turned = []
    for i in range(count):
        basis_t = jnp.transpose(basis_ref[i])
        turned.append(basis_t)
        for c in range(n_cols):
            cores[i, :, pl.ds(c * deep, deep)] = dot(basis_t, panel_ref[c, pl.ds(base + i * size, size), :]).astype(BF16)
    for i in range(0, count, 2):
        for j in range(columns):
            core = []
            for m in range(2):
                product = dot(turned[i + m][j * half : (j + 1) * half], target_ref[i + m, j])
                core.append(jnp.where(first, 0.0, swap(product, half)).astype(BF16))
            left = jnp.concatenate([target_ref[i, j], target_ref[i + 1, j]], axis=1)
            right = jnp.concatenate(
                [jnp.concatenate([core[0], zero], axis=1), jnp.concatenate([zero, core[1]], axis=1)], axis=0
            )
            value_ref[j, :, pl.ds(i * half, width)] = dot(left, right, NT)

    owner = arrivals(n_rows)
    me = lax.axis_index("rows")

    def one_pair(t, mid_ref, slot):
        o = owner(me, t)
        lanes = pl.ds(pl.multiple_of(t * width, width), width)
        from_lanes = pl.ds(pl.multiple_of(o * width, width), width)
        for i in range(count):
            for j in range(columns):
                product = dot(
                    cores[i, pl.ds(j * half, half), from_lanes],
                    mid_ref[slot, pl.ds(i * width, width), pl.ds(j * width, width)],
                )
                left_ref[j, pl.ds(i * half, half), lanes] = product.astype(BF16)
            near = pl.ds(pl.multiple_of(near_ref[0, i] * width, width), width)
            x_part = panel_ref[
                o // per_col, pl.ds(base + i * size, size), pl.ds(pl.multiple_of(o % per_col * width, width), width)
            ]
            near_left_ref[i, :, lanes] = dot(x_part, mid_ref[slot, pl.ds(i * width, width), near]).astype(BF16)

    def step(t, carry):
        one_pair(t, early_ref, t)
        return carry

    lax.fori_loop(0, n_rows - 2, step, 0)
    for m in range(2):
        one_pair(n_rows - 2 + m, late_ref, m)


def output_kernel(n_rows, near_ref, q_all, *refs):
    basis_ref, left_ref, value_ref, near_left_ref, near_block_ref, near_out_ref, far_out_ref = refs
    count, columns, size, width = far_out_ref.shape
    half = width // 2
    root_size = math.sqrt(size)
    first = halves((size, width), half)
    for j in range(columns):
        right = jnp.concatenate([q_all[o, :, pl.ds(j * width, width)] for o in range(n_rows)], axis=1)
        weights = (value_ref[j] - dot(right, left_ref[j], NT)) / root_size
        for i in range(count):
            tile = weights[:, i // 2 * width : (i // 2 + 1) * width]
            if i % 2 == 0:
                tile = swap(tile, half)
            basis = basis_ref[i, :, pl.ds(j // 2 * width, width)]
            if j % 2 == 1:
                basis = swap(basis, half)
            block = jnp.where(first, basis, tile.astype(BF16))
            is_near = near_ref[0, i] == j
            for s in range(1, near_ref.shape[0]):
                is_near = jnp.logical_or(is_near, near_ref[s, i] == j)
            far_out_ref[i, j] = jnp.where(is_near, jnp.zeros_like(block), block)
    for i in range(count):
        near = pl.ds(pl.multiple_of(near_ref[0, i] * width, width), width)
        right = jnp.concatenate([q_all[o, :, near] for o in range(n_rows)], axis=1)
        update = dot(near_left_ref[i], right, NT)
        near_out_ref[i, 0] = (near_block_ref[i, 0].astype(F32) - update).astype(BF16)


def arrivals(n):
    if n != 8:
        return lambda me, t: t
    third = lambda me: jnp.where(me < 4, 4, 2) + me % 2
    fourth = lambda me: jnp.where(me < 4, 6, 0) + me % 2

    def owner(me, t):
        base = jnp.where(t < 2, me, jnp.where(t < 4, me ^ 2, jnp.where(t < 6, third(me), fourth(me))))
        return base ^ (t % 2)

    return owner


def held(value, *events):
    events = [event for event in events if event is not None]
    return lax.optimization_barrier((value,) + tuple(events))[0] if events else value


def place(buffer, t, blocks, n, micros):
    def kernel(*refs):
        sources, target, sem = refs[:2], refs[-2], refs[-1]
        slot = t(lax.axis_index("rows")) if callable(t) else t
        copies = fetch_all(sources, target, [slot, slot + 1], sem)
        for copy in copies:
            copy.wait()

    given = [] if buffer is None else [buffer]
    return pl.pallas_call(
        kernel,
        out_shape=jax.ShapeDtypeStruct((n,) + blocks[0].shape, blocks[0].dtype),
        in_specs=[IN_VMEM] * (2 + len(given)),
        out_specs=IN_VMEM,
        scratch_shapes=[pltpu.SemaphoreType.DMA((2,))],
        input_output_aliases={2: 0} if given else {},
        compiler_params=pltpu.CompilerParams(vmem_limit_bytes=1024 * 1024),
        cost_estimate=pl.CostEstimate(flops=int(micros * 1.15e9), bytes_accessed=0, transcendentals=0),
    )(*blocks, *given)


class Gather:
    slots = [0, 2, 4, 6]
    inner = [(2, 4), (4, 2), (3, 5), (5, 3)]
    outward = [(2, 0), (3, 1), (4, 6), (5, 7)]

    def __init__(self, block, micros):
        self.n = lax.axis_size("rows")
        self.block, self.micros, self.whole = block, micros, None
        me = lax.axis_index("rows")
        self.is_end = jnp.logical_or(me < 2, me >= self.n - 2)

    def send(self, value, pairs):
        return lax.ppermute(value, "rows", pairs)

    def flip(self, value, bits):
        return self.send(value, [(i, i ^ bits) for i in range(self.n)])

    def start_across(self, *events):
        self.x_own = self.flip(held(self.block, *events), 1)

    def start_along(self, *events):
        block = held(self.block, *events)
        self.near, self.mid = self.flip(block, 2), self.send(block, self.inner)

    def forward(self, *events):
        self.x_near = self.flip(held(self.near, *events), 1)
        self.far = self.send(held(self.near, *events), self.inner)
        out = self.send(held(self.mid, *events), self.outward)
        self.second = jnp.where(self.is_end, out, self.mid)

    def forward_again(self, *events):
        self.x_second = self.flip(held(self.second, *events), 1)
        out = self.send(held(self.far, *events), self.outward)
        self.third = jnp.where(self.is_end, out, self.far)

    def finish(self, *events):
        self.x_third = self.flip(held(self.third, *events), 1)

    def put(self, stage, *events):
        pair = [
            lambda: (self.block, self.x_own),
            lambda: (self.near, self.x_near),
            lambda: (self.second, self.x_second),
            lambda: (self.third, self.x_third),
        ][stage]()
        pair = (pair[0], held(pair[1], *events)) if stage == 0 else pair
        whole = self.whole if stage == 0 or all(event is None for event in events) else held(self.whole, *events)
        self.whole = place(whole, self.slots[stage], pair, self.n, self.micros)
        return self.whole


class DirectGather(Gather):
    slots = [0, 2, lambda me: jnp.where((me < 2) | (me > 5), 4, 6), lambda me: jnp.where((me < 2) | (me > 5), 6, 4)]

    def start_along(self, *events):
        block = held(self.block, *events)
        self.second, self.near = self.flip(block, 4), self.flip(block, 2)

    def exchange_near(self, *events):
        self.x_near = self.flip(held(self.near, *events), 1)

    def forward(self, *events):
        out = self.send(held(self.second, *events), self.outward)
        middle = self.send(held(self.block, self.second, *events), self.inner)
        self.x_second = self.flip(held(self.second, *events), 1)
        self.third = jnp.where(self.is_end, out, middle)


class PlainGather:
    def __init__(self, block, micros):
        self.block = self.near = self.second = self.third = self.far = block
        self.whole = None

    def start_across(self, *events):
        pass

    start_along = forward = forward_again = finish = exchange_near = start_across

    def put(self, stage, *events):
        if self.whole is None:
            self.whole = lax.all_gather(self.block, "rows")
        return self.whole


def column_owners(n):
    me = lax.axis_index("cols")
    return [me ^ t for t in range(n)] if n == 4 else list(range(n))


def gather_cols(block):
    n = lax.axis_size("cols")
    if n != 4:
        whole = lax.all_gather(block, "cols")
        return [whole[o] for o in range(n)]
    core = [(i, i ^ 1) for i in range(n)]
    other = [(i, i ^ 2) for i in range(n)]
    y = lax.ppermute(block, "cols", other)
    own = lax.ppermute(block, "cols", core)
    return [block, own, y, lax.ppermute(y, "cols", core)]


def per_device(panel_cols, pivot_inv, pivot_rows, target_factors, near_blocks, near_cols, sketch):
    n_rows, n_cols = lax.axis_size("rows"), lax.axis_size("cols")
    count, pivots, size, width = panel_cols.shape
    owned, columns = pivot_rows.shape[:2]
    half = width // 2
    wide = columns * half
    assert owned == 2 and columns % 2 == 0 and count % 2 == 0 and pivots % 2 == 0
    assert near_cols.shape[1] == 1
    shape = jax.ShapeDtypeStruct
    sketch_t = jnp.swapaxes(sketch, 1, 2)
    near_t = near_cols.T

    with jax.named_scope("pack_rows"):
        pb, q = call(
            pack_rows_kernel,
            (shape((size + half, columns * width), BF16), shape((size, columns * width), BF16)),
            [IN_VMEM] * 2,
            flops=2 * columns * half * size * width,
            moved=4 * pivot_rows.size,
        )(pivot_rows, sketch_t)
    panel_rows = (pivots // 2) * count * width + count * size
    with jax.named_scope("pack_panel"):
        panel = call(
            pack_panel_kernel,
            shape((panel_rows, pivots * half), BF16),
            [IN_VMEM] * 2,
            flops=2 * count * pivots * half * size * size,
            moved=4 * panel_cols.size,
        )(panel_cols, pivot_inv)
    panels = gather_cols(panel)
    vmem = pltpu.VMEM
    deep = n_rows * width
    mid_flops = 4 * count * width * size * columns * width
    weight_scratch = vmem((count, 2 * width, wide), BF16)

    def mids(arrived, target):
        with jax.named_scope("mid"):
            return call(
                lambda *refs: mid_kernel(n_rows, n_cols, *refs),
                (
                    shape((n_rows - 2, count * width, columns * width), BF16),
                    shape((count, size, wide), F32),
                    shape((n_cols,) + panel.shape, BF16),
                ),
                [IN_VMEM] * 3 + [ANYWHERE] * n_cols,
                [weight_scratch, pltpu.SemaphoreType.DMA((n_cols,))],
                flops=mid_flops * (n_rows - 2) * MID_SCALE,
            )(arrived, target, sketch_t, *panels)

    kind = Gather if n_rows == 8 else PlainGather
    pb_way = kind(pb, PLACE_P)
    q_way = (DirectGather if n_rows == 8 else kind)(q, PLACE_Q)
    pb_way.start_along()
    pb_way.start_across()
    pb_way.forward()
    if TIE0 < 3:
        q_way.start_across(pb_way.near)
    pb_way.forward_again()
    pb_way.finish()
    pb_way.put(0, panels[2] if TIE_Y == 2 else None)
    q_way.micros = PLACE_Q0
    q_first = q_way.put(0) if TIE0 < 3 else None
    pb_way.put(1, q_first if TIE0 == 1 else None, panels[2] if TIE_Y == 1 else None)
    arrived = pb_way.put(2, q_first if TIE0 == 2 else None)
    q_way.micros = PLACE_Q
    mid_early, total, panel_whole = mids(arrived, held(target_factors, pb_way.far))
    if GATE_ALONG == "third":
        q_way.start_along(pb_way.third)
    if GATE_ALONG == "mid":
        q_way.start_along(total)
    if GATE_ALONG == "far":
        q_way.start_along(pb_way.far)
    pb_all = pb_way.put(3, total)
    if TIE0 == 3:
        q_way.start_across(pb_all)
        q_way.put(0)
    with jax.named_scope("sampled"):
        mid_late, sampled = call(
            lambda *refs: sampled_kernel(n_rows, *refs),
            (shape((2,) + mid_early.shape[1:], BF16), shape((count, size, wide), F32)),
            [IN_VMEM] * 3,
            [weight_scratch],
            flops=mid_flops * 2 * SAMPLED_SCALE,
        )(pb_all, panel_whole, total)
    if NEAR_AT != "gram":
        q_way.exchange_near({"pb": pb_all, "sampled": sampled}[NEAR_AT])
    if FORWARD_AT == "pb":
        q_way.forward(pb_all)
    state_shape = shape((half, -(-count * columns // 2 // 8) * 8, width), F32)
    with jax.named_scope("gram"):
        state = call(
            lambda *refs: gram_kernel(BLOCKS, *refs),
            state_shape,
            [IN_VMEM],
            flops=GRAM_FLOPS,
        )(held(sampled, q_way.near if TIE_GRAM else None))
    if NEAR_AT == "gram":
        q_way.exchange_near(state)
    if FORWARD_AT == "gram":
        q_way.forward(state)
    q_way.finish()
    q_second = q_way.put(1)
    q_way.put(2)
    q_all = q_way.put(3)
    state = held(state, {"near": q_way.near, "none": None, "second": q_way.second}[BETWEEN])
    with jax.named_scope("basis"):
        _, basis = call(
            lambda *refs: basis_kernel(BLOCKS, *refs),
            (state_shape, shape((count, size, wide), BF16)),
            [IN_VMEM] * 2,
            flops=BASIS_FLOPS,
            aliases={1: 0},
        )(sampled, state)
    basis = held(basis, q_second if TIE1 == "cores" else None)
    with jax.named_scope("cores"):
        left, value, near_left = call(
            lambda *refs: cores_kernel(n_rows, *refs),
            (
                shape((columns, count * half, deep), BF16),
                shape((columns, size, count * half), F32),
                shape((count, size, deep), BF16),
            ),
            [IN_SMEM] + [IN_VMEM] * 5,
            [vmem((count, wide, deep), BF16)],
            flops=3 * n_rows * count * width * size * columns * width * CORES_SCALE,
            moved=2 * n_rows * (pb.size + count * width * columns * width),
        )(near_t, basis, mid_early, mid_late, panel_whole, target_factors)
    with jax.named_scope("output"):
        near_new, far_new = call(
            lambda *refs: output_kernel(n_rows, *refs),
            (shape(near_blocks.shape, BF16), shape(target_factors.shape, BF16)),
            [IN_SMEM] + [IN_VMEM] * 6,
            flops=2 * columns * size * deep * count * half,
            moved=2 * n_rows * q.size,
        )(near_t, q_all, basis, left, value, near_left, near_blocks)
    return near_new, far_new


def solution(mesh):
    placed = (
        P("rows", "cols", None, None),
        P("cols", None, None),
        P("rows", "cols", None, None),
        P("rows", "cols", None, None),
        P("rows", "cols", None, None),
        P("rows", "cols"),
        P("cols", None, None),
    )
    return jax.shard_map(
        per_device,
        mesh=mesh,
        in_specs=placed,
        out_specs=(P("rows", "cols", None, None), P("rows", "cols", None, None)),
        check_vma=False,
    )
```

time: 106 us -> 100 us (0.943)
  Pallas kernels: 39.8 us -> 36 us
  waiting for transfers between devices: 36.2 us -> 33.6 us
    pallas_call x11 -> x12, Pallas kernels: 27.9 us -> 25.2 us  [the longest x1 6.83 us: mids(): call(lambda *refs: mid_kernel(n_rows, n_cols, *refs), (shape((n_rows - 2,...]
    ppermute x19 -> x18, waiting for transfers between devices: 36.2 us -> 33.6 us  [the longest x17 33.6 us: send(): return lax.ppermute(value, 'rows', pairs)]
    ppermute x19 -> x18, starting transfers between devices: 21.1 us -> 20.9 us  [the longest x17 20.9 us: send(): return lax.ppermute(value, 'rows', pairs)]
    unnamed x17 -> x16, local copies, waits for them, and re-layouts: 5.03 us -> 4.95 us
  transfers between devices with their start and end apart: 21 -> 20, of which waited for: 8 -> 7; matrix products, arithmetic and copies ran while one was open for 0% -> 0% of each run, Pallas kernels for 33% -> 33%
where the time goes in v4:
time: 100 us; the launch traced here: 98.3 us
  Pallas kernels  36 us (36%)
  waiting for transfers between devices  33.6 us (34%)
  starting transfers between devices  22.5 us (22%)
  local copies, waits for them, and re-layouts  4.95 us (5%)
    ppermute x17, waiting for transfers between devices, send(): return lax.ppermute(value, 'rows', pairs)  33.6 us
    ppermute x17, starting transfers between devices, send(): return lax.ppermute(value, 'rows', pairs)  20.9 us
    pallas_call x1, Pallas kernels, mids(): call(lambda *refs: mid_kernel(n_rows, n_cols, *refs), (shape((n_rows - 2,...  6.83 us
    pallas_call x1, Pallas kernels, per_device(): call(lambda *refs: cores_kernel(n_rows, *refs), (shape((columns, count *...  6.76 us
    pallas_call x1, Pallas kernels, per_device(): call(lambda *refs: gram_kernel(BLOCKS, *refs), state_shape, [IN_VMEM], fl...  6.65 us
    pallas_call x8, Pallas kernels, place(): pl.pallas_call(kernel, out_shape=jax.ShapeDtypeStruct((n,) + blocks[0].sh...  5.19 us
    pallas_call x1, Pallas kernels, per_device(): call(lambda *refs: basis_kernel(BLOCKS, *refs), (state_shape, shape((coun...  5.02 us
    unnamed x16, local copies, waits for them, and re-layouts  4.95 us
  transfers between devices with their start and end apart: 20, of which 7 were waited for; matrix products, arithmetic and copies ran while one was open for 0% of the time, Pallas kernels for 33%

profile of v4, /device:TPU:0, one launch (start us, length us, event | category | flops | bytes accessed | tf_op | source)
XLA Modules:
  0.0 98.3 jit_solution(1883276905168269039)
XLA Ops:
  0.6 1.1 %copy-done.2 = bf16[2,6,256,128]{3,2,1,0:T(8,128)(2,1)S(1)} copy-done((bf16[2,6,256,128]{3,2,1,0:T(8,128)(2,1)S(1)}, bf16[2,6,256,128]{3,2,1,0:T(8,128)(2,1)}, u32[]{:S(2)}) %copy-start.2) | copy-done | bytes 786456
  1.8 0.9 copy-done.3
  2.7 0.3 pack_rows.1
  3.0 3.1 %collective-permute-start = (bf16[320,768]{1,0:T(8,128)(2,1)S(1)}, bf16[320,768]{1,0:T(8,128)(2,1)S(1)}, u32[]{:S(2)}, u32[]{:S(2)}) collective-permute-start(bf16[320,768]{1,0:T(8,128)(2,1)S(1)} %get-tuple-element.25.refs_0_), channel_id=1, source_target_pairs={{0,8},{4,12},{8,0},{12,4},{16,24},{20,28},{24,16},{28,20},{1,9},{5... | collective-permute-start | bytes 1474568 | tf_op jit(solution)/shard_map/ppermute | solution.py:402
  6.1 1.5 %collective-permute-start.9 = (bf16[320,768]{1,0:T(8,128)(2,1)S(1)}, bf16[320,768]{1,0:T(8,128)(2,1)}, u32[]{:S(2)}, u32[]{:S(2)}) collective-permute-start(bf16[320,768]{1,0:T(8,128)(2,1)S(1)} %get-tuple-element.25.refs_0_), channel_id=1, source_target_pairs={{0,4},{4,0},{8,12},{12,8},{16,20},{20,16},{24,28},{28,24},{1,5},{5... | collective-permute-start | bytes 1474568 | tf_op jit(solution)/shard_map/ppermute | solution.py:402
  7.6 1.5 %collective-permute-start.5 = (bf16[320,768]{1,0:T(8,128)(2,1)S(1)}, bf16[320,768]{1,0:T(8,128)(2,1)}, u32[]{:S(2)}, u32[]{:S(2)}) collective-permute-start(bf16[320,768]{1,0:T(8,128)(2,1)S(1)} %get-tuple-element.25.refs_0_), channel_id=1, source_target_pairs={{8,16},{16,8},{12,20},{20,12},{9,17},{17,9},{13,21},{21,13},{10,18... | collective-permute-start | bytes 1474568 | tf_op jit(solution)/shard_map/ppermute | solution.py:402
  9.1 1.2 %copy-done.1 = bf16[4,4,256,128]{3,2,1,0:T(8,128)(2,1)S(1)} copy-done((bf16[4,4,256,128]{3,2,1,0:T(8,128)(2,1)S(1)}, bf16[4,4,256,128]{3,2,1,0:T(8,128)(2,1)}, u32[]{:S(2)}) %copy-start.1) | copy-done | bytes 1048600
  10.3 1.0 %copy-done.5 = bf16[4,256,256]{2,1,0:T(8,128)(2,1)S(1)} copy-done((bf16[4,256,256]{2,1,0:T(8,128)(2,1)S(1)}, bf16[4,256,256]{2,1,0:T(8,128)(2,1)}, u32[]{:S(2)}) %copy-start.5) | copy-done | bytes 524312
  11.3 0.5 pack_panel.1.refs_3_
  11.8 1.6 %collective-permute-start.10 = (bf16[2048,256]{1,0:T(8,128)(2,1)S(1)}, bf16[2048,256]{1,0:T(8,128)(2,1)S(1)}, u32[]{:S(2)}, u32[]{:S(2)}) collective-permute-start(bf16[2048,256]{1,0:T(8,128)(2,1)S(1)} %pack_panel.1.refs_3_), channel_id=1, source_target_pairs={{0,2},{1,3},{2,0},{3,1},{4,6},{5,7},{6,4},{7,5},{8,10},{9,11},{10,... | collective-permute-start | bytes 3145736 | tf_op jit(solution)/shard_map/ppermute | solution.py:486
  13.4 3.9 %collective-permute-done.refs_0_ = bf16[320,768]{1,0:T(8,128)(2,1)S(1)} collective-permute-done((bf16[320,768]{1,0:T(8,128)(2,1)S(1)}, bf16[320,768]{1,0:T(8,128)(2,1)S(1)}, u32[]{:S(2)}, u32[]{:S(2)}) %collective-permute-start) | collective-permute-done | bytes 491552 | tf_op jit(solution)/shard_map/ppermute | solution.py:402
  17.3 1.7 %collective-permute-start.11 = (bf16[256,768]{1,0:T(8,128)(2,1)S(1)}, bf16[256,768]{1,0:T(8,128)(2,1)S(1)}, u32[]{:S(2)}, u32[]{:S(2)}) collective-permute-start(bf16[256,768]{1,0:T(8,128)(2,1)S(1)} %get-tuple-element.36.refs_0_), channel_id=1, source_target_pairs={{0,4},{4,0},{8,12},{12,8},{16,20},{20,16},{24,28},{28,24},{1,5},{5... | collective-permute-start | bytes 1179656 | tf_op jit(solution)/shard_map/ppermute | solution.py:402
  19.0 0.4 collective-permute-start.8
  19.4 0.7 collective-permute-start.1
  20.1 1.3 %collective-permute-start.6 = (bf16[320,768]{1,0:T(8,128)(2,1)}, bf16[320,768]{1,0:T(8,128)(2,1)S(1)}, u32[]{:S(2)}, u32[]{:S(2)}) collective-permute-start(bf16[320,768]{1,0:T(8,128)(2,1)} %collective-permute-done.5), channel_id=1, source_target_pairs={{8,0},{12,4},{16,24},{20,28},{9,1},{13,5},{17,25},{21,29},{10,2},{... | collective-permute-start | bytes 1474568 | tf_op jit(solution)/shard_map/ppermute | solution.py:402
  21.4 1.7 %shard_map.86.refs_2_ = bf16[8,320,768]{2,1,0:T(8,128)(2,1)S(1)} custom-call(bf16[320,768]{1,0:T(8,128)(2,1)S(1)} %get-tuple-element.25.refs_0_, bf16[320,768]{1,0:T(8,128)(2,1)} %collective-permute-done.9.refs_1_), custom_call_target="tpu_custom_call" | custom-call | flops 11500000256 | tf_op jit(solution)/shard_map/pallas_call | solution.py:378
  23.0 6.3 %collective-permute-done.11.refs_1_ = bf16[256,768]{1,0:T(8,128)(2,1)S(1)} collective-permute-done((bf16[256,768]{1,0:T(8,128)(2,1)S(1)}, bf16[256,768]{1,0:T(8,128)(2,1)S(1)}, u32[]{:S(2)}, u32[]{:S(2)}) %collective-permute-start.11) | collective-permute-done | bytes 393248 | tf_op jit(solution)/shard_map/ppermute | solution.py:402
  29.4 0.4 shard_map.88.refs_2_
  29.8 5.9 %collective-permute-done.6 = bf16[320,768]{1,0:T(8,128)(2,1)S(1)} collective-permute-done((bf16[320,768]{1,0:T(8,128)(2,1)}, bf16[320,768]{1,0:T(8,128)(2,1)S(1)}, u32[]{:S(2)}, u32[]{:S(2)}) %collective-permute-start.6) | collective-permute-done | bytes 491552 | tf_op jit(solution)/shard_map/ppermute | solution.py:402
  35.7 0.1 broadcast_select_fusion.refs_0_
  35.8 1.6 %collective-permute-start.7 = (bf16[320,768]{1,0:T(8,128)(2,1)S(1)}, bf16[320,768]{1,0:T(8,128)(2,1)S(1)}, u32[]{:S(2)}, u32[]{:S(2)}) collective-permute-start(bf16[320,768]{1,0:T(8,128)(2,1)S(1)} %broadcast_select_fusion.refs_0_), channel_id=1, source_target_pairs={{0,4},{4,0},{8,12},{12,8},{16,20},{20,16},{24,28},{28,24},{1,5},{5... | collective-permute-start | bytes 1474568 | tf_op jit(solution)/shard_map/ppermute | solution.py:402
  37.3 1.3 %collective-permute-start.2 = (bf16[320,768]{1,0:T(8,128)(2,1)S(1)}, bf16[320,768]{1,0:T(8,128)(2,1)S(1)}, u32[]{:S(2)}, u32[]{:S(2)}) collective-permute-start(bf16[320,768]{1,0:T(8,128)(2,1)S(1)} %collective-permute-done.1), channel_id=1, source_target_pairs={{8,0},{12,4},{16,24},{20,28},{9,1},{13,5},{17,25},{21,29},{10,2},{... | collective-permute-start | bytes 1474568 | tf_op jit(solution)/shard_map/ppermute | solution.py:402
  38.6 1.3 %collective-permute-done.8.refs_1_ = bf16[320,768]{1,0:T(8,128)(2,1)S(1)} collective-permute-done((bf16[320,768]{1,0:T(8,128)(2,1)S(1)}, bf16[320,768]{1,0:T(8,128)(2,1)S(1)}, u32[]{:S(2)}, u32[]{:S(2)}) %collective-permute-start.8) | collective-permute-done | bytes 491552 | tf_op jit(solution)/shard_map/ppermute | solution.py:402
  39.9 0.6 shard_map.87.refs_2_
  40.6 0.1 collective-permute-start.13
  40.6 9.5 %collective-permute-done.2 = bf16[320,768]{1,0:T(8,128)(2,1)S(1)} collective-permute-done((bf16[320,768]{1,0:T(8,128)(2,1)S(1)}, bf16[320,768]{1,0:T(8,128)(2,1)S(1)}, u32[]{:S(2)}, u32[]{:S(2)}) %collective-permute-start.2) | collective-permute-done | bytes 491552 | tf_op jit(solution)/shard_map/ppermute | solution.py:402
  50.3 0.1 collective-permute-start.4
  50.3 0.1 collective-permute-start.18
  50.4 2.8 %collective-permute-start.3 = (bf16[256,768]{1,0:T(8,128)(2,1)S(1)}, bf16[256,768]{1,0:T(8,128)(2,1)S(1)}, u32[]{:S(2)}, u32[]{:S(2)}) collective-permute-start(bf16[256,768]{1,0:T(8,128)(2,1)S(1)} %get-tuple-element.36.refs_0_), channel_id=1, source_target_pairs={{0,16},{4,20},{8,24},{12,28},{16,0},{20,4},{24,8},{28,12},{1,17},{... | collective-permute-start | bytes 1179656 | tf_op jit(solution)/shard_map/ppermute | solution.py:402
  53.2 0.6 shard_map.89.refs_0_.refs_2_
  53.9 6.8 %mid.1 = (bf16[6,512,768]{2,1,0:T(8,128)(2,1)S(1)}, f32[4,256,384]{2,1,0:T(8,128)S(1)}, bf16[4,2048,256]{2,1,0:T(8,128)(2,1)S(1)}) custom-call(bf16[8,320,768]{2,1,0:T(8,128)(2,1)S(1)} %shard_map.89.refs_0_.refs_2_, bf16[4,6,256,128]{3,2,1,0:T(8,128)(2,1)S(1)} %copy-done, bf16[6,64,256]{2,1,0:T(8,128)(2,1)S(1)} %bitcast.3, ...), custom_call_target="tpu_custom_call" | custom-call | flops 2415919104 | tf_op jit(solution)/shard_map/mid/pallas_call | solution.py:528
  60.7 0.6 shard_map.90.refs_0_
  61.4 3.5 %collective-permute-done.18.refs_0_ = bf16[256,768]{1,0:T(8,128)(2,1)S(1)} collective-permute-done((bf16[256,768]{1,0:T(8,128)(2,1)S(1)}, bf16[256,768]{1,0:T(8,128)(2,1)S(1)}, u32[]{:S(2)}, u32[]{:S(2)}) %collective-permute-start.18) | collective-permute-done | bytes 393248 | tf_op jit(solution)/shard_map/ppermute | solution.py:402
  64.9 1.4 %collective-permute-start.19 = (bf16[256,768]{1,0:T(8,128)(2,1)S(1)}, bf16[256,768]{1,0:T(8,128)(2,1)S(1)}, u32[]{:S(2)}, u32[]{:S(2)}) collective-permute-start(bf16[256,768]{1,0:T(8,128)(2,1)S(1)} %collective-permute-done.18.refs_0_), channel_id=1, source_target_pairs={{0,4},{4,0},{8,12},{12,8},{16,20},{20,16},{24,28},{28,24},{1,5},{5... | collective-permute-start | bytes 1179656 | tf_op jit(solution)/shard_map/ppermute | solution.py:402
  66.3 1.5 %sampled.1 = (bf16[2,512,768]{2,1,0:T(8,128)(2,1)S(1)}, f32[4,256,384]{2,1,0:T(8,128)S(1)}) custom-call(bf16[8,320,768]{2,1,0:T(8,128)(2,1)S(1)} %shard_map.90.refs_0_, bf16[4,2048,256]{2,1,0:T(8,128)(2,1)S(1)} %get-tuple-element.33.refs_1_.refs_4_, f32[4,256,384]{2,1,0:T(8,128)S(1)} %get-tuple-element.31.refs_2_), custom_call_target="tpu_custom_call" | custom-call | flops 805306368 | tf_op jit(solution)/shard_map/sampled/pallas_call | solution.py:568
  67.8 6.6 %gram.1.refs_1_ = f32[64,16,128]{2,1,0:T(8,128)S(1)} custom-call(f32[4,256,384]{2,1,0:T(8,128)S(1)} %get-tuple-element.34.refs_0_), custom_call_target="tpu_custom_call" | custom-call | flops 1000000000 | tf_op jit(solution)/shard_map/gram/pallas_call | solution.py:581
  74.4 0.7 collective-permute-start.17
  75.2 1.3 %collective-permute-start.14 = (bf16[256,768]{1,0:T(8,128)(2,1)S(1)}, bf16[256,768]{1,0:T(8,128)(2,1)S(1)}, u32[]{:S(2)}, u32[]{:S(2)}) collective-permute-start(bf16[256,768]{1,0:T(8,128)(2,1)S(1)} %collective-permute-done.3.refs_0_), channel_id=1, source_target_pairs={{8,0},{12,4},{16,24},{20,28},{9,1},{13,5},{17,25},{21,29},{10,2},{... | collective-permute-start | bytes 1179656 | tf_op jit(solution)/shard_map/ppermute | solution.py:402
  76.5 0.9 collective-permute-start.15
  77.3 5.0 %basis.1 = (f32[64,16,128]{2,1,0:T(8,128)S(1)}, bf16[4,256,384]{2,1,0:T(8,128)(2,1)S(1)}) custom-call(f32[4,256,384]{2,1,0:T(8,128)S(1)} %get-tuple-element.34.refs_0_, f32[64,16,128]{2,1,0:T(8,128)S(1)} %gram.1.refs_1_), custom_call_target="tpu_custom_call", output_to_operand_aliasing={{0}: (1, {})} | custom-call | flops 1000000000 | tf_op jit(solution)/shard_map/basis/pallas_call | solution.py:597
  82.4 0.4 shard_map.91.refs_2_
  82.8 3.1 %collective-permute-done.14 = bf16[256,768]{1,0:T(8,128)(2,1)S(1)} collective-permute-done((bf16[256,768]{1,0:T(8,128)(2,1)S(1)}, bf16[256,768]{1,0:T(8,128)(2,1)S(1)}, u32[]{:S(2)}, u32[]{:S(2)}) %collective-permute-start.14) | collective-permute-done | bytes 393248 | tf_op jit(solution)/shard_map/ppermute | solution.py:402
  85.9 0.8 collective-permute-start.16
  86.8 0.4 shard_map.92.refs_2_
  87.2 6.8 %cores.1 = (bf16[6,256,1024]{2,1,0:T(8,128)(2,1)S(1)}, f32[6,256,256]{2,1,0:T(8,128)S(1)}, bf16[4,256,1024]{2,1,0:T(8,128)(2,1)S(1)}) custom-call(s32[1,4]{1,0:T(1,128)S(1)} %bitcast.4, bf16[4,256,384]{2,1,0:T(8,128)(2,1)S(1)} %get-tuple-element.40.refs_1_.refs_2_, bf16[6,512,768]{2,1,0:T(8,128)(2,1)S(1)} %get-tuple-element.41.refs_2_, ...), custom_call_target="tpu_custom_call" | custom-call | flops 2415919104 | bytes 10223616 | tf_op jit(solution)/shard_map/cores/pallas_call | solution.py:606
  94.0 0.4 shard_map.93.refs_1_
  94.4 0.6 copy-done.6
  95.0 3.3 %output.1 = (bf16[4,1,256,256]{3,2,1,0:T(8,128)(2,1)}, bf16[4,6,256,128]{3,2,1,0:T(8,128)(2,1)}) custom-call(s32[1,4]{1,0:T(1,128)S(1)} %bitcast.5, bf16[8,256,768]{2,1,0:T(8,128)(2,1)S(1)} %shard_map.93.refs_1_, bf16[4,256,384]{2,1,0:T(8,128)(2,1)S(1)} %get-tuple-element.40.refs_1_.refs_2_, bf16[6,256,1024]{2,1,0:T(8,128)(2,1)S(1)} %get-tuple-element.43.refs_3_, ...), custom_call_target="tpu_custom_call" | custom-call | flops 805306368 | bytes 3145728 | tf_op jit(solution)/shard_map/output/pallas_call | solution.py:619
  (27 shorter events, 0.2 us)
Async XLA Ops:
  0.6 1.1 %copy-start.2 = (bf16[2,6,256,128]{3,2,1,0:T(8,128)(2,1)S(1)}, bf16[2,6,256,128]{3,2,1,0:T(8,128)(2,1)}, u32[]{:S(2)}) copy-start(bf16[2,6,256,128]{3,2,1,0:T(8,128)(2,1)} %rows_ref.1) | copy-start | bytes 2359300
  1.8 0.9 copy-start.3
  3.0 14.3 %collective-permute-start = (bf16[320,768]{1,0:T(8,128)(2,1)S(1)}, bf16[320,768]{1,0:T(8,128)(2,1)S(1)}, u32[]{:S(2)}, u32[]{:S(2)}) collective-permute-start(bf16[320,768]{1,0:T(8,128)(2,1)S(1)} %get-tuple-element.25.refs_0_), channel_id=1, source_target_pairs={{0,8},{4,12},{8,0},{12,4},{16,24},{20,28},{24,16},{28,20},{1,9},{5... | collective-permute-start | bytes 1474568 | tf_op jit(solution)/shard_map/ppermute | solution.py:402
  6.1 13.3 %collective-permute-start.9 = (bf16[320,768]{1,0:T(8,128)(2,1)S(1)}, bf16[320,768]{1,0:T(8,128)(2,1)}, u32[]{:S(2)}, u32[]{:S(2)}) collective-permute-start(bf16[320,768]{1,0:T(8,128)(2,1)S(1)} %get-tuple-element.25.refs_0_), channel_id=1, source_target_pairs={{0,4},{4,0},{8,12},{12,8},{16,20},{20,16},{24,28},{28,24},{1,5},{5... | collective-permute-start | bytes 1474568 | tf_op jit(solution)/shard_map/ppermute | solution.py:402
  7.6 12.5 %collective-permute-start.5 = (bf16[320,768]{1,0:T(8,128)(2,1)S(1)}, bf16[320,768]{1,0:T(8,128)(2,1)}, u32[]{:S(2)}, u32[]{:S(2)}) collective-permute-start(bf16[320,768]{1,0:T(8,128)(2,1)S(1)} %get-tuple-element.25.refs_0_), channel_id=1, source_target_pairs={{8,16},{16,8},{12,20},{20,12},{9,17},{17,9},{13,21},{21,13},{10,18... | collective-permute-start | bytes 1474568 | tf_op jit(solution)/shard_map/ppermute | solution.py:402
  9.1 1.2 %copy-start.1 = (bf16[4,4,256,128]{3,2,1,0:T(8,128)(2,1)S(1)}, bf16[4,4,256,128]{3,2,1,0:T(8,128)(2,1)}, u32[]{:S(2)}) copy-start(bf16[4,4,256,128]{3,2,1,0:T(8,128)(2,1)} %panel_ref.1) | copy-start | bytes 3145732
  10.3 1.0 %copy-start.5 = (bf16[4,256,256]{2,1,0:T(8,128)(2,1)S(1)}, bf16[4,256,256]{2,1,0:T(8,128)(2,1)}, u32[]{:S(2)}) copy-start(bf16[4,256,256]{2,1,0:T(8,128)(2,1)} %inv_ref.1) | copy-start | bytes 1572868
  11.8 26.8 %collective-permute-start.10 = (bf16[2048,256]{1,0:T(8,128)(2,1)S(1)}, bf16[2048,256]{1,0:T(8,128)(2,1)S(1)}, u32[]{:S(2)}, u32[]{:S(2)}) collective-permute-start(bf16[2048,256]{1,0:T(8,128)(2,1)S(1)} %pack_panel.1.refs_3_), channel_id=1, source_target_pairs={{0,2},{1,3},{2,0},{3,1},{4,6},{5,7},{6,4},{7,5},{8,10},{9,11},{10,... | collective-permute-start | bytes 3145736 | tf_op jit(solution)/shard_map/ppermute | solution.py:486
  17.3 12.1 %collective-permute-start.11 = (bf16[256,768]{1,0:T(8,128)(2,1)S(1)}, bf16[256,768]{1,0:T(8,128)(2,1)S(1)}, u32[]{:S(2)}, u32[]{:S(2)}) collective-permute-start(bf16[256,768]{1,0:T(8,128)(2,1)S(1)} %get-tuple-element.36.refs_0_), channel_id=1, source_target_pairs={{0,4},{4,0},{8,12},{12,8},{16,20},{20,16},{24,28},{28,24},{1,5},{5... | collective-permute-start | bytes 1179656 | tf_op jit(solution)/shard_map/ppermute | solution.py:402
  19.0 20.9 %collective-permute-start.8 = (bf16[320,768]{1,0:T(8,128)(2,1)S(1)}, bf16[320,768]{1,0:T(8,128)(2,1)S(1)}, u32[]{:S(2)}, u32[]{:S(2)}) collective-permute-start(bf16[320,768]{1,0:T(8,128)(2,1)S(1)} %collective-permute-done.refs_0_), channel_id=1, source_target_pairs={{0,4},{4,0},{8,12},{12,8},{16,20},{20,16},{24,28},{28,24},{1,5},{5... | collective-permute-start | bytes 1474568 | tf_op jit(solution)/shard_map/ppermute | solution.py:402
  19.4 17.9 %collective-permute-start.1 = (bf16[320,768]{1,0:T(8,128)(2,1)S(1)}, bf16[320,768]{1,0:T(8,128)(2,1)S(1)}, u32[]{:S(2)}, u32[]{:S(2)}) collective-permute-start(bf16[320,768]{1,0:T(8,128)(2,1)S(1)} %collective-permute-done.refs_0_), channel_id=1, source_target_pairs={{8,16},{16,8},{12,20},{20,12},{9,17},{17,9},{13,21},{21,13},{10,18... | collective-permute-start | bytes 1474568 | tf_op jit(solution)/shard_map/ppermute | solution.py:402
  20.1 15.6 %collective-permute-start.6 = (bf16[320,768]{1,0:T(8,128)(2,1)}, bf16[320,768]{1,0:T(8,128)(2,1)S(1)}, u32[]{:S(2)}, u32[]{:S(2)}) collective-permute-start(bf16[320,768]{1,0:T(8,128)(2,1)} %collective-permute-done.5), channel_id=1, source_target_pairs={{8,0},{12,4},{16,24},{20,28},{9,1},{13,5},{17,25},{21,29},{10,2},{... | collective-permute-start | bytes 1474568 | tf_op jit(solution)/shard_map/ppermute | solution.py:402
  29.4 24.5 %collective-permute-start.12 = (bf16[2048,256]{1,0:T(8,128)(2,1)S(1)}, bf16[2048,256]{1,0:T(8,128)(2,1)S(1)}, u32[]{:S(2)}, u32[]{:S(2)}) collective-permute-start(bf16[2048,256]{1,0:T(8,128)(2,1)S(1)} %pack_panel.1.refs_3_), channel_id=1, source_target_pairs={{0,1},{1,0},{2,3},{3,2},{4,5},{5,4},{6,7},{7,6},{8,9},{9,8},{10,11... | collective-permute-start | bytes 3145736 | tf_op jit(solution)/shard_map/ppermute | solution.py:487
  35.8 14.7 %collective-permute-start.7 = (bf16[320,768]{1,0:T(8,128)(2,1)S(1)}, bf16[320,768]{1,0:T(8,128)(2,1)S(1)}, u32[]{:S(2)}, u32[]{:S(2)}) collective-permute-start(bf16[320,768]{1,0:T(8,128)(2,1)S(1)} %broadcast_select_fusion.refs_0_), channel_id=1, source_target_pairs={{0,4},{4,0},{8,12},{12,8},{16,20},{20,16},{24,28},{28,24},{1,5},{5... | collective-permute-start | bytes 1474568 | tf_op jit(solution)/shard_map/ppermute | solution.py:402
  37.3 12.9 %collective-permute-start.2 = (bf16[320,768]{1,0:T(8,128)(2,1)S(1)}, bf16[320,768]{1,0:T(8,128)(2,1)S(1)}, u32[]{:S(2)}, u32[]{:S(2)}) collective-permute-start(bf16[320,768]{1,0:T(8,128)(2,1)S(1)} %collective-permute-done.1), channel_id=1, source_target_pairs={{8,0},{12,4},{16,24},{20,28},{9,1},{13,5},{17,25},{21,29},{10,2},{... | collective-permute-start | bytes 1474568 | tf_op jit(solution)/shard_map/ppermute | solution.py:402
  40.6 13.3 %collective-permute-start.13 = (bf16[2048,256]{1,0:T(8,128)(2,1)S(1)}, bf16[2048,256]{1,0:T(8,128)(2,1)S(1)}, u32[]{:S(2)}, u32[]{:S(2)}) collective-permute-start(bf16[2048,256]{1,0:T(8,128)(2,1)S(1)} %collective-permute-done.10.refs_5_), channel_id=1, source_target_pairs={{0,1},{1,0},{2,3},{3,2},{4,5},{5,4},{6,7},{7,6},{8,9},{9,8},{10,11... | collective-permute-start | bytes 3145736 | tf_op jit(solution)/shard_map/ppermute | solution.py:488
  50.2 3.6 %copy-start = (bf16[4,6,256,128]{3,2,1,0:T(8,128)(2,1)S(1)}, bf16[4,6,256,128]{3,2,1,0:T(8,128)(2,1)}, u32[]{:S(2)}) copy-start(bf16[4,6,256,128]{3,2,1,0:T(8,128)(2,1)} %refs_5_.1) | copy-start | bytes 4718596
  50.3 3.6 %copy-start.4 = (bf16[6,256,64]{1,2,0:T(8,128)(2,1)S(1)}, bf16[6,256,64]{1,2,0:T(8,128)(2,1)}, u32[]{:S(2)}) copy-start(bf16[6,256,64]{1,2,0:T(8,128)(2,1)} %param.13) | copy-start | bytes 589828
  50.3 10.5 %collective-permute-start.4 = (bf16[320,768]{1,0:T(8,128)(2,1)S(1)}, bf16[320,768]{1,0:T(8,128)(2,1)S(1)}, u32[]{:S(2)}, u32[]{:S(2)}) collective-permute-start(bf16[320,768]{1,0:T(8,128)(2,1)S(1)} %broadcast_select_fusion.1.refs_0_), channel_id=1, source_target_pairs={{0,4},{4,0},{8,12},{12,8},{16,20},{20,16},{24,28},{28,24},{1,5},{5... | collective-permute-start | bytes 1474568 | tf_op jit(solution)/shard_map/ppermute | solution.py:402
  50.3 14.6 %collective-permute-start.18 = (bf16[256,768]{1,0:T(8,128)(2,1)S(1)}, bf16[256,768]{1,0:T(8,128)(2,1)S(1)}, u32[]{:S(2)}, u32[]{:S(2)}) collective-permute-start(bf16[256,768]{1,0:T(8,128)(2,1)S(1)} %get-tuple-element.36.refs_0_), channel_id=1, source_target_pairs={{0,8},{4,12},{8,0},{12,4},{16,24},{20,28},{24,16},{28,20},{1,9},{5... | collective-permute-start | bytes 1179656 | tf_op jit(solution)/shard_map/ppermute | solution.py:402
  50.4 24.0 %collective-permute-start.3 = (bf16[256,768]{1,0:T(8,128)(2,1)S(1)}, bf16[256,768]{1,0:T(8,128)(2,1)S(1)}, u32[]{:S(2)}, u32[]{:S(2)}) collective-permute-start(bf16[256,768]{1,0:T(8,128)(2,1)S(1)} %get-tuple-element.36.refs_0_), channel_id=1, source_target_pairs={{0,16},{4,20},{8,24},{12,28},{16,0},{20,4},{24,8},{28,12},{1,17},{... | collective-permute-start | bytes 1179656 | tf_op jit(solution)/shard_map/ppermute | solution.py:402
  64.9 17.4 %collective-permute-start.19 = (bf16[256,768]{1,0:T(8,128)(2,1)S(1)}, bf16[256,768]{1,0:T(8,128)(2,1)S(1)}, u32[]{:S(2)}, u32[]{:S(2)}) collective-permute-start(bf16[256,768]{1,0:T(8,128)(2,1)S(1)} %collective-permute-done.18.refs_0_), channel_id=1, source_target_pairs={{0,4},{4,0},{8,12},{12,8},{16,20},{20,16},{24,28},{28,24},{1,5},{5... | collective-permute-start | bytes 1179656 | tf_op jit(solution)/shard_map/ppermute | solution.py:402
  74.4 12.3 %collective-permute-start.17 = (bf16[256,768]{1,0:T(8,128)(2,1)S(1)}, bf16[256,768]{1,0:T(8,128)(2,1)S(1)}, u32[]{:S(2)}, u32[]{:S(2)}) collective-permute-start(bf16[256,768]{1,0:T(8,128)(2,1)S(1)} %collective-permute-done.3.refs_0_), channel_id=1, source_target_pairs={{0,4},{4,0},{8,12},{12,8},{16,20},{20,16},{24,28},{28,24},{1,5},{5... | collective-permute-start | bytes 1179656 | tf_op jit(solution)/shard_map/ppermute | solution.py:402
  75.2 10.7 %collective-permute-start.14 = (bf16[256,768]{1,0:T(8,128)(2,1)S(1)}, bf16[256,768]{1,0:T(8,128)(2,1)S(1)}, u32[]{:S(2)}, u32[]{:S(2)}) collective-permute-start(bf16[256,768]{1,0:T(8,128)(2,1)S(1)} %collective-permute-done.3.refs_0_), channel_id=1, source_target_pairs={{8,0},{12,4},{16,24},{20,28},{9,1},{13,5},{17,25},{21,29},{10,2},{... | collective-permute-start | bytes 1179656 | tf_op jit(solution)/shard_map/ppermute | solution.py:402
  76.5 6.3 %collective-permute-start.15 = (bf16[256,768]{1,0:T(8,128)(2,1)S(1)}, bf16[256,768]{1,0:T(8,128)(2,1)S(1)}, u32[]{:S(2)}, u32[]{:S(2)}) collective-permute-start(bf16[256,768]{1,0:T(8,128)(2,1)S(1)} %get-tuple-element.36.refs_0_), channel_id=1, source_target_pairs={{8,16},{16,8},{12,20},{20,12},{9,17},{17,9},{13,21},{21,13},{10,18... | collective-permute-start | bytes 1179656 | tf_op jit(solution)/shard_map/ppermute | solution.py:402
  85.9 1.2 %copy-start.7 = (s32[4,1]{0,1:T(1,128)S(1)}, s32[4,1]{0,1:T(1,128)}, u32[]{:S(2)}) copy-start(s32[4,1]{0,1:T(1,128)} %param.12) | copy-start | bytes 52
  85.9 8.0 %collective-permute-start.16 = (bf16[256,768]{1,0:T(8,128)(2,1)S(1)}, bf16[256,768]{1,0:T(8,128)(2,1)S(1)}, u32[]{:S(2)}, u32[]{:S(2)}) collective-permute-start(bf16[256,768]{1,0:T(8,128)(2,1)S(1)} %broadcast_select_fusion.2.refs_0_), channel_id=1, source_target_pairs={{0,4},{4,0},{8,12},{12,8},{16,20},{20,16},{24,28},{28,24},{1,5},{5... | collective-permute-start | bytes 1179656 | tf_op jit(solution)/shard_map/ppermute | solution.py:402
  93.9 1.0 %copy-start.6 = (bf16[4,1,256,256]{3,2,1,0:T(8,128)(2,1)S(1)}, bf16[4,1,256,256]{3,2,1,0:T(8,128)(2,1)}, u32[]{:S(2)}) copy-start(bf16[4,1,256,256]{3,2,1,0:T(8,128)(2,1)} %refs_6_.1) | copy-start | bytes 1572868

commit v5 on v4

--- a/solution.py
+++ b/solution.py
@@ -14,8 +14,11 @@
 TN = (((0,), (0,)), ((), ()))
 PLACE_VMEM = 1024 * 1024
 PLACE_P = 10
-PLACE_Q = 8
+PLACE_Q = 1
 PLACE_Q0 = 1
+PLACE_Q1 = 10
+B_AT = "third"
+TIE_B = 0
 MID_SCALE = 1
 SAMPLED_SCALE = 1
 BLOCKS = 3
@@ -26,6 +29,10 @@
 TIE_Y = 1
 TIE_GRAM = 0
 BASIS_FLOPS = int(1e9)
+PROJECT_FLOPS = int(1e9)
+CORES_FLOPS = int(1e9)
+MOST_FLOPS = int(1e9)
+TIE_CORES = 1
 FORWARD_AT = "gram"
 NEAR_AT = "pb"
 GATE_ALONG = "third"
@@ -121,13 +128,13 @@
     return copies
 
 
-def mid_pair(n_rows, t, pb_all, panel_ref, mid_ref, slot, weight_ref):
+def mid_pair(n_rows, t, blocks, panel_ref, mid_ref, slot, weight_ref):
     _, tall, wide = mid_ref.shape
     count = weight_ref.shape[0]
     width = tall // count
     half = width // 2
     columns = wide // width
-    size = pb_all.shape[1] - half
+    size = blocks[0].shape[0] - half
     row_half = lax.broadcasted_iota(jnp.int32, (tall, 2 * width), 0) // half % 2
     lane_half = lax.broadcasted_iota(jnp.int32, (tall, 2 * width), 1) // half % 2
     same = row_half == lane_half
@@ -139,10 +146,10 @@
         left = panel_ref[plane, pl.ds(pl.multiple_of(part * tall, tall), tall), :]
         for j in range(0, columns, 2):
             lanes = pl.ds(j * width, 2 * width)
-            mid = dot(left, pb_all[t + m, :size, lanes])
+            mid = dot(left, blocks[m][:size, lanes])
             mid = jnp.where(same, mid, 0.0).astype(BF16)
             mid_ref[slot + m, :, lanes] = mid
-            b_pair = pb_all[t + m, size:, lanes]
+            b_pair = blocks[m][size:, lanes]
             right = jnp.concatenate(
                 [
                     jnp.concatenate([b_pair[:, :width], zero], axis=1),
@@ -174,15 +181,16 @@
         copy.wait()
 
     def step(s, carry):
-        plane = mid_pair(n_rows, 2 * s, pb_all, panel_ref, mid_ref, 2 * s, weight)
+        blocks = pb_all.at[2 * s], pb_all.at[2 * s + 1]
+        plane = mid_pair(n_rows, 2 * s, blocks, panel_ref, mid_ref, 2 * s, weight)
         subtract(total_ref, panel_ref, plane, weight)
         return carry
 
     lax.fori_loop(0, n_rows // 2 - 1, step, 0)
 
 
-def sampled_kernel(n_rows, pb_all, panel_ref, total_ref, mid_ref, sampled_ref, weight):
-    plane = mid_pair(n_rows, n_rows - 2, pb_all, panel_ref, mid_ref, 0, weight)
+def sampled_kernel(n_rows, first_ref, second_ref, panel_ref, total_ref, mid_ref, sampled_ref, weight):
+    plane = mid_pair(n_rows, n_rows - 2, (first_ref, second_ref), panel_ref, mid_ref, 0, weight)
     sampled_ref[...] = total_ref[...]
     subtract(sampled_ref, panel_ref, plane, weight)
 
@@ -261,24 +269,21 @@
     lax.fori_loop(first_block, last_block, one_block, 0)
 
 
-def cores_kernel(
-    n_rows, near_ref, basis_ref, early_ref, late_ref, panel_ref, target_ref, left_ref, value_ref, near_left_ref, cores
-):
-    count, size, wide = basis_ref.shape
+def project_kernel(basis_ref, panel_ref, target_ref, cores_ref, value_ref):
+    count, size, _ = basis_ref.shape
     columns, width = target_ref.shape[1], target_ref.shape[3]
     half = width // 2
-    n_cols, _, deep = panel_ref.shape
-    per_col = deep // width
-    base = per_col * count * width
+    n_cols, rows, deep = panel_ref.shape
+    base = rows - count * size
     first = halves((half, width), half)
     zero = jnp.zeros((half, width), BF16)
-    tall = count * width
     turned = []
     for i in range(count):
         basis_t = jnp.transpose(basis_ref[i])
         turned.append(basis_t)
         for c in range(n_cols):
-            cores[i, :, pl.ds(c * deep, deep)] = dot(basis_t, panel_ref[c, pl.ds(base + i * size, size), :]).astype(BF16)
+            product = dot(basis_t, panel_ref[c, pl.ds(base + i * size, size), :])
+            cores_ref[i, :, pl.ds(c * deep, deep)] = product.astype(BF16)
     for i in range(0, count, 2):
         for j in range(columns):
             core = []
@@ -291,6 +296,16 @@
             )
             value_ref[j, :, pl.ds(i * half, width)] = dot(left, right, NT)
 
+
+def cores_kernel(n_rows, near_ref, cores_ref, early_ref, late_ref, panel_ref, left_ref, near_left_ref):
+    count, wide, _ = cores_ref.shape
+    columns = left_ref.shape[0]
+    half = wide // columns
+    width = 2 * half
+    n_cols, rows, deep = panel_ref.shape
+    size = near_left_ref.shape[1]
+    per_col = deep // width
+    base = rows - count * size
     owner = arrivals(n_rows)
     me = lax.axis_index("rows")
 
@@ -301,7 +316,7 @@
         for i in range(count):
             for j in range(columns):
                 product = dot(
-                    cores[i, pl.ds(j * half, half), from_lanes],
+                    cores_ref[i, pl.ds(j * half, half), from_lanes],
                     mid_ref[slot, pl.ds(i * width, width), pl.ds(j * width, width)],
                 )
                 left_ref[j, pl.ds(i * half, half), lanes] = product.astype(BF16)
@@ -320,15 +335,54 @@
         one_pair(n_rows - 2 + m, late_ref, m)
 
 
-def output_kernel(n_rows, near_ref, q_all, *refs):
-    basis_ref, left_ref, value_ref, near_left_ref, near_block_ref, near_out_ref, far_out_ref = refs
+def last_slot(n_rows):
+    if n_rows != 8:
+        return n_rows - 2
+    me = lax.axis_index("rows")
+    return jnp.where((me < 2) | (me > 5), 6, 4)
+
+
+def most_slots(n_rows):
+    return [*range(0, n_rows - 4, 2), 2 * n_rows - 6 - last_slot(n_rows)]
+
+
+def joined(q_ref, slots, lanes):
+    return jnp.concatenate([q_ref[slot + m, :, lanes] for slot in slots for m in range(2)], axis=1)
+
+
+def lanes_of(slot, width):
+    return pl.ds(pl.multiple_of(slot * width, width), 2 * width)
+
+
+def most_kernel(n_rows, near_ref, q_ref, left_ref, value_ref, near_left_ref, near_block_ref, far_ref, near_sum_ref):
+    columns = left_ref.shape[0]
+    count = near_left_ref.shape[0]
+    width = q_ref.shape[2] // columns
+    slots = most_slots(n_rows)
+    for j in range(columns):
+        right = jnp.concatenate([left_ref[j, :, lanes_of(slot, width)] for slot in slots], axis=1)
+        far_ref[j] = value_ref[j] - dot(joined(q_ref, slots, pl.ds(j * width, width)), right, NT)
+    for i in range(count):
+        near = pl.ds(pl.multiple_of(near_ref[0, i] * width, width), width)
+        left = jnp.concatenate([near_left_ref[i, :, lanes_of(slot, width)] for slot in slots], axis=1)
+        near_sum_ref[i] = near_block_ref[i, 0].astype(F32) - dot(left, joined(q_ref, slots, near), NT)
+
+
+def output_kernel(
+    n_rows, near_ref, own_ref, other_ref, basis_ref, left_ref, far_ref, near_left_ref, near_sum_ref, near_out_ref, far_out_ref
+):
     count, columns, size, width = far_out_ref.shape
     half = width // 2
     root_size = math.sqrt(size)
     first = halves((size, width), half)
+    lanes = lanes_of(last_slot(n_rows), width)
+
+    def q_at(columns_at):
+        return jnp.concatenate([ref[:, columns_at] for ref in (own_ref, other_ref)], axis=1)
+
     for j in range(columns):
-        right = jnp.concatenate([q_all[o, :, pl.ds(j * width, width)] for o in range(n_rows)], axis=1)
-        weights = (value_ref[j] - dot(right, left_ref[j], NT)) / root_size
+        q_last = q_at(pl.ds(j * width, width))
+        weights = (far_ref[j] - dot(q_last, left_ref[j, :, lanes], NT)) / root_size
         for i in range(count):
             tile = weights[:, i // 2 * width : (i // 2 + 1) * width]
             if i % 2 == 0:
@@ -337,15 +391,11 @@
             if j % 2 == 1:
                 basis = swap(basis, half)
             block = jnp.where(first, basis, tile.astype(BF16))
-            is_near = near_ref[0, i] == j
-            for s in range(1, near_ref.shape[0]):
-                is_near = jnp.logical_or(is_near, near_ref[s, i] == j)
-            far_out_ref[i, j] = jnp.where(is_near, jnp.zeros_like(block), block)
+            far_out_ref[i, j] = jnp.where(near_ref[0, i] == j, jnp.zeros_like(block), block)
     for i in range(count):
         near = pl.ds(pl.multiple_of(near_ref[0, i] * width, width), width)
-        right = jnp.concatenate([q_all[o, :, near] for o in range(n_rows)], axis=1)
-        update = dot(near_left_ref[i], right, NT)
-        near_out_ref[i, 0] = (near_block_ref[i, 0].astype(F32) - update).astype(BF16)
+        update = dot(near_left_ref[i, :, lanes], q_at(near), NT)
+        near_out_ref[i, 0] = (near_sum_ref[i] - update).astype(BF16)
 
 
 def arrivals(n):
@@ -437,6 +487,12 @@
         self.whole = place(whole, self.slots[stage], pair, self.n, self.micros)
         return self.whole
 
+    def last(self):
+        return self.third, self.x_third
+
+    def last_but_one(self):
+        return self.x_second
+
 
 class DirectGather(Gather):
     slots = [0, 2, lambda me: jnp.where((me < 2) | (me > 5), 4, 6), lambda me: jnp.where((me < 2) | (me > 5), 6, 4)]
@@ -450,9 +506,11 @@
 
     def forward(self, *events):
         out = self.send(held(self.second, *events), self.outward)
-        middle = self.send(held(self.block, self.second, *events), self.inner)
         self.x_second = self.flip(held(self.second, *events), 1)
-        self.third = jnp.where(self.is_end, out, middle)
+        self.third = jnp.where(self.is_end, out, self.middle)
+
+    def cross_middle(self, *events):
+        self.middle = self.send(held(self.block, *events), self.inner)
 
 
 class PlainGather:
@@ -463,7 +521,13 @@
     def start_across(self, *events):
         pass
 
-    start_along = forward = forward_again = finish = exchange_near = start_across
+    start_along = forward = forward_again = finish = exchange_near = cross_middle = start_across
+
+    def last_but_one(self):
+        return self.block
+
+    def last(self):
+        return self.put(0)[-2], self.whole[-1]
 
     def put(self, stage, *events):
         if self.whole is None:
@@ -553,29 +617,43 @@
     pb_way.put(1, q_first if TIE0 == 1 else None, panels[2] if TIE_Y == 1 else None)
     arrived = pb_way.put(2, q_first if TIE0 == 2 else None)
     q_way.micros = PLACE_Q
+    if B_AT == "near":
+        q_way.cross_middle(pb_way.near, pb_way.mid)
+    if B_AT == "far":
+        q_way.cross_middle(pb_way.far)
+    if B_AT == "second":
+        q_way.cross_middle(pb_way.second)
+    if B_AT == "third":
+        q_way.cross_middle(pb_way.third)
+    if B_AT == "pb":
+        q_way.cross_middle(pb_way.x_third if n_rows == 8 else None)
+    if n_rows == 8 and TIE_B:
+        arrived = held(arrived, q_way.middle)
     mid_early, total, panel_whole = mids(arrived, held(target_factors, pb_way.far))
+    if GATE_ALONG == "both":
+        q_way.start_along(pb_way.third, pb_way.last_but_one())
     if GATE_ALONG == "third":
         q_way.start_along(pb_way.third)
     if GATE_ALONG == "mid":
         q_way.start_along(total)
     if GATE_ALONG == "far":
         q_way.start_along(pb_way.far)
-    pb_all = pb_way.put(3, total)
+    pb_done = pb_way.last()[1]
     if TIE0 == 3:
-        q_way.start_across(pb_all)
+        q_way.start_across(pb_done)
         q_way.put(0)
     with jax.named_scope("sampled"):
         mid_late, sampled = call(
             lambda *refs: sampled_kernel(n_rows, *refs),
             (shape((2,) + mid_early.shape[1:], BF16), shape((count, size, wide), F32)),
-            [IN_VMEM] * 3,
+            [IN_VMEM] * 4,
             [weight_scratch],
             flops=mid_flops * 2 * SAMPLED_SCALE,
-        )(pb_all, panel_whole, total)
+        )(*pb_way.last(), panel_whole, total)
     if NEAR_AT != "gram":
-        q_way.exchange_near({"pb": pb_all, "sampled": sampled}[NEAR_AT])
+        q_way.exchange_near({"pb": pb_done, "sampled": sampled}[NEAR_AT])
     if FORWARD_AT == "pb":
-        q_way.forward(pb_all)
+        q_way.forward(pb_done)
     state_shape = shape((half, -(-count * columns // 2 // 8) * 8, width), F32)
     with jax.named_scope("gram"):
         state = call(
@@ -588,11 +666,10 @@
         q_way.exchange_near(state)
     if FORWARD_AT == "gram":
         q_way.forward(state)
-    q_way.finish()
-    q_second = q_way.put(1)
-    q_way.put(2)
-    q_all = q_way.put(3)
-    state = held(state, {"near": q_way.near, "none": None, "second": q_way.second}[BETWEEN])
+    q_way.micros = PLACE_Q1
+    q_near = q_way.put(1)
+    q_way.micros = PLACE_Q
+    state = held(state, *{"near": [q_way.near], "none": [], "second": [q_way.second], "put": [q_near, q_way.second]}[BETWEEN])
     with jax.named_scope("basis"):
         _, basis = call(
             lambda *refs: basis_kernel(BLOCKS, *refs),
@@ -601,28 +678,36 @@
             flops=BASIS_FLOPS,
             aliases={1: 0},
         )(sampled, state)
-    basis = held(basis, q_second if TIE1 == "cores" else None)
+    q_most = q_way.put(2)
+    with jax.named_scope("project"):
+        cores, value = call(
+            project_kernel,
+            (shape((count, wide, deep), BF16), shape((columns, size, count * half), F32)),
+            [IN_VMEM] * 3,
+            flops=PROJECT_FLOPS,
+        )(held(basis, q_near if TIE1 == "near" else None), panel_whole, target_factors)
     with jax.named_scope("cores"):
-        left, value, near_left = call(
+        left, near_left = call(
             lambda *refs: cores_kernel(n_rows, *refs),
-            (
-                shape((columns, count * half, deep), BF16),
-                shape((columns, size, count * half), F32),
-                shape((count, size, deep), BF16),
-            ),
+            (shape((columns, count * half, deep), BF16), shape((count, size, deep), BF16)),
+            [IN_SMEM] + [IN_VMEM] * 4,
+            flops=CORES_FLOPS,
+        )(near_t, held(cores, q_way.third if TIE_CORES else None), mid_early, mid_late, panel_whole)
+    with jax.named_scope("most"):
+        far_sum, near_sum = call(
+            lambda *refs: most_kernel(n_rows, *refs),
+            (shape((columns, size, count * half), F32), shape((count, size, size), F32)),
             [IN_SMEM] + [IN_VMEM] * 5,
-            [vmem((count, wide, deep), BF16)],
-            flops=3 * n_rows * count * width * size * columns * width * CORES_SCALE,
-            moved=2 * n_rows * (pb.size + count * width * columns * width),
-        )(near_t, basis, mid_early, mid_late, panel_whole, target_factors)
+            flops=MOST_FLOPS,
+        )(near_t, q_most, left, value, near_left, near_blocks)
+    q_way.finish()
     with jax.named_scope("output"):
         near_new, far_new = call(
             lambda *refs: output_kernel(n_rows, *refs),
             (shape(near_blocks.shape, BF16), shape(target_factors.shape, BF16)),
-            [IN_SMEM] + [IN_VMEM] * 6,
+            [IN_SMEM] + [IN_VMEM] * 7,
             flops=2 * columns * size * deep * count * half,
-            moved=2 * n_rows * q.size,
-        )(near_t, q_all, basis, left, value, near_left, near_blocks)
+        )(near_t, *q_way.last(), basis, left, far_sum, near_left, near_sum)
     return near_new, far_new
 
 

time: 100 us -> 98.6 us (0.986)
  waiting for transfers between devices: 33.6 us -> 32.2 us
    pallas_call x0 -> x2, Pallas kernels: none -> 4.67 us  [the longest x1 2.81 us: per_device(): call(project_kernel, (shape((count, wide, deep), BF16), shape((columns, s...]
    pallas_call x1, Pallas kernels: 6.76 us -> 3.95 us  [per_device(): call(lambda *refs: cores_kernel(n_rows, *refs), (shape((columns, count *...]
    ppermute x17, waiting for transfers between devices: 33.6 us -> 32.2 us  [send(): return lax.ppermute(value, 'rows', pairs)]
    pallas_call x8 -> x6, Pallas kernels: 5.19 us -> 4.12 us  [place(): pl.pallas_call(kernel, out_shape=jax.ShapeDtypeStruct((n,) + blocks[0].sh...]
  transfers between devices with their start and end apart: 20 -> 20, of which waited for: 7 -> 8; matrix products, arithmetic and copies ran while one was open for 0% -> 0% of each run, Pallas kernels for 33% -> 34%
where the time goes in v5:
time: 98.6 us; the launch traced here: 97.2 us
  Pallas kernels  36.2 us (37%)
  waiting for transfers between devices  32.2 us (33%)
  starting transfers between devices  23.4 us (24%)
  local copies, waits for them, and re-layouts  4.34 us (4%)
    ppermute x17, waiting for transfers between devices, send(): return lax.ppermute(value, 'rows', pairs)  32.2 us
    ppermute x17, starting transfers between devices, send(): return lax.ppermute(value, 'rows', pairs)  21.7 us
    pallas_call x1, Pallas kernels, mids(): call(lambda *refs: mid_kernel(n_rows, n_cols, *refs), (shape((n_rows - 2,...  6.79 us
    pallas_call x1, Pallas kernels, per_device(): call(lambda *refs: gram_kernel(BLOCKS, *refs), state_shape, [IN_VMEM], fl...  6.65 us
    pallas_call x1, Pallas kernels, per_device(): call(lambda *refs: basis_kernel(BLOCKS, *refs), (state_shape, shape((coun...  5.02 us
    unnamed x16, local copies, waits for them, and re-layouts  4.34 us
    pallas_call x6, Pallas kernels, place(): pl.pallas_call(kernel, out_shape=jax.ShapeDtypeStruct((n,) + blocks[0].sh...  4.12 us
    pallas_call x1, Pallas kernels, per_device(): call(lambda *refs: cores_kernel(n_rows, *refs), (shape((columns, count *...  3.95 us
  transfers between devices with their start and end apart: 20, of which 8 were waited for; matrix products, arithmetic and copies ran while one was open for 0% of the time, Pallas kernels for 34%

profile of v5, /device:TPU:0, one launch (start us, length us, event | category | flops | bytes accessed | tf_op | source)
XLA Modules:
  0.0 97.2 jit_solution(11800813656774692517)
XLA Ops:
  0.6 1.1 %copy-done.2 = bf16[2,6,256,128]{3,2,1,0:T(8,128)(2,1)S(1)} copy-done((bf16[2,6,256,128]{3,2,1,0:T(8,128)(2,1)S(1)}, bf16[2,6,256,128]{3,2,1,0:T(8,128)(2,1)}, u32[]{:S(2)}) %copy-start.2) | copy-done | bytes 786456
  1.8 0.9 copy-done.3
  2.7 0.3 pack_rows.1
  3.0 3.1 %collective-permute-start = (bf16[320,768]{1,0:T(8,128)(2,1)S(1)}, bf16[320,768]{1,0:T(8,128)(2,1)S(1)}, u32[]{:S(2)}, u32[]{:S(2)}) collective-permute-start(bf16[320,768]{1,0:T(8,128)(2,1)S(1)} %get-tuple-element.26.refs_0_), channel_id=1, source_target_pairs={{0,8},{4,12},{8,0},{12,4},{16,24},{20,28},{24,16},{28,20},{1,9},{5... | collective-permute-start | bytes 1474568 | tf_op jit(solution)/shard_map/ppermute | solution.py:452
  6.1 1.5 %collective-permute-start.9 = (bf16[320,768]{1,0:T(8,128)(2,1)S(1)}, bf16[320,768]{1,0:T(8,128)(2,1)}, u32[]{:S(2)}, u32[]{:S(2)}) collective-permute-start(bf16[320,768]{1,0:T(8,128)(2,1)S(1)} %get-tuple-element.26.refs_0_), channel_id=1, source_target_pairs={{0,4},{4,0},{8,12},{12,8},{16,20},{20,16},{24,28},{28,24},{1,5},{5... | collective-permute-start | bytes 1474568 | tf_op jit(solution)/shard_map/ppermute | solution.py:452
  7.6 1.4 %collective-permute-start.5 = (bf16[320,768]{1,0:T(8,128)(2,1)S(1)}, bf16[320,768]{1,0:T(8,128)(2,1)}, u32[]{:S(2)}, u32[]{:S(2)}) collective-permute-start(bf16[320,768]{1,0:T(8,128)(2,1)S(1)} %get-tuple-element.26.refs_0_), channel_id=1, source_target_pairs={{8,16},{16,8},{12,20},{20,12},{9,17},{17,9},{13,21},{21,13},{10,18... | collective-permute-start | bytes 1474568 | tf_op jit(solution)/shard_map/ppermute | solution.py:452
  9.0 1.2 %copy-done.1 = bf16[4,4,256,128]{3,2,1,0:T(8,128)(2,1)S(1)} copy-done((bf16[4,4,256,128]{3,2,1,0:T(8,128)(2,1)S(1)}, bf16[4,4,256,128]{3,2,1,0:T(8,128)(2,1)}, u32[]{:S(2)}) %copy-start.1) | copy-done | bytes 1048600
  10.3 1.0 %copy-done.5 = bf16[4,256,256]{2,1,0:T(8,128)(2,1)S(1)} copy-done((bf16[4,256,256]{2,1,0:T(8,128)(2,1)S(1)}, bf16[4,256,256]{2,1,0:T(8,128)(2,1)}, u32[]{:S(2)}) %copy-start.5) | copy-done | bytes 524312
  11.3 0.5 pack_panel.1.refs_3_
  11.8 1.6 %collective-permute-start.10 = (bf16[2048,256]{1,0:T(8,128)(2,1)S(1)}, bf16[2048,256]{1,0:T(8,128)(2,1)S(1)}, u32[]{:S(2)}, u32[]{:S(2)}) collective-permute-start(bf16[2048,256]{1,0:T(8,128)(2,1)S(1)} %pack_panel.1.refs_3_), channel_id=1, source_target_pairs={{0,2},{1,3},{2,0},{3,1},{4,6},{5,7},{6,4},{7,5},{8,10},{9,11},{10,... | collective-permute-start | bytes 3145736 | tf_op jit(solution)/shard_map/ppermute | solution.py:550
  13.4 4.0 %collective-permute-done.refs_0_ = bf16[320,768]{1,0:T(8,128)(2,1)S(1)} collective-permute-done((bf16[320,768]{1,0:T(8,128)(2,1)S(1)}, bf16[320,768]{1,0:T(8,128)(2,1)S(1)}, u32[]{:S(2)}, u32[]{:S(2)}) %collective-permute-start) | collective-permute-done | bytes 491552 | tf_op jit(solution)/shard_map/ppermute | solution.py:452
  17.3 1.7 %collective-permute-start.11 = (bf16[256,768]{1,0:T(8,128)(2,1)S(1)}, bf16[256,768]{1,0:T(8,128)(2,1)S(1)}, u32[]{:S(2)}, u32[]{:S(2)}) collective-permute-start(bf16[256,768]{1,0:T(8,128)(2,1)S(1)} %get-tuple-element.29.refs_0_), channel_id=1, source_target_pairs={{0,4},{4,0},{8,12},{12,8},{16,20},{20,16},{24,28},{28,24},{1,5},{5... | collective-permute-start | bytes 1179656 | tf_op jit(solution)/shard_map/ppermute | solution.py:452
  19.0 0.4 collective-permute-start.8
  19.4 0.7 collective-permute-start.1
  20.1 1.3 %collective-permute-start.6 = (bf16[320,768]{1,0:T(8,128)(2,1)}, bf16[320,768]{1,0:T(8,128)(2,1)S(1)}, u32[]{:S(2)}, u32[]{:S(2)}) collective-permute-start(bf16[320,768]{1,0:T(8,128)(2,1)} %collective-permute-done.5), channel_id=1, source_target_pairs={{8,0},{12,4},{16,24},{20,28},{9,1},{13,5},{17,25},{21,29},{10,2},{... | collective-permute-start | bytes 1474568 | tf_op jit(solution)/shard_map/ppermute | solution.py:452
  21.4 1.7 %shard_map.86.refs_2_ = bf16[8,320,768]{2,1,0:T(8,128)(2,1)S(1)} custom-call(bf16[320,768]{1,0:T(8,128)(2,1)S(1)} %get-tuple-element.26.refs_0_, bf16[320,768]{1,0:T(8,128)(2,1)} %collective-permute-done.9.refs_1_), custom_call_target="tpu_custom_call" | custom-call | flops 11500000256 | tf_op jit(solution)/shard_map/pallas_call | solution.py:428
  23.0 6.3 %collective-permute-done.11.refs_1_ = bf16[256,768]{1,0:T(8,128)(2,1)S(1)} collective-permute-done((bf16[256,768]{1,0:T(8,128)(2,1)S(1)}, bf16[256,768]{1,0:T(8,128)(2,1)S(1)}, u32[]{:S(2)}, u32[]{:S(2)}) %collective-permute-start.11) | collective-permute-done | bytes 393248 | tf_op jit(solution)/shard_map/ppermute | solution.py:452
  29.4 0.4 shard_map.88.refs_2_
  29.8 5.9 %collective-permute-done.6 = bf16[320,768]{1,0:T(8,128)(2,1)S(1)} collective-permute-done((bf16[320,768]{1,0:T(8,128)(2,1)}, bf16[320,768]{1,0:T(8,128)(2,1)S(1)}, u32[]{:S(2)}, u32[]{:S(2)}) %collective-permute-start.6) | collective-permute-done | bytes 491552 | tf_op jit(solution)/shard_map/ppermute | solution.py:452
  35.7 0.1 broadcast_select_fusion.refs_0_
  35.8 1.6 %collective-permute-start.7 = (bf16[320,768]{1,0:T(8,128)(2,1)S(1)}, bf16[320,768]{1,0:T(8,128)(2,1)S(1)}, u32[]{:S(2)}, u32[]{:S(2)}) collective-permute-start(bf16[320,768]{1,0:T(8,128)(2,1)S(1)} %broadcast_select_fusion.refs_0_), channel_id=1, source_target_pairs={{0,4},{4,0},{8,12},{12,8},{16,20},{20,16},{24,28},{28,24},{1,5},{5... | collective-permute-start | bytes 1474568 | tf_op jit(solution)/shard_map/ppermute | solution.py:452
  37.3 1.3 %collective-permute-start.2 = (bf16[320,768]{1,0:T(8,128)(2,1)S(1)}, bf16[320,768]{1,0:T(8,128)(2,1)S(1)}, u32[]{:S(2)}, u32[]{:S(2)}) collective-permute-start(bf16[320,768]{1,0:T(8,128)(2,1)S(1)} %collective-permute-done.1), channel_id=1, source_target_pairs={{8,0},{12,4},{16,24},{20,28},{9,1},{13,5},{17,25},{21,29},{10,2},{... | collective-permute-start | bytes 1474568 | tf_op jit(solution)/shard_map/ppermute | solution.py:452
  38.6 1.3 %collective-permute-done.8.refs_1_ = bf16[320,768]{1,0:T(8,128)(2,1)S(1)} collective-permute-done((bf16[320,768]{1,0:T(8,128)(2,1)S(1)}, bf16[320,768]{1,0:T(8,128)(2,1)S(1)}, u32[]{:S(2)}, u32[]{:S(2)}) %collective-permute-start.8) | collective-permute-done | bytes 491552 | tf_op jit(solution)/shard_map/ppermute | solution.py:452
  39.9 0.6 shard_map.87.refs_2_
  40.6 0.1 collective-permute-start.13
  40.6 9.0 %collective-permute-done.2 = bf16[320,768]{1,0:T(8,128)(2,1)S(1)} collective-permute-done((bf16[320,768]{1,0:T(8,128)(2,1)S(1)}, bf16[320,768]{1,0:T(8,128)(2,1)S(1)}, u32[]{:S(2)}, u32[]{:S(2)}) %collective-permute-start.2) | collective-permute-done | bytes 491552 | tf_op jit(solution)/shard_map/ppermute | solution.py:452
  49.6 0.1 broadcast_select_fusion.1.refs_0_
  49.7 0.6 collective-permute-start.4
  50.3 2.4 %collective-permute-start.18 = (bf16[256,768]{1,0:T(8,128)(2,1)S(1)}, bf16[256,768]{1,0:T(8,128)(2,1)S(1)}, u32[]{:S(2)}, u32[]{:S(2)}) collective-permute-start(bf16[256,768]{1,0:T(8,128)(2,1)S(1)} %get-tuple-element.29.refs_0_), channel_id=1, source_target_pairs={{0,8},{4,12},{8,0},{12,4},{16,24},{20,28},{24,16},{28,20},{1,9},{5... | collective-permute-start | bytes 1179656 | tf_op jit(solution)/shard_map/ppermute | solution.py:452
  52.8 0.6 shard_map.89.refs_0_
  53.4 0.7 collective-permute-start.15
  54.1 6.8 %mid.1 = (bf16[6,512,768]{2,1,0:T(8,128)(2,1)S(1)}, f32[4,256,384]{2,1,0:T(8,128)S(1)}, bf16[4,2048,256]{2,1,0:T(8,128)(2,1)S(1)}) custom-call(bf16[8,320,768]{2,1,0:T(8,128)(2,1)S(1)} %shard_map.89.refs_0_, bf16[4,6,256,128]{3,2,1,0:T(8,128)(2,1)S(1)} %copy-done, bf16[6,64,256]{2,1,0:T(8,128)(2,1)S(1)} %bitcast.3, bf16[2048,256]{1,0:T(8,128)(2,1)S(1)} %pack_panel.1.refs_3_, ...), custom_call_target="tpu_custom_call" | custom-call | flops 2415919104 | tf_op jit(solution)/shard_map/mid/pallas_call | solution.py:592
  60.9 1.5 %sampled.1 = (bf16[2,512,768]{2,1,0:T(8,128)(2,1)S(1)}, f32[4,256,384]{2,1,0:T(8,128)S(1)}) custom-call(bf16[320,768]{1,0:T(8,128)(2,1)S(1)} %broadcast_select_fusion.1.refs_0_, bf16[320,768]{1,0:T(8,128)(2,1)S(1)} %collective-permute-done.4.refs_1_, bf16[4,2048,256]{2,1,0:T(8,128)(2,1)S(1)} %get-tuple-element.32.refs_2_.panel_ref.refs_4_, ...), custom_call_target="tpu_custom_call" | custom-call | flops 805306368 | tf_op jit(solution)/shard_map/sampled/pallas_call | solution.py:646
  62.4 6.6 %gram.1.refs_1_ = f32[64,16,128]{2,1,0:T(8,128)S(1)} custom-call(f32[4,256,384]{2,1,0:T(8,128)S(1)} %get-tuple-element.34.refs_0_), custom_call_target="tpu_custom_call" | custom-call | flops 1000000000 | tf_op jit(solution)/shard_map/gram/pallas_call | solution.py:659
  69.1 1.5 %collective-permute-start.14 = (bf16[256,768]{1,0:T(8,128)(2,1)S(1)}, bf16[256,768]{1,0:T(8,128)(2,1)S(1)}, u32[]{:S(2)}, u32[]{:S(2)}) collective-permute-start(bf16[256,768]{1,0:T(8,128)(2,1)S(1)} %collective-permute-done.3.refs_0_), channel_id=1, source_target_pairs={{8,0},{12,4},{16,24},{20,28},{9,1},{13,5},{17,25},{21,29},{10,2},{... | collective-permute-start | bytes 1179656 | tf_op jit(solution)/shard_map/ppermute | solution.py:452
  70.6 1.6 %collective-permute-start.19 = (bf16[256,768]{1,0:T(8,128)(2,1)S(1)}, bf16[256,768]{1,0:T(8,128)(2,1)S(1)}, u32[]{:S(2)}, u32[]{:S(2)}) collective-permute-start(bf16[256,768]{1,0:T(8,128)(2,1)S(1)} %collective-permute-done.18.refs_0_), channel_id=1, source_target_pairs={{0,4},{4,0},{8,12},{12,8},{16,20},{20,16},{24,28},{28,24},{1,5},{5... | collective-permute-start | bytes 1179656 | tf_op jit(solution)/shard_map/ppermute | solution.py:452
  72.2 0.5 collective-permute-start.17
  72.7 5.0 %basis.1 = (f32[64,16,128]{2,1,0:T(8,128)S(1)}, bf16[4,256,384]{2,1,0:T(8,128)(2,1)S(1)}) custom-call(f32[4,256,384]{2,1,0:T(8,128)S(1)} %get-tuple-element.34.refs_0_, f32[64,16,128]{2,1,0:T(8,128)S(1)} %gram.1.refs_1_), custom_call_target="tpu_custom_call", output_to_operand_aliasing={{0}: (1, {})} | custom-call | flops 1000000000 | tf_op jit(solution)/shard_map/basis/pallas_call | solution.py:674
  77.7 2.8 %project.1 = (bf16[4,384,1024]{2,1,0:T(8,128)(2,1)S(1)}, f32[6,256,256]{2,1,0:T(8,128)S(1)}) custom-call(bf16[4,256,384]{2,1,0:T(8,128)(2,1)S(1)} %get-tuple-element.37.basis_ref.refs_3_, bf16[4,2048,256]{2,1,0:T(8,128)(2,1)S(1)} %get-tuple-element.32.refs_2_.panel_ref.refs_4_, bf16[4,6,256,128]{3,2,1,0:T(8,128)(2,1)S(1)} %copy-done), custom_call_target="tpu_custom_call" | custom-call | flops 1000000000 | tf_op jit(solution)/shard_map/project/pallas_call | solution.py:683
  80.6 1.6 %collective-permute-start.16 = (bf16[256,768]{1,0:T(8,128)(2,1)S(1)}, bf16[256,768]{1,0:T(8,128)(2,1)S(1)}, u32[]{:S(2)}, u32[]{:S(2)}) collective-permute-start(bf16[256,768]{1,0:T(8,128)(2,1)S(1)} %broadcast_select_fusion.2.refs_1_), channel_id=1, source_target_pairs={{0,4},{4,0},{8,12},{12,8},{16,20},{20,16},{24,28},{28,24},{1,5},{5... | collective-permute-start | bytes 1179656 | tf_op jit(solution)/shard_map/ppermute | solution.py:452
  82.2 0.5 collective-permute-done.19.refs_1_
  82.7 0.4 shard_map.90.refs_2_
  83.1 3.9 %cores.1 = (bf16[6,256,1024]{2,1,0:T(8,128)(2,1)S(1)}, bf16[4,256,1024]{2,1,0:T(8,128)(2,1)S(1)}) custom-call(s32[1,4]{1,0:T(1,128)S(1)} %bitcast.4, bf16[4,384,1024]{2,1,0:T(8,128)(2,1)S(1)} %get-tuple-element.39.refs_1_, bf16[6,512,768]{2,1,0:T(8,128)(2,1)S(1)} %get-tuple-element.40.refs_2_, bf16[2,512,768]{2,1,0:T(8,128)(2,1)S(1)} %get-tuple-element.41.refs_3_, ...), custom_call_target="tpu_custom_call" | custom-call | flops 1000000000 | tf_op jit(solution)/shard_map/cores/pallas_call | solution.py:690
  87.1 3.2 %collective-permute-done.17.refs_1_ = bf16[256,768]{1,0:T(8,128)(2,1)S(1)} collective-permute-done((bf16[256,768]{1,0:T(8,128)(2,1)S(1)}, bf16[256,768]{1,0:T(8,128)(2,1)S(1)}, u32[]{:S(2)}, u32[]{:S(2)}) %collective-permute-start.17) | collective-permute-done | bytes 393248 | tf_op jit(solution)/shard_map/ppermute | solution.py:452
  90.3 0.4 shard_map.91.refs_1_
  90.7 1.9 %most.1 = (f32[6,256,256]{2,1,0:T(8,128)S(1)}, f32[4,256,256]{2,1,0:T(8,128)S(1)}) custom-call(s32[1,4]{1,0:T(1,128)S(1)} %bitcast.5, bf16[8,256,768]{2,1,0:T(8,128)(2,1)S(1)} %shard_map.91.refs_1_, bf16[6,256,1024]{2,1,0:T(8,128)(2,1)S(1)} %get-tuple-element.42.refs_2_.refs_4_, f32[6,256,256]{2,1,0:T(8,128)S(1)} %get-tuple-element.44.refs_3_, ...), custom_call_target="tpu_custom_call" | custom-call | flops 1000000000 | tf_op jit(solution)/shard_map/most/pallas_call | solution.py:697
  92.6 1.9 %collective-permute-done.16.refs_2_ = bf16[256,768]{1,0:T(8,128)(2,1)S(1)} collective-permute-done((bf16[256,768]{1,0:T(8,128)(2,1)S(1)}, bf16[256,768]{1,0:T(8,128)(2,1)S(1)}, u32[]{:S(2)}, u32[]{:S(2)}) %collective-permute-start.16) | collective-permute-done | bytes 393248 | tf_op jit(solution)/shard_map/ppermute | solution.py:452
  94.5 2.7 %output.1 = (bf16[4,1,256,256]{3,2,1,0:T(8,128)(2,1)}, bf16[4,6,256,128]{3,2,1,0:T(8,128)(2,1)}) custom-call(s32[1,4]{1,0:T(1,128)S(1)} %bitcast.6, bf16[256,768]{1,0:T(8,128)(2,1)S(1)} %broadcast_select_fusion.2.refs_1_, bf16[256,768]{1,0:T(8,128)(2,1)S(1)} %collective-permute-done.16.refs_2_, bf16[4,256,384]{2,1,0:T(8,128)(2,1)S(1)} %get-tuple-element.37.basis_ref.refs_3_, ...), custom_call_target="tpu_custom_call" | custom-call | flops 805306368 | tf_op jit(solution)/shard_map/output/pallas_call | solution.py:705
  (27 shorter events, 0.1 us)
Async XLA Ops:
  0.6 1.1 %copy-start.2 = (bf16[2,6,256,128]{3,2,1,0:T(8,128)(2,1)S(1)}, bf16[2,6,256,128]{3,2,1,0:T(8,128)(2,1)}, u32[]{:S(2)}) copy-start(bf16[2,6,256,128]{3,2,1,0:T(8,128)(2,1)} %rows_ref.1) | copy-start | bytes 2359300
  1.8 0.9 copy-start.3
  3.0 14.3 %collective-permute-start = (bf16[320,768]{1,0:T(8,128)(2,1)S(1)}, bf16[320,768]{1,0:T(8,128)(2,1)S(1)}, u32[]{:S(2)}, u32[]{:S(2)}) collective-permute-start(bf16[320,768]{1,0:T(8,128)(2,1)S(1)} %get-tuple-element.26.refs_0_), channel_id=1, source_target_pairs={{0,8},{4,12},{8,0},{12,4},{16,24},{20,28},{24,16},{28,20},{1,9},{5... | collective-permute-start | bytes 1474568 | tf_op jit(solution)/shard_map/ppermute | solution.py:452
  6.1 13.3 %collective-permute-start.9 = (bf16[320,768]{1,0:T(8,128)(2,1)S(1)}, bf16[320,768]{1,0:T(8,128)(2,1)}, u32[]{:S(2)}, u32[]{:S(2)}) collective-permute-start(bf16[320,768]{1,0:T(8,128)(2,1)S(1)} %get-tuple-element.26.refs_0_), channel_id=1, source_target_pairs={{0,4},{4,0},{8,12},{12,8},{16,20},{20,16},{24,28},{28,24},{1,5},{5... | collective-permute-start | bytes 1474568 | tf_op jit(solution)/shard_map/ppermute | solution.py:452
  7.6 12.5 %collective-permute-start.5 = (bf16[320,768]{1,0:T(8,128)(2,1)S(1)}, bf16[320,768]{1,0:T(8,128)(2,1)}, u32[]{:S(2)}, u32[]{:S(2)}) collective-permute-start(bf16[320,768]{1,0:T(8,128)(2,1)S(1)} %get-tuple-element.26.refs_0_), channel_id=1, source_target_pairs={{8,16},{16,8},{12,20},{20,12},{9,17},{17,9},{13,21},{21,13},{10,18... | collective-permute-start | bytes 1474568 | tf_op jit(solution)/shard_map/ppermute | solution.py:452
  9.0 1.2 %copy-start.1 = (bf16[4,4,256,128]{3,2,1,0:T(8,128)(2,1)S(1)}, bf16[4,4,256,128]{3,2,1,0:T(8,128)(2,1)}, u32[]{:S(2)}) copy-start(bf16[4,4,256,128]{3,2,1,0:T(8,128)(2,1)} %panel_ref.1) | copy-start | bytes 3145732
  10.3 1.0 %copy-start.5 = (bf16[4,256,256]{2,1,0:T(8,128)(2,1)S(1)}, bf16[4,256,256]{2,1,0:T(8,128)(2,1)}, u32[]{:S(2)}) copy-start(bf16[4,256,256]{2,1,0:T(8,128)(2,1)} %inv_ref.1) | copy-start | bytes 1572868
  11.8 26.8 %collective-permute-start.10 = (bf16[2048,256]{1,0:T(8,128)(2,1)S(1)}, bf16[2048,256]{1,0:T(8,128)(2,1)S(1)}, u32[]{:S(2)}, u32[]{:S(2)}) collective-permute-start(bf16[2048,256]{1,0:T(8,128)(2,1)S(1)} %pack_panel.1.refs_3_), channel_id=1, source_target_pairs={{0,2},{1,3},{2,0},{3,1},{4,6},{5,7},{6,4},{7,5},{8,10},{9,11},{10,... | collective-permute-start | bytes 3145736 | tf_op jit(solution)/shard_map/ppermute | solution.py:550
  17.3 12.1 %collective-permute-start.11 = (bf16[256,768]{1,0:T(8,128)(2,1)S(1)}, bf16[256,768]{1,0:T(8,128)(2,1)S(1)}, u32[]{:S(2)}, u32[]{:S(2)}) collective-permute-start(bf16[256,768]{1,0:T(8,128)(2,1)S(1)} %get-tuple-element.29.refs_0_), channel_id=1, source_target_pairs={{0,4},{4,0},{8,12},{12,8},{16,20},{20,16},{24,28},{28,24},{1,5},{5... | collective-permute-start | bytes 1179656 | tf_op jit(solution)/shard_map/ppermute | solution.py:452
  19.0 20.9 %collective-permute-start.8 = (bf16[320,768]{1,0:T(8,128)(2,1)S(1)}, bf16[320,768]{1,0:T(8,128)(2,1)S(1)}, u32[]{:S(2)}, u32[]{:S(2)}) collective-permute-start(bf16[320,768]{1,0:T(8,128)(2,1)S(1)} %collective-permute-done.refs_0_), channel_id=1, source_target_pairs={{0,4},{4,0},{8,12},{12,8},{16,20},{20,16},{24,28},{28,24},{1,5},{5... | collective-permute-start | bytes 1474568 | tf_op jit(solution)/shard_map/ppermute | solution.py:452
  19.4 17.9 %collective-permute-start.1 = (bf16[320,768]{1,0:T(8,128)(2,1)S(1)}, bf16[320,768]{1,0:T(8,128)(2,1)S(1)}, u32[]{:S(2)}, u32[]{:S(2)}) collective-permute-start(bf16[320,768]{1,0:T(8,128)(2,1)S(1)} %collective-permute-done.refs_0_), channel_id=1, source_target_pairs={{8,16},{16,8},{12,20},{20,12},{9,17},{17,9},{13,21},{21,13},{10,18... | collective-permute-start | bytes 1474568 | tf_op jit(solution)/shard_map/ppermute | solution.py:452
  20.1 15.6 %collective-permute-start.6 = (bf16[320,768]{1,0:T(8,128)(2,1)}, bf16[320,768]{1,0:T(8,128)(2,1)S(1)}, u32[]{:S(2)}, u32[]{:S(2)}) collective-permute-start(bf16[320,768]{1,0:T(8,128)(2,1)} %collective-permute-done.5), channel_id=1, source_target_pairs={{8,0},{12,4},{16,24},{20,28},{9,1},{13,5},{17,25},{21,29},{10,2},{... | collective-permute-start | bytes 1474568 | tf_op jit(solution)/shard_map/ppermute | solution.py:452
  29.4 24.0 %collective-permute-start.12 = (bf16[2048,256]{1,0:T(8,128)(2,1)S(1)}, bf16[2048,256]{1,0:T(8,128)(2,1)S(1)}, u32[]{:S(2)}, u32[]{:S(2)}) collective-permute-start(bf16[2048,256]{1,0:T(8,128)(2,1)S(1)} %pack_panel.1.refs_3_), channel_id=1, source_target_pairs={{0,1},{1,0},{2,3},{3,2},{4,5},{5,4},{6,7},{7,6},{8,9},{9,8},{10,11... | collective-permute-start | bytes 3145736 | tf_op jit(solution)/shard_map/ppermute | solution.py:551
  35.8 14.6 %collective-permute-start.7 = (bf16[320,768]{1,0:T(8,128)(2,1)S(1)}, bf16[320,768]{1,0:T(8,128)(2,1)S(1)}, u32[]{:S(2)}, u32[]{:S(2)}) collective-permute-start(bf16[320,768]{1,0:T(8,128)(2,1)S(1)} %broadcast_select_fusion.refs_0_), channel_id=1, source_target_pairs={{0,4},{4,0},{8,12},{12,8},{16,20},{20,16},{24,28},{28,24},{1,5},{5... | collective-permute-start | bytes 1474568 | tf_op jit(solution)/shard_map/ppermute | solution.py:452
  37.3 12.3 %collective-permute-start.2 = (bf16[320,768]{1,0:T(8,128)(2,1)S(1)}, bf16[320,768]{1,0:T(8,128)(2,1)S(1)}, u32[]{:S(2)}, u32[]{:S(2)}) collective-permute-start(bf16[320,768]{1,0:T(8,128)(2,1)S(1)} %collective-permute-done.1), channel_id=1, source_target_pairs={{8,0},{12,4},{16,24},{20,28},{9,1},{13,5},{17,25},{21,29},{10,2},{... | collective-permute-start | bytes 1474568 | tf_op jit(solution)/shard_map/ppermute | solution.py:452
  40.6 13.5 %collective-permute-start.13 = (bf16[2048,256]{1,0:T(8,128)(2,1)S(1)}, bf16[2048,256]{1,0:T(8,128)(2,1)S(1)}, u32[]{:S(2)}, u32[]{:S(2)}) collective-permute-start(bf16[2048,256]{1,0:T(8,128)(2,1)S(1)} %collective-permute-done.10.refs_5_), channel_id=1, source_target_pairs={{0,1},{1,0},{2,3},{3,2},{4,5},{5,4},{6,7},{7,6},{8,9},{9,8},{10,11... | collective-permute-start | bytes 3145736 | tf_op jit(solution)/shard_map/ppermute | solution.py:552
  49.7 4.4 %copy-start = (bf16[4,6,256,128]{3,2,1,0:T(8,128)(2,1)S(1)}, bf16[4,6,256,128]{3,2,1,0:T(8,128)(2,1)}, u32[]{:S(2)}) copy-start(bf16[4,6,256,128]{3,2,1,0:T(8,128)(2,1)} %target_ref.1) | copy-start | bytes 4718596
  49.7 4.4 %copy-start.4 = (bf16[6,256,64]{1,2,0:T(8,128)(2,1)S(1)}, bf16[6,256,64]{1,2,0:T(8,128)(2,1)}, u32[]{:S(2)}) copy-start(bf16[6,256,64]{1,2,0:T(8,128)(2,1)} %param.13) | copy-start | bytes 589828
  49.7 11.2 %collective-permute-start.4 = (bf16[320,768]{1,0:T(8,128)(2,1)S(1)}, bf16[320,768]{1,0:T(8,128)(2,1)S(1)}, u32[]{:S(2)}, u32[]{:S(2)}) collective-permute-start(bf16[320,768]{1,0:T(8,128)(2,1)S(1)} %broadcast_select_fusion.1.refs_0_), channel_id=1, source_target_pairs={{0,4},{4,0},{8,12},{12,8},{16,20},{20,16},{24,28},{28,24},{1,5},{5... | collective-permute-start | bytes 1474568 | tf_op jit(solution)/shard_map/ppermute | solution.py:452
  50.3 18.8 %collective-permute-start.3 = (bf16[256,768]{1,0:T(8,128)(2,1)S(1)}, bf16[256,768]{1,0:T(8,128)(2,1)S(1)}, u32[]{:S(2)}, u32[]{:S(2)}) collective-permute-start(bf16[256,768]{1,0:T(8,128)(2,1)S(1)} %get-tuple-element.29.refs_0_), channel_id=1, source_target_pairs={{0,16},{4,20},{8,24},{12,28},{16,0},{20,4},{24,8},{28,12},{1,17},{... | collective-permute-start | bytes 1179656 | tf_op jit(solution)/shard_map/ppermute | solution.py:452
  50.3 20.3 %collective-permute-start.18 = (bf16[256,768]{1,0:T(8,128)(2,1)S(1)}, bf16[256,768]{1,0:T(8,128)(2,1)S(1)}, u32[]{:S(2)}, u32[]{:S(2)}) collective-permute-start(bf16[256,768]{1,0:T(8,128)(2,1)S(1)} %get-tuple-element.29.refs_0_), channel_id=1, source_target_pairs={{0,8},{4,12},{8,0},{12,4},{16,24},{20,28},{24,16},{28,20},{1,9},{5... | collective-permute-start | bytes 1179656 | tf_op jit(solution)/shard_map/ppermute | solution.py:452
  53.4 27.1 %collective-permute-start.15 = (bf16[256,768]{1,0:T(8,128)(2,1)S(1)}, bf16[256,768]{1,0:T(8,128)(2,1)S(1)}, u32[]{:S(2)}, u32[]{:S(2)}) collective-permute-start(bf16[256,768]{1,0:T(8,128)(2,1)S(1)} %get-tuple-element.29.refs_0_), channel_id=1, source_target_pairs={{8,16},{16,8},{12,20},{20,12},{9,17},{17,9},{13,21},{21,13},{10,18... | collective-permute-start | bytes 1179656 | tf_op jit(solution)/shard_map/ppermute | solution.py:452
  69.1 11.4 %collective-permute-start.14 = (bf16[256,768]{1,0:T(8,128)(2,1)S(1)}, bf16[256,768]{1,0:T(8,128)(2,1)S(1)}, u32[]{:S(2)}, u32[]{:S(2)}) collective-permute-start(bf16[256,768]{1,0:T(8,128)(2,1)S(1)} %collective-permute-done.3.refs_0_), channel_id=1, source_target_pairs={{8,0},{12,4},{16,24},{20,28},{9,1},{13,5},{17,25},{21,29},{10,2},{... | collective-permute-start | bytes 1179656 | tf_op jit(solution)/shard_map/ppermute | solution.py:452
  70.6 12.1 %collective-permute-start.19 = (bf16[256,768]{1,0:T(8,128)(2,1)S(1)}, bf16[256,768]{1,0:T(8,128)(2,1)S(1)}, u32[]{:S(2)}, u32[]{:S(2)}) collective-permute-start(bf16[256,768]{1,0:T(8,128)(2,1)S(1)} %collective-permute-done.18.refs_0_), channel_id=1, source_target_pairs={{0,4},{4,0},{8,12},{12,8},{16,20},{20,16},{24,28},{28,24},{1,5},{5... | collective-permute-start | bytes 1179656 | tf_op jit(solution)/shard_map/ppermute | solution.py:452
  72.2 18.1 %collective-permute-start.17 = (bf16[256,768]{1,0:T(8,128)(2,1)S(1)}, bf16[256,768]{1,0:T(8,128)(2,1)S(1)}, u32[]{:S(2)}, u32[]{:S(2)}) collective-permute-start(bf16[256,768]{1,0:T(8,128)(2,1)S(1)} %collective-permute-done.3.refs_0_), channel_id=1, source_target_pairs={{0,4},{4,0},{8,12},{12,8},{16,20},{20,16},{24,28},{28,24},{1,5},{5... | collective-permute-start | bytes 1179656 | tf_op jit(solution)/shard_map/ppermute | solution.py:452
  80.6 2.5 %copy-start.7 = (s32[4,1]{0,1:T(1,128)S(1)}, s32[4,1]{0,1:T(1,128)}, u32[]{:S(2)}) copy-start(s32[4,1]{0,1:T(1,128)} %param.12) | copy-start | bytes 52
  80.6 13.9 %collective-permute-start.16 = (bf16[256,768]{1,0:T(8,128)(2,1)S(1)}, bf16[256,768]{1,0:T(8,128)(2,1)S(1)}, u32[]{:S(2)}, u32[]{:S(2)}) collective-permute-start(bf16[256,768]{1,0:T(8,128)(2,1)S(1)} %broadcast_select_fusion.2.refs_1_), channel_id=1, source_target_pairs={{0,4},{4,0},{8,12},{12,8},{16,20},{20,16},{24,28},{28,24},{1,5},{5... | collective-permute-start | bytes 1179656 | tf_op jit(solution)/shard_map/ppermute | solution.py:452
  87.1 3.6 %copy-start.6 = (bf16[4,1,256,256]{3,2,1,0:T(8,128)(2,1)S(1)}, bf16[4,1,256,256]{3,2,1,0:T(8,128)(2,1)}, u32[]{:S(2)}) copy-start(bf16[4,1,256,256]{3,2,1,0:T(8,128)(2,1)} %refs_5_.1) | copy-start | bytes 1572868
